TPU v7x, 256 devices: a whole 4x4x8 slice. The times are simulated.
256 devices in a mesh: dp: 4 (over x), ctx: 64 (over y, z, core).
Axes of the slice: x: 4, y: 4, z: 8, core: 2. Of those that a mesh axis runs over, the one named last changes fastest.
Arguments:
- video_query: bfloat16 [4, 8192, 3072], P('dp', 'ctx'), may hold values from -80 to 80
- video_key: bfloat16 [4, 8192, 3072], P('dp', 'ctx'), may hold values from -6 to 6
- video_value: bfloat16 [4, 8192, 3072], P('dp', 'ctx'), may hold values from -6 to 6
- audio_key: bfloat16 [4, 1024, 3072], P('dp', 'ctx'), may hold values from -6 to 6
- audio_value: bfloat16 [4, 1024, 3072], P('dp', 'ctx'), may hold values from -6 to 6
- cross_gate: float32 [3072], replicated, may hold values from -6 to 6
- out_cotangent: bfloat16 [4, 8192, 3072], P('dp', 'ctx'), may hold values from -6 to 6
- tile_list: int32 [128, 4], replicated, may hold values from 0 to 127, as said below
- tile_count: int32 [128], replicated, may hold values from 2 to 4, as said below
- audio_list: int32 [128, 2], replicated, may hold values from 0 to 63, as said below
Outputs:
- query_grad: bfloat16 [4, 8192, 3072], P('dp', 'ctx')
- key_grad: bfloat16 [4, 8192, 3072], P('dp', 'ctx')
- value_grad: bfloat16 [4, 8192, 3072], P('dp', 'ctx')
- audio_key_grad: bfloat16 [4, 1024, 3072], P('dp', 'ctx')
- audio_value_grad: bfloat16 [4, 1024, 3072], P('dp', 'ctx')
- gate_grad: float32 [3072], replicated
Inputs may be any that keep to these rules, and one draw needn't show every extreme that they name: `tile_list`: entry 0 of row t is t itself; every entry lies in tiles (t // 2 - 1) * 2 to (t // 2 + 2) * 2 - 1; the first tile_count[t] entries are distinct, the others are padding. `tile_count`: live slots of row t of tile_list. `audio_list`: entry 0 of row t is block t // 2, aligned with the tile in time; entry 1 is a block next to it.
All inputs are finite; a program needn't handle non-finite values.
Results may differ from a plain program's by a relative error of at most 0.015.
Values may be sent and summed in bfloat16 or wider, within the bound.
No kernel may reach another device: no remote copies, remote signals or barrier semaphores. Data moves between devices by JAX's collectives and lax.ppermute only.
A program may use at most 128 MiB of HBM per device.

v0:
```python
import math

import jax
import jax.numpy as jnp
from jax import lax
from jax.sharding import PartitionSpec as P

HEADS = 24
HEAD_DIM = 128
TILE = 64


def padded(cells, sides, width):
    for axis, dim in sides:
        count = lax.axis_size(axis)
        ends = count - 1
        head = lax.slice_in_dim(cells, 0, width, axis=dim)
        tail = lax.slice_in_dim(cells, cells.shape[dim] - width, cells.shape[dim], axis=dim)
        cells = jnp.concatenate(
            [
                lax.ppermute(tail, axis, [(i, (i + 1) % count) for i in range(ends)]),
                cells,
                lax.ppermute(head, axis, [((i + 1) % count, i) for i in range(ends)]),
            ],
            axis=dim,
        )
    return cells


def passed_along(shard, axis, by):
    count = lax.axis_size(axis)
    pairs = [(i, i + by) for i in range(count) if 0 <= i + by < count]
    return lax.ppermute(shard, axis, pairs)


def gather_slots(window, slot_ids):
    picked = jnp.take(window, slot_ids, axis=1)
    return picked.reshape(
        picked.shape[0], slot_ids.shape[0], slot_ids.shape[1] * window.shape[2], window.shape[3]
    )


def split_heads(array, group_heads):
    return array.reshape(array.shape[:-1] + (group_heads, array.shape[-1] // group_heads))


def key_scores(queries, key_rows, key_mask, group_heads):
    score_scale = 1.0 / math.sqrt(HEAD_DIM)
    scores = (
        jnp.einsum(
            "cnlhe,cnkhe->cnhlk",
            split_heads(queries, group_heads),
            split_heads(key_rows, group_heads),
            preferred_element_type=jnp.float32,
        )
        * score_scale
    )
    return jnp.where(key_mask[None, :, None, None, :], scores, -jnp.inf)


def attend(queries, key_rows, value_rows, key_mask, group_heads):
    scores = key_scores(queries, key_rows, key_mask, group_heads)
    row_top = jnp.max(scores, axis=-1, keepdims=True)
    log_total = row_top + jnp.log(jnp.sum(jnp.exp(scores - row_top), axis=-1, keepdims=True))
    weights = jnp.exp(scores - log_total).astype(jnp.bfloat16)
    mixed = jnp.einsum(
        "cnhlk,cnkhe->cnlhe",
        weights,
        split_heads(value_rows, group_heads),
        preferred_element_type=jnp.float32,
    )
    return (mixed.reshape(queries.shape), log_total[..., 0])


def head_sums(cotangent, mixed, group_heads):
    product = split_heads(cotangent.astype(jnp.float32) * mixed, group_heads)
    return jnp.swapaxes(jnp.sum(product, axis=-1), -1, -2)


def attend_back(
    queries, cotangent, key_rows, value_rows, key_mask, log_total, row_delta, group_heads
):
    score_scale = 1.0 / math.sqrt(HEAD_DIM)
    probabilities = jnp.exp(
        key_scores(queries, key_rows, key_mask, group_heads) - log_total[..., None]
    )
    weights = probabilities.astype(jnp.bfloat16)
    split_cotangent = split_heads(cotangent, group_heads)
    prob_grads = jnp.einsum(
        "cnlhe,cnkhe->cnhlk",
        split_cotangent,
        split_heads(value_rows, group_heads),
        preferred_element_type=jnp.float32,
    )
    score_grads = (probabilities * (prob_grads - row_delta[..., None])).astype(jnp.bfloat16)
    grad_query = (
        jnp.einsum(
            "cnhlk,cnkhe->cnlhe",
            score_grads,
            split_heads(key_rows, group_heads),
            preferred_element_type=jnp.float32,
        )
        * score_scale
    )
    grad_key = (
        jnp.einsum(
            "cnhlk,cnlhe->cnkhe",
            score_grads,
            split_heads(queries, group_heads),
            preferred_element_type=jnp.float32,
        )
        * score_scale
    )
    grad_value = jnp.einsum(
        "cnhlk,cnlhe->cnkhe", weights, split_cotangent, preferred_element_type=jnp.float32
    )
    return (
        grad_query.reshape(queries.shape),
        grad_key.reshape(key_rows.shape),
        grad_value.reshape(key_rows.shape),
    )


def spread_slots(slot_grads, slot_ids, window_count):
    clip_count, tile_total, slot_rows, width = slot_grads.shape
    slots = slot_ids.shape[1]
    blocks = slot_grads.reshape(clip_count, tile_total * slots, slot_rows // slots, width)
    leading = jnp.moveaxis(blocks, 1, 0)
    summed = jax.ops.segment_sum(leading, slot_ids.reshape(-1), num_segments=window_count)
    return jnp.moveaxis(summed, 0, 1)


def channel_slice(array, group_id, group_width):
    return lax.dynamic_slice_in_dim(array, group_id * group_width, group_width, array.ndim - 1)


def channel_put(array, piece, group_id, group_width):
    return lax.dynamic_update_slice_in_dim(array, piece, group_id * group_width, array.ndim - 1)


def own_pass(
    query_tiles,
    dout_tiles,
    gated_tiles,
    video_window,
    audio_window,
    tile_ids,
    tile_mask,
    audio_ids,
    audio_mask,
):
    group_heads = math.gcd(HEADS, 8)
    group_width = group_heads * HEAD_DIM
    clip_count, tile_total, tile_rows, model_width = query_tiles.shape
    window_tiles = video_window.shape[2]
    audio_blocks = audio_window.shape[2]

    def one_group(group_id, loop_state):
        grad_query, video_grads, audio_grads, gate_part, statistics = loop_state
        queries = channel_slice(query_tiles, group_id, group_width)
        cotangent = channel_slice(dout_tiles, group_id, group_width)
        gated_rows = channel_slice(gated_tiles, group_id, group_width)
        video_slice = channel_slice(video_window, group_id, group_width)
        audio_slice = channel_slice(audio_window, group_id, group_width)
        key_rows = gather_slots(video_slice[0], tile_ids)
        value_rows = gather_slots(video_slice[1], tile_ids)
        audio_keys = gather_slots(audio_slice[0], audio_ids)
        audio_values = gather_slots(audio_slice[1], audio_ids)
        mixed_video, total_video = attend(queries, key_rows, value_rows, tile_mask, group_heads)
        mixed_cross, total_cross = attend(
            queries, audio_keys, audio_values, audio_mask, group_heads
        )
        delta_video = head_sums(cotangent, mixed_video, group_heads)
        delta_cross = head_sums(gated_rows, mixed_cross, group_heads)
        query_video, key_video, value_video = attend_back(
            queries,
            cotangent,
            key_rows,
            value_rows,
            tile_mask,
            total_video,
            delta_video,
            group_heads,
        )
        query_cross, key_cross, value_cross = attend_back(
            queries,
            gated_rows,
            audio_keys,
            audio_values,
            audio_mask,
            total_cross,
            delta_cross,
            group_heads,
        )
        grad_query = channel_put(grad_query, query_video + query_cross, group_id, group_width)
        video_new = jnp.stack(
            (
                spread_slots(key_video, tile_ids, window_tiles),
                spread_slots(value_video, tile_ids, window_tiles),
            )
        )
        audio_new = jnp.stack(
            (
                spread_slots(key_cross, audio_ids, audio_blocks),
                spread_slots(value_cross, audio_ids, audio_blocks),
            )
        )
        video_grads = channel_put(video_grads, video_new, group_id, group_width)
        audio_grads = channel_put(audio_grads, audio_new, group_id, group_width)
        gate_piece = jnp.sum(cotangent.astype(jnp.float32) * mixed_cross, axis=(0, 1, 2))
        gate_part = channel_put(gate_part, gate_piece, group_id, group_width)
        fresh_stats = jnp.stack((total_video, delta_video, total_cross, delta_cross))
        statistics = lax.dynamic_update_slice_in_dim(
            statistics, fresh_stats, group_id * group_heads, 3
        )
        return (grad_query, video_grads, audio_grads, gate_part, statistics)

    initial = (
        jnp.zeros(query_tiles.shape, jnp.float32),
        jnp.zeros(video_window.shape, jnp.float32),
        jnp.zeros(audio_window.shape, jnp.float32),
        jnp.zeros((model_width,), jnp.float32),
        jnp.zeros((4, clip_count, tile_total, HEADS, tile_rows), jnp.float32),
    )
    return lax.fori_loop(0, HEADS // group_heads, one_group, initial)


def per_device(
    video_query,
    video_key,
    video_value,
    audio_key,
    audio_value,
    cross_gate,
    out_cotangent,
    tile_list,
    tile_count,
    audio_list,
):
    clip_count, row_count, model_width = video_query.shape
    audio_rows = audio_key.shape[1]
    local_tiles = row_count // TILE
    position = lax.axis_index("ctx")
    slot_order = jnp.arange(tile_list.shape[1], dtype=jnp.int32)
    gated_full = (cross_gate * out_cotangent).astype(jnp.bfloat16)
    packed = jnp.concatenate(
        (jnp.stack((video_key, video_value)), jnp.stack((audio_key, audio_value))), axis=2
    )
    stride_rows = row_count + audio_rows
    beside_all = padded(packed, (("ctx", 2),), stride_rows)
    video_window = jnp.concatenate(
        [
            beside_all[:, :, third * stride_rows : third * stride_rows + row_count]
            for third in range(3)
        ],
        axis=2,
    ).reshape(2, clip_count, 3 * local_tiles, TILE, model_width)
    audio_window = jnp.concatenate(
        [
            beside_all[:, :, third * stride_rows + row_count : (third + 1) * stride_rows]
            for third in range(3)
        ],
        axis=2,
    ).reshape(2, clip_count, 3, audio_rows, model_width)
    own_list = lax.dynamic_slice_in_dim(tile_list, position * local_tiles, local_tiles, 0)
    own_count = lax.dynamic_slice_in_dim(tile_count, position * local_tiles, local_tiles, 0)
    own_audio = lax.dynamic_slice_in_dim(audio_list, position * local_tiles, local_tiles, 0)
    tile_ids = own_list - (position - 1) * local_tiles
    tile_mask = jnp.repeat(slot_order[None, :] < own_count[:, None], TILE, axis=1)
    audio_ids = own_audio - (position - 1)
    audio_mask = jnp.ones((local_tiles, audio_list.shape[1] * audio_rows), dtype=bool)
    query_tiles = video_query.reshape(clip_count, local_tiles, TILE, model_width)
    dout_tiles = out_cotangent.reshape(clip_count, local_tiles, TILE, model_width)
    gated_tiles = gated_full.reshape(clip_count, local_tiles, TILE, model_width)
    grad_query, video_grads, audio_grads, gate_part, statistics = own_pass(
        query_tiles,
        dout_tiles,
        gated_tiles,
        video_window,
        audio_window,
        tile_ids,
        tile_mask,
        audio_ids,
        audio_mask,
    )
    lower_send = jnp.concatenate(
        (
            video_grads[:, :, :local_tiles].reshape(2, clip_count, row_count, model_width),
            audio_grads[:, :, 0],
        ),
        axis=2,
    )
    upper_send = jnp.concatenate(
        (
            video_grads[:, :, 2 * local_tiles :].reshape(2, clip_count, row_count, model_width),
            audio_grads[:, :, 2],
        ),
        axis=2,
    )
    from_upper = passed_along(lower_send, "ctx", -1)
    from_lower = passed_along(upper_send, "ctx", 1)
    arrived = from_upper + from_lower
    video_extra = arrived[:, :, :row_count]
    audio_extra = arrived[:, :, row_count:]
    video_total = (
        video_grads[:, :, local_tiles : 2 * local_tiles].reshape(
            2, clip_count, row_count, model_width
        )
        + video_extra
    )
    audio_total = audio_grads[:, :, 1] + audio_extra
    gate_total = lax.psum(gate_part, ("dp", "ctx"))
    query_out = grad_query.reshape(clip_count, row_count, model_width).astype(jnp.bfloat16)
    return (
        query_out,
        video_total[0].astype(jnp.bfloat16),
        video_total[1].astype(jnp.bfloat16),
        audio_total[0].astype(jnp.bfloat16),
        audio_total[1].astype(jnp.bfloat16),
        gate_total,
    )


def solution(mesh):
    placed = (
        P("dp", "ctx", None),
        P("dp", "ctx", None),
        P("dp", "ctx", None),
        P("dp", "ctx", None),
        P("dp", "ctx", None),
        P(),
        P("dp", "ctx", None),
        P(),
        P(),
        P(),
    )
    return jax.shard_map(
        per_device,
        mesh=mesh,
        in_specs=placed,
        out_specs=(
            P("dp", "ctx", None),
            P("dp", "ctx", None),
            P("dp", "ctx", None),
            P("dp", "ctx", None),
            P("dp", "ctx", None),
            P(),
        ),
        check_vma=False,
    )
```

profile of v0, /device:TPU:1, one launch (start us, length us, event | category | flops | bytes accessed | tf_op | source)
XLA Modules:
  0.0 341.1 jit_solution(7197152418343410977)
XLA Ops:
  0.7 2.8 maximum_maximum_fusion
  3.5 5.1 %collective-permute-start.1 = (bf16[2,1,144,3072]{3,2,1,0:T(8,128)(2,1)}, bf16[2,1,144,3072]{3,2,1,0:T(8,128)(2,1)S(1)}, u32[]{:S(2)}, u32[]{:S(2)}) collective-permute-start(bf16[2,1,144,3072]{3,2,1,0:T(8,128)(2,1)} %maximum_maximum_fusion), channel_id=1, source_target_pairs={{1,0},{2,1},{3,2},{4,3},{5,4},{6,5},{7,6},{8,7},{9,8},{10,9},{11,1... | collective-permute-start | bytes 5308424 | tf_op jit(solution)/shard_map/ppermute | solution.py:23
  8.7 1.9 collective-permute-start
  13.6 2.2 multiply_convert_fusion
  15.8 13.1 %collective-permute-done.1 = bf16[2,1,144,3072]{3,2,1,0:T(8,128)(2,1)S(1)} collective-permute-done((bf16[2,1,144,3072]{3,2,1,0:T(8,128)(2,1)}, bf16[2,1,144,3072]{3,2,1,0:T(8,128)(2,1)S(1)}, u32[]{:S(2)}, u32[]{:S(2)}) %collective-permute-start.1) | collective-permute-done | bytes 1769504 | tf_op jit(solution)/shard_map/ppermute | solution.py:23
  32.7 2.4 pad_maximum_fusion.1
  37.8 4.8 %broadcast_in_dim.101 = f32[2,1,6,64,3072]{4,3,2,1,0:T(8,128)} broadcast(f32[]{:T(128)} %constant.88.clone.1), dimensions={} | broadcast | bytes 9437188 | tf_op jit(solution)/shard_map/broadcast_in_dim | solution.py:220
  42.6 157.6 %while.21 = (s32[]{:T(128)}, bf16[1,2,64,3072]{3,2,1,0:T(8,128)(2,1)}, f32[2,1,6,64,3072]{4,3,2,1,0:T(8,128)}, f32[2,1,3,16,3072]{4,3,0,2,1:T(8,128)}, f32[3072]...) while((s32[]{:T(128)}, ...), condition=%wide.wide.region_12.15_spmd.clone, body=%wide.wide.region_0.14_spmd.clone.sunk | while | flops 461927552 | bytes 116885336 | solution.py:225
  54.1 1.6 dynamic-slice_bitcast_fusion.9
  60.3 2.1 multiply_reduce_fusion.3
  68.5 1.7 reshape.724
  70.2 1.8 scatter_fusion.3
  74.7 1.9 convolution_bitcast_fusion.14
  76.6 2.1 copy.281
  81.5 1.8 copy.282
  83.3 2.7 reshape.722
  86.2 3.4 scatter_fusion
  89.8 3.4 scatter_fusion.1
  93.2 2.1 maximum_dynamic-update-slice_fusion.3
  106.7 1.6 dynamic-slice_bitcast_fusion.9
  112.9 2.1 multiply_reduce_fusion.3
  121.1 1.7 reshape.724
  122.8 1.8 scatter_fusion.3
  127.3 1.9 convolution_bitcast_fusion.14
  129.2 2.1 copy.281
  134.1 1.8 copy.282
  135.9 2.7 reshape.722
  138.8 3.4 scatter_fusion
  142.4 3.4 scatter_fusion.1
  145.8 2.1 maximum_dynamic-update-slice_fusion.3
  159.3 1.6 dynamic-slice_bitcast_fusion.9
  165.6 2.1 multiply_reduce_fusion.3
  173.7 1.7 reshape.724
  175.4 1.8 scatter_fusion.3
  179.8 1.9 convolution_bitcast_fusion.14
  181.7 2.1 copy.281
  186.6 1.8 copy.282
  188.5 2.7 reshape.722
  191.4 3.4 scatter_fusion
  194.9 3.4 scatter_fusion.1
  198.3 2.0 maximum_dynamic-update-slice_fusion.3
  201.5 4.5 %fusion.39 = (f32[2,1,2,64,3072]{4,3,2,1,0:T(8,128)S(1)}, f32[2,1,2,64,3072]{4,3,2,1,0:T(8,128)S(1)}, f32[2,1,2,64,3072]{4,3,2,1,0:T(8,128)S(1)}) fusion(f32[2,1,6,64,3072]{4,3,2,1,0:T(8,128)} %get-tuple-element.226), kind=kLoop, calls=%fused_computation.102 | loop fusion | bytes 18874368 | tf_op jit(solution)/shard_map/slice | solution.py:306
  205.9 2.1 pad_maximum_fusion.3
  208.0 4.2 %collective-permute-start.3 = (f32[2,1,144,3072]{3,2,1,0:T(8,128)}, f32[2,1,144,3072]{3,2,1,0:T(8,128)}, u32[]{:S(2)}, u32[]{:S(2)}) collective-permute-start(f32[2,1,144,3072]{3,2,1,0:T(8,128)} %pad_maximum_fusion.3), channel_id=1, source_target_pairs={{0,1},{1,2},{2,3},{3,4},{4,5},{5,6},{6,7},{7,8},{8,9},{9,10},{10,1... | collective-permute-start | bytes 10616840 | tf_op jit(solution)/shard_map/ppermute | solution.py:33
  212.2 2.1 pad_maximum_fusion.2
  214.3 1.9 collective-permute-start.2
  216.2 117.7 %psum.7 = f32[3072]{0:T(1024)} all-reduce(f32[3072]{0:T(1024)S(1)} %copy-done.25), channel_id=1, replica_groups=mesh['dp'=4,'ctx'=64] {'dp','ctx'}, use_global_device_ids=true, to_apply=%region_13.16 | all-reduce | flops 3072 | bytes 24576 | tf_op jit(solution)/shard_map/psum | solution.py:312
  333.9 3.6 %add.111 = f32[2,1,144,3072]{3,2,1,0:T(8,128)S(1)} add(f32[2,1,144,3072]{3,2,1,0:T(8,128)} %collective-permute-done.2, f32[2,1,144,3072]{3,2,1,0:T(8,128)} %collective-permute-done.3) | non-fusion elementwise | flops 884736 | bytes 10616832 | tf_op jit(solution)/shard_map/add | solution.py:302
  (368 shorter events, 96.7 us)
Async XLA Ops:
  0.6 11.4 %copy-start = (s32[128,4]{0,1:T(4,128)S(1)}, s32[128,4]{0,1:T(4,128)}, u32[]{:S(2)}) copy-start(s32[128,4]{0,1:T(4,128)} %param.23) | copy-start | bytes 6148
  0.6 10.0 %copy-start.32 = (s32[128]{0:T(128)S(1)}, s32[128]{0:T(128)}, u32[]{:S(2)}) copy-start(s32[128]{0:T(128)} %param.24) | copy-start | bytes 1540
  0.7 10.5 %copy-start.31 = (s32[128,2]{0,1:T(2,128)S(1)}, s32[128,2]{0,1:T(2,128)}, u32[]{:S(2)}) copy-start(s32[128,2]{0,1:T(2,128)} %param.25) | copy-start | bytes 3076
  3.5 25.3 %collective-permute-start.1 = (bf16[2,1,144,3072]{3,2,1,0:T(8,128)(2,1)}, bf16[2,1,144,3072]{3,2,1,0:T(8,128)(2,1)S(1)}, u32[]{:S(2)}, u32[]{:S(2)}) collective-permute-start(bf16[2,1,144,3072]{3,2,1,0:T(8,128)(2,1)} %maximum_maximum_fusion), channel_id=1, source_target_pairs={{1,0},{2,1},{3,2},{4,3},{5,4},{6,5},{7,6},{8,7},{9,8},{10,9},{11,1... | collective-permute-start | bytes 5308424 | tf_op jit(solution)/shard_map/ppermute | solution.py:23
  8.7 21.7 %collective-permute-start = (bf16[2,1,144,3072]{3,2,1,0:T(8,128)(2,1)}, bf16[2,1,144,3072]{3,2,1,0:T(8,128)(2,1)S(1)}, u32[]{:S(2)}, u32[]{:S(2)}) collective-permute-start(bf16[2,1,144,3072]{3,2,1,0:T(8,128)(2,1)} %maximum_maximum_fusion), channel_id=1, source_target_pairs={{0,1},{1,2},{2,3},{3,4},{4,5},{5,6},{6,7},{7,8},{8,9},{9,10},{10,1... | collective-permute-start | bytes 5308424 | tf_op jit(solution)/shard_map/ppermute | solution.py:21
  12.2 18.1 %copy-start.23 = (bf16[1,16,3072]{2,1,0:T(8,128)(2,1)S(1)}, bf16[1,16,3072]{2,1,0:T(8,128)(2,1)}, u32[]{:S(2)}) copy-start(bf16[1,16,3072]{2,1,0:T(8,128)(2,1)} %param.20) | copy-start | bytes 294916
  12.3 18.1 %copy-start.24 = (bf16[1,16,3072]{2,1,0:T(8,128)(2,1)S(1)}, bf16[1,16,3072]{2,1,0:T(8,128)(2,1)}, u32[]{:S(2)}) copy-start(bf16[1,16,3072]{2,1,0:T(8,128)(2,1)} %param.19) | copy-start | bytes 294916
  42.7 5.2 %copy-start.26 = (s32[2,2]{1,0:T(2,128)}, s32[2,2]{1,0:T(2,128)S(1)}, u32[]{:S(2)}) copy-start(s32[2,2]{1,0:T(2,128)S(1)} %get-tuple-element.581) | copy-start | bytes 52 | tf_op jit(solution)/shard_map/while
  46.5 2.9 copy-start.17
  47.6 3.7 %copy-start.4 = (bf16[16,8,8,128]{3,2,1,0:T(8,128)(2,1)}, bf16[16,8,8,128]{3,2,1,0:T(8,128)(2,1)S(1)}, u32[]{:S(2)}) copy-start(bf16[16,8,8,128]{3,2,1,0:T(8,128)(2,1)S(1)} %copy.270) | copy-start | bytes 786436 | tf_op jit(solution)/shard_map/while
  50.4 1.8 copy-start.8
  50.4 1.8 copy-start.10
  59.1 6.2 %copy-start.19 = (f32[2,8,64]{2,1,0:T(8,128)}, f32[2,8,64]{2,1,0:T(8,128)S(1)}, u32[]{:S(2)}) copy-start(f32[2,8,64]{2,1,0:T(8,128)S(1)} %log_add_fusion.7) | copy-start | bytes 12292 | tf_op jit(solution)/shard_map/while
  59.6 4.2 %copy-start.7 = (bf16[16,8,8,128]{3,2,1,0:T(8,128)(2,1)S(1)}, bf16[16,8,8,128]{3,2,1,0:T(8,128)(2,1)}, u32[]{:S(2)}) copy-start(bf16[16,8,8,128]{3,2,1,0:T(8,128)(2,1)} %copy-done.6) | copy-start | bytes 786436 | tf_op jit(solution)/shard_map/while
  60.3 5.1 %copy-start.12 = (bf16[16,8,8,128]{3,2,1,0:T(8,128)(2,1)S(1)}, bf16[16,8,8,128]{3,2,1,0:T(8,128)(2,1)}, u32[]{:S(2)}) copy-start(bf16[16,8,8,128]{3,2,1,0:T(8,128)(2,1)} %copy.279) | copy-start | bytes 786436 | tf_op jit(solution)/shard_map/while
  64.0 3.6 %copy-start.16 = (bf16[2,8,64,32]{2,3,1,0:T(8,128)(2,1)}, bf16[2,8,64,32]{2,3,1,0:T(8,128)(2,1)S(1)}, u32[]{:S(2)}) copy-start(bf16[2,8,64,32]{2,3,1,0:T(8,128)(2,1)S(1)} %fusion.120) | copy-start | bytes 196612 | tf_op jit(solution)/shard_map/while
  65.4 6.7 %copy-start.18 = (bf16[8,8,8,128]{3,2,1,0:T(8,128)(2,1)S(1)}, bf16[8,8,8,128]{3,2,1,0:T(8,128)(2,1)}, u32[]{:S(2)}) copy-start(bf16[8,8,8,128]{3,2,1,0:T(8,128)(2,1)} %copy-done.17) | copy-start | bytes 393220 | tf_op jit(solution)/shard_map/while
  65.9 7.3 %copy-start.3 = (bf16[64,8,8,128]{3,2,1,0:T(8,128)(2,1)S(1)}, bf16[64,8,8,128]{3,2,1,0:T(8,128)(2,1)}, u32[]{:S(2)}) copy-start(bf16[64,8,8,128]{3,2,1,0:T(8,128)(2,1)} %copy-done.2) | copy-start | bytes 3145732 | tf_op jit(solution)/shard_map/while
  93.2 2.1 copy-start.27
  93.2 2.1 copy-start.29
  95.2 5.2 %copy-start.26 = (s32[2,2]{1,0:T(2,128)}, s32[2,2]{1,0:T(2,128)S(1)}, u32[]{:S(2)}) copy-start(s32[2,2]{1,0:T(2,128)S(1)} %get-tuple-element.581) | copy-start | bytes 52 | tf_op jit(solution)/shard_map/while
  99.1 2.9 copy-start.17
  100.2 3.7 %copy-start.4 = (bf16[16,8,8,128]{3,2,1,0:T(8,128)(2,1)}, bf16[16,8,8,128]{3,2,1,0:T(8,128)(2,1)S(1)}, u32[]{:S(2)}) copy-start(bf16[16,8,8,128]{3,2,1,0:T(8,128)(2,1)S(1)} %copy.270) | copy-start | bytes 786436 | tf_op jit(solution)/shard_map/while
  103.0 1.8 copy-start.8
  111.7 6.2 %copy-start.19 = (f32[2,8,64]{2,1,0:T(8,128)}, f32[2,8,64]{2,1,0:T(8,128)S(1)}, u32[]{:S(2)}) copy-start(f32[2,8,64]{2,1,0:T(8,128)S(1)} %log_add_fusion.7) | copy-start | bytes 12292 | tf_op jit(solution)/shard_map/while
  112.2 4.2 %copy-start.7 = (bf16[16,8,8,128]{3,2,1,0:T(8,128)(2,1)S(1)}, bf16[16,8,8,128]{3,2,1,0:T(8,128)(2,1)}, u32[]{:S(2)}) copy-start(bf16[16,8,8,128]{3,2,1,0:T(8,128)(2,1)} %copy-done.6) | copy-start | bytes 786436 | tf_op jit(solution)/shard_map/while
  112.9 5.1 %copy-start.12 = (bf16[16,8,8,128]{3,2,1,0:T(8,128)(2,1)S(1)}, bf16[16,8,8,128]{3,2,1,0:T(8,128)(2,1)}, u32[]{:S(2)}) copy-start(bf16[16,8,8,128]{3,2,1,0:T(8,128)(2,1)} %copy.279) | copy-start | bytes 786436 | tf_op jit(solution)/shard_map/while
  116.6 3.6 %copy-start.16 = (bf16[2,8,64,32]{2,3,1,0:T(8,128)(2,1)}, bf16[2,8,64,32]{2,3,1,0:T(8,128)(2,1)S(1)}, u32[]{:S(2)}) copy-start(bf16[2,8,64,32]{2,3,1,0:T(8,128)(2,1)S(1)} %fusion.120) | copy-start | bytes 196612 | tf_op jit(solution)/shard_map/while
  118.0 6.7 %copy-start.18 = (bf16[8,8,8,128]{3,2,1,0:T(8,128)(2,1)S(1)}, bf16[8,8,8,128]{3,2,1,0:T(8,128)(2,1)}, u32[]{:S(2)}) copy-start(bf16[8,8,8,128]{3,2,1,0:T(8,128)(2,1)} %copy-done.17) | copy-start | bytes 393220 | tf_op jit(solution)/shard_map/while
  118.5 7.3 %copy-start.3 = (bf16[64,8,8,128]{3,2,1,0:T(8,128)(2,1)S(1)}, bf16[64,8,8,128]{3,2,1,0:T(8,128)(2,1)}, u32[]{:S(2)}) copy-start(bf16[64,8,8,128]{3,2,1,0:T(8,128)(2,1)} %copy-done.2) | copy-start | bytes 3145732 | tf_op jit(solution)/shard_map/while
  145.8 2.1 copy-start.27
  145.8 2.1 copy-start.29
  147.9 5.2 %copy-start.26 = (s32[2,2]{1,0:T(2,128)}, s32[2,2]{1,0:T(2,128)S(1)}, u32[]{:S(2)}) copy-start(s32[2,2]{1,0:T(2,128)S(1)} %get-tuple-element.581) | copy-start | bytes 52 | tf_op jit(solution)/shard_map/while
  151.7 2.9 copy-start.17
  152.8 3.7 %copy-start.4 = (bf16[16,8,8,128]{3,2,1,0:T(8,128)(2,1)}, bf16[16,8,8,128]{3,2,1,0:T(8,128)(2,1)S(1)}, u32[]{:S(2)}) copy-start(bf16[16,8,8,128]{3,2,1,0:T(8,128)(2,1)S(1)} %copy.270) | copy-start | bytes 786436 | tf_op jit(solution)/shard_map/while
  155.7 1.8 copy-start.8
  164.4 6.2 %copy-start.19 = (f32[2,8,64]{2,1,0:T(8,128)}, f32[2,8,64]{2,1,0:T(8,128)S(1)}, u32[]{:S(2)}) copy-start(f32[2,8,64]{2,1,0:T(8,128)S(1)} %log_add_fusion.7) | copy-start | bytes 12292 | tf_op jit(solution)/shard_map/while
  164.8 4.2 %copy-start.7 = (bf16[16,8,8,128]{3,2,1,0:T(8,128)(2,1)S(1)}, bf16[16,8,8,128]{3,2,1,0:T(8,128)(2,1)}, u32[]{:S(2)}) copy-start(bf16[16,8,8,128]{3,2,1,0:T(8,128)(2,1)} %copy-done.6) | copy-start | bytes 786436 | tf_op jit(solution)/shard_map/while
  165.6 5.1 %copy-start.12 = (bf16[16,8,8,128]{3,2,1,0:T(8,128)(2,1)S(1)}, bf16[16,8,8,128]{3,2,1,0:T(8,128)(2,1)}, u32[]{:S(2)}) copy-start(bf16[16,8,8,128]{3,2,1,0:T(8,128)(2,1)} %copy.279) | copy-start | bytes 786436 | tf_op jit(solution)/shard_map/while
  169.2 3.6 %copy-start.16 = (bf16[2,8,64,32]{2,3,1,0:T(8,128)(2,1)}, bf16[2,8,64,32]{2,3,1,0:T(8,128)(2,1)S(1)}, u32[]{:S(2)}) copy-start(bf16[2,8,64,32]{2,3,1,0:T(8,128)(2,1)S(1)} %fusion.120) | copy-start | bytes 196612 | tf_op jit(solution)/shard_map/while
  170.6 6.6 %copy-start.18 = (bf16[8,8,8,128]{3,2,1,0:T(8,128)(2,1)S(1)}, bf16[8,8,8,128]{3,2,1,0:T(8,128)(2,1)}, u32[]{:S(2)}) copy-start(bf16[8,8,8,128]{3,2,1,0:T(8,128)(2,1)} %copy-done.17) | copy-start | bytes 393220 | tf_op jit(solution)/shard_map/while
  171.2 7.2 %copy-start.3 = (bf16[64,8,8,128]{3,2,1,0:T(8,128)(2,1)S(1)}, bf16[64,8,8,128]{3,2,1,0:T(8,128)(2,1)}, u32[]{:S(2)}) copy-start(bf16[64,8,8,128]{3,2,1,0:T(8,128)(2,1)} %copy-done.2) | copy-start | bytes 3145732 | tf_op jit(solution)/shard_map/while
  198.3 2.0 copy-start.27
  198.3 2.0 copy-start.29
  208.0 125.9 %collective-permute-start.3 = (f32[2,1,144,3072]{3,2,1,0:T(8,128)}, f32[2,1,144,3072]{3,2,1,0:T(8,128)}, u32[]{:S(2)}, u32[]{:S(2)}) collective-permute-start(f32[2,1,144,3072]{3,2,1,0:T(8,128)} %pad_maximum_fusion.3), channel_id=1, source_target_pairs={{0,1},{1,2},{2,3},{3,4},{4,5},{5,6},{6,7},{7,8},{8,9},{9,10},{10,1... | collective-permute-start | bytes 10616840 | tf_op jit(solution)/shard_map/ppermute | solution.py:33
  212.2 4.0 %copy-start.25 = (f32[3072]{0:T(1024)S(1)}, f32[3072]{0:T(1024)}, u32[]{:S(2)}) copy-start(f32[3072]{0:T(1024)} %get-tuple-element.228) | copy-start | bytes 36868
  214.3 119.6 %collective-permute-start.2 = (f32[2,1,144,3072]{3,2,1,0:T(8,128)}, f32[2,1,144,3072]{3,2,1,0:T(8,128)}, u32[]{:S(2)}, u32[]{:S(2)}) collective-permute-start(f32[2,1,144,3072]{3,2,1,0:T(8,128)} %pad_maximum_fusion.2), channel_id=1, source_target_pairs={{1,0},{2,1},{3,2},{4,3},{5,4},{6,5},{7,6},{8,7},{9,8},{10,9},{11,1... | collective-permute-start | bytes 10616840 | tf_op jit(solution)/shard_map/ppermute | solution.py:33
  338.6 2.5 copy-start.1
  (37 other events, 44.4 us)
where the time goes:
time: 343 us; the launch traced here: 341 us
  blocking collectives  118 us (34%)
  local copies, waits for them, and re-layouts  101 us (29%)
  other arithmetic  72.2 us (21%)
  matrix products  19.5 us (6%)
  waiting for transfers between devices  14.6 us (4%)
  starting transfers between devices  13.2 us (4%)
    psum x1, blocking collectives, per_device(): gate_total = lax.psum(gate_part, ('dp', 'ctx'))  118 us
    scatter-add x12, other arithmetic, spread_slots(): jax.ops.segment_sum(leading, slot_ids.reshape(-1), num_segments=window_co...  28.2 us
    reshape x12, local copies, waits for them, and re-layouts, spread_slots(): leading = jnp.moveaxis(blocks, 1, 0)  17.9 us
    ppermute x1, waiting for transfers between devices, padded(): lax.ppermute(head, axis, [((i + 1) % count, i) for i in range(ends)])  13.1 us
    while x165, local copies, waits for them, and re-layouts  11.3 us
    dynamic_update_slice x6, other arithmetic, channel_put(): lax.dynamic_update_slice_in_dim(array, piece, group_id * group_width, arr...  8.52 us
    mul x6, local copies, waits for them, and re-layouts, attend_back(): jnp.einsum('cnhlk,cnlhe->cnkhe', score_grads, split_heads(queries, group_...  8.11 us
    reduce_sum x6, other arithmetic, head_sums(): return jnp.swapaxes(jnp.sum(product, axis=-1), -1, -2)  7.63 us
  transfers between devices with their start and end apart: 4, of which 2 were waited for; matrix products, arithmetic and copies ran while one was open for 2% of the time, Pallas kernels for 0%

commit v1 on v0

v1 whole, which is shorter than its diff:
```python
import functools
import math

import jax
import jax.numpy as jnp
from jax import lax
from jax.experimental import pallas as pl
from jax.experimental.pallas import tpu as pltpu
from jax.sharding import PartitionSpec as P

HEAD_DIM = 128
TILE = 64
SCALE = 1.0 / math.sqrt(HEAD_DIM)
SCORE_FACTOR = SCALE * math.log2(math.e)
NEG_INF = float("-inf")


def dot_t(a, b):
    return lax.dot_general(a, b, (((1,), (1,)), ((), ())), preferred_element_type=jnp.float32)


def dot(a, b):
    return lax.dot_general(a, b, (((1,), (0,)), ((), ())), preferred_element_type=jnp.float32)


def dot_lead(a, b):
    return lax.dot_general(a, b, (((0,), (0,)), ((), ())), preferred_element_type=jnp.float32)


def mate_of(position):
    return position + 1 - 2 * lax.rem(position, 2)


def far_of(position):
    return position - 1 + 2 * lax.rem(position, 2)


def tile_bias(list_ref, count_ref, row_tile, key_tile):
    tiles, slots = list_ref.shape
    row = jnp.clip(row_tile, 0, tiles - 1)
    inside = row == row_tile
    hit = jnp.bool_(False)
    for j in range(slots):
        hit = hit | ((list_ref[row, j] == key_tile) & (j < count_ref[row]))
    return jnp.where(hit & inside, 0.0, NEG_INF).astype(jnp.float32)


def block_bias(list_ref, row_tile, block):
    tiles, slots = list_ref.shape
    row = jnp.clip(row_tile, 0, tiles - 1)
    inside = row == row_tile
    hit = jnp.bool_(False)
    for j in range(slots):
        hit = hit | (list_ref[row, j] == block)
    return jnp.where(hit & inside, 0.0, NEG_INF).astype(jnp.float32)


def lanes_of(first, second):
    lane = lax.broadcasted_iota(jnp.int32, (1, 2 * TILE), 1)
    return jnp.where(lane < TILE, first, second)


def own_video_rows(list_ref, count_ref, position):
    rows = []
    for holder in (position, mate_of(position), far_of(position)):
        for w in range(2):
            key_tile = 2 * holder + w
            rows.append(
                lanes_of(
                    tile_bias(list_ref, count_ref, 2 * position, key_tile),
                    tile_bias(list_ref, count_ref, 2 * position + 1, key_tile),
                )
            )
    return rows


def own_audio_rows(list_ref, position):
    rows = []
    for block in (position, mate_of(position), far_of(position)):
        rows.append(
            lanes_of(
                block_bias(list_ref, 2 * position, block),
                block_bias(list_ref, 2 * position + 1, block),
            )
        )
    return rows


def masked(scores, rows, height):
    return jnp.concatenate(
        [scores[i * height : (i + 1) * height] * SCORE_FACTOR + row for i, row in enumerate(rows)],
        axis=0,
    )


def softmax_cols(scores):
    top = jnp.max(scores, axis=0, keepdims=True)
    grown = jnp.exp2(scores - top)
    total = jnp.sum(grown, axis=0, keepdims=True)
    return grown * (1.0 / total), top + jnp.log2(total)


def gate_kernel(position_ref, audio_list, q_ref, do_ref, ak0, ak1, ak2, av0, av1, av2, gate_out):
    rows = own_audio_rows(audio_list, position_ref[0])
    block = ak0.shape[0]
    for h in range(q_ref.shape[1] // HEAD_DIM):
        cols = slice(h * HEAD_DIM, (h + 1) * HEAD_DIM)
        keys = jnp.concatenate([ak0[:, cols], ak1[:, cols], ak2[:, cols]], axis=0)
        values = jnp.concatenate([av0[:, cols], av1[:, cols], av2[:, cols]], axis=0)
        scores = masked(dot_t(keys, q_ref[:, cols]), rows, block)
        prob, _ = softmax_cols(scores)
        spread = dot(prob.astype(jnp.bfloat16), do_ref[:, cols])
        gate_out[:, cols] = jnp.sum(spread * values.astype(jnp.float32), axis=0, keepdims=True)


def own_kernel(
    position_ref,
    tile_list,
    tile_count,
    audio_list,
    q_ref,
    do_ref,
    k0,
    k1,
    k2,
    v0,
    v1,
    v2,
    ak0,
    ak1,
    ak2,
    av0,
    av1,
    av2,
    gate_ref,
    dq_out,
    dk_out,
    dv_out,
    dak_out,
    dav_out,
    stat_out,
):
    position = position_ref[0]
    video_rows = own_video_rows(tile_list, tile_count, position)
    audio_rows = own_audio_rows(audio_list, position)
    own = k0.shape[0]
    window = 3 * own
    block = ak0.shape[0]
    for h in range(q_ref.shape[1] // HEAD_DIM):
        cols = slice(h * HEAD_DIM, (h + 1) * HEAD_DIM)
        q = q_ref[:, cols]
        do = do_ref[:, cols]
        gated = (gate_ref[:, cols] * do.astype(jnp.float32)).astype(jnp.bfloat16)
        keys = jnp.concatenate([r[:, cols] for r in (k0, k1, k2, ak0, ak1, ak2)], axis=0)
        raw = dot_t(keys, q)
        video_prob, video_total = softmax_cols(masked(raw[:window], video_rows, TILE))
        cross_prob, cross_total = softmax_cols(masked(raw[window:], audio_rows, block))
        video_weights = video_prob.astype(jnp.bfloat16)
        cross_weights = cross_prob.astype(jnp.bfloat16)
        values = jnp.concatenate([r[:, cols] for r in (v0, v1, v2)], axis=0)
        audio_values = jnp.concatenate([r[:, cols] for r in (av0, av1, av2)], axis=0)
        video_dp = dot_t(values, do)
        cross_dp = dot_t(audio_values, gated)
        video_delta = jnp.sum(video_weights.astype(jnp.float32) * video_dp, axis=0, keepdims=True)
        cross_delta = jnp.sum(cross_weights.astype(jnp.float32) * cross_dp, axis=0, keepdims=True)
        video_ds = (video_prob * (video_dp - video_delta)).astype(jnp.bfloat16)
        cross_ds = (cross_prob * (cross_dp - cross_delta)).astype(jnp.bfloat16)
        both_ds = jnp.concatenate([video_ds, cross_ds], axis=0)
        dq_out[:, cols] = (dot_lead(both_ds, keys) * SCALE).astype(jnp.bfloat16)
        dk_out[:, cols] = dot(video_ds[:own], q)
        dv_out[:, cols] = dot(video_weights[:own], do)
        dak_out[:, cols] = dot(cross_ds[:block], q)
        dav_out[:, cols] = dot(cross_weights[:block], gated)
        stat_out[4 * h : 4 * h + 4, :] = jnp.concatenate(
            [video_total, video_delta, cross_total, cross_delta], axis=0
        )


def beside_kernel(
    far,
    last,
    position_ref,
    tile_list,
    tile_count,
    audio_list,
    q_ref,
    do_ref,
    stat_ref,
    k_ref,
    v_ref,
    ak_ref,
    av_ref,
    gate_ref,
    dk_in,
    dv_in,
    dak_in,
    dav_in,
    dk_out,
    dv_out,
    dak_out,
    dav_out,
):
    position = position_ref[0]
    beside = far_of(position) if far else mate_of(position)
    video_rows = [
        lanes_of(
            tile_bias(tile_list, tile_count, 2 * beside, 2 * position + w),
            tile_bias(tile_list, tile_count, 2 * beside + 1, 2 * position + w),
        )
        for w in range(2)
    ]
    audio_row = lanes_of(
        block_bias(audio_list, 2 * beside, position),
        block_bias(audio_list, 2 * beside + 1, position),
    )
    own = k_ref.shape[0]
    factor = SCALE if last else 1.0
    for h in range(q_ref.shape[1] // HEAD_DIM):
        cols = slice(h * HEAD_DIM, (h + 1) * HEAD_DIM)
        q = q_ref[:, cols]
        do = do_ref[:, cols]
        gated = (gate_ref[:, cols] * do.astype(jnp.float32)).astype(jnp.bfloat16)
        stats = stat_ref[4 * h : 4 * h + 4, :]
        keys = jnp.concatenate([k_ref[:, cols], ak_ref[:, cols]], axis=0)
        raw = dot_t(keys, q)
        video_prob = jnp.exp2(masked(raw[:own], video_rows, TILE) - stats[0:1])
        cross_prob = jnp.exp2(raw[own:] * SCORE_FACTOR + audio_row - stats[2:3])
        video_dp = dot_t(v_ref[:, cols], do)
        cross_dp = dot_t(av_ref[:, cols], gated)
        video_ds = (video_prob * (video_dp - stats[1:2])).astype(jnp.bfloat16)
        cross_ds = (cross_prob * (cross_dp - stats[3:4])).astype(jnp.bfloat16)
        from_q = dot(jnp.concatenate([video_ds, cross_ds], axis=0), q)
        dk_out[:, cols] = ((dk_in[:, cols] + from_q[:own]) * factor).astype(dk_out.dtype)
        dak_out[:, cols] = ((dak_in[:, cols] + from_q[own:]) * factor).astype(dak_out.dtype)
        dv_out[:, cols] = (dv_in[:, cols] + dot(video_prob.astype(jnp.bfloat16), do)).astype(
            dv_out.dtype
        )
        dav_out[:, cols] = (dav_in[:, cols] + dot(cross_prob.astype(jnp.bfloat16), gated)).astype(
            dav_out.dtype
        )


def heads_per_step(heads, most):
    return max(g for g in range(1, most + 1) if heads % g == 0)


SMEM = pl.BlockSpec(memory_space=pltpu.SMEM)


def cols_spec(rows, width):
    return pl.BlockSpec((rows, width), lambda i: (0, i))


def cost(flops, arrays):
    return pl.CostEstimate(
        flops=flops,
        bytes_accessed=sum(a.size * a.dtype.itemsize for a in arrays),
        transcendentals=0,
    )


def per_device(
    video_query,
    video_key,
    video_value,
    audio_key,
    audio_value,
    cross_gate,
    out_cotangent,
    tile_list,
    tile_count,
    audio_list,
):
    clips, rows, width = video_query.shape
    block = audio_key.shape[1]
    heads = width // HEAD_DIM
    count = lax.axis_size("ctx")
    position = lax.axis_index("ctx").astype(jnp.int32).reshape(1)
    mate_pairs = [(i, i ^ 1) for i in range(count)]
    far_pairs = [(i + s, i + 1 - s) for i in range(1, count - 1, 2) for s in range(2)]

    def to_mate(x):
        return lax.ppermute(x, "ctx", mate_pairs)

    def to_far(x):
        return lax.ppermute(x, "ctx", far_pairs)

    q, k, v, do = (x.reshape(rows, width) for x in (video_query, video_key, video_value, out_cotangent))
    ak, av = (x.reshape(block, width) for x in (audio_key, audio_value))
    gate = cross_gate.reshape(1, width)

    ak_far, av_far = to_far(ak), to_far(av)
    ak_mate, av_mate = to_mate(ak), to_mate(av)
    k_far, v_far = to_far(k), to_far(v)
    k_mate, v_mate = to_mate(k), to_mate(v)
    q_far, do_far = to_far(q), to_far(do)
    q_mate, do_mate = to_mate(q), to_mate(do)

    group = heads_per_step(heads, 4)
    step = group * HEAD_DIM
    grid = (heads // group,)
    vspec = cols_spec(rows, step)
    aspec = cols_spec(block, step)
    gspec = cols_spec(1, step)
    sspec = pl.BlockSpec((4 * group, rows), lambda i: (i, 0))
    f32, bf16 = jnp.float32, jnp.bfloat16

    def array(n, dtype):
        return jax.ShapeDtypeStruct((n, width), dtype)

    gate_args = (q, do, ak, ak_mate, ak_far, av, av_mate, av_far)
    gate_part = pl.pallas_call(
        gate_kernel,
        grid=grid,
        in_specs=[SMEM, SMEM] + [vspec] * 2 + [aspec] * 6,
        out_specs=gspec,
        out_shape=array(1, f32),
        cost_estimate=cost(4 * rows * 3 * block * width, gate_args),
        name="gate_terms",
    )(position, audio_list, *gate_args)

    own_args = (q, do, k, k_mate, k_far, v, v_mate, v_far, ak, ak_mate, ak_far, av, av_mate, av_far)
    dq, dk, dv, dak, dav, stats = pl.pallas_call(
        own_kernel,
        grid=grid,
        in_specs=[SMEM] * 4 + [vspec] * 8 + [aspec] * 6 + [gspec],
        out_specs=[vspec] * 3 + [aspec] * 2 + [sspec],
        out_shape=[
            array(rows, bf16),
            array(rows, f32),
            array(rows, f32),
            array(block, f32),
            array(block, f32),
            jax.ShapeDtypeStruct((4 * heads, rows), f32),
        ],
        cost_estimate=cost(22 * rows * rows * width, own_args),
        name="own_queries",
    )(position, tile_list, tile_count, audio_list, *own_args, gate)

    stats_far, stats_mate = to_far(stats), to_mate(stats)

    def beside(far, last, q, do, stats, sums):
        out = bf16 if last else f32
        return pl.pallas_call(
            functools.partial(beside_kernel, far, last),
            grid=grid,
            in_specs=[SMEM] * 4
            + [vspec] * 2
            + [sspec]
            + [vspec] * 2
            + [aspec] * 2
            + [gspec]
            + [vspec] * 2
            + [aspec] * 2,
            out_specs=[vspec] * 2 + [aspec] * 2,
            out_shape=[array(rows, out), array(rows, out), array(block, out), array(block, out)],
            cost_estimate=cost(8 * rows * rows * width, (q, do, k, v) + tuple(sums)),
            name="far_queries" if far else "mate_queries",
        )(position, tile_list, tile_count, audio_list, q, do, stats, k, v, ak, av, gate, *sums)

    sums = beside(False, False, q_mate, do_mate, stats_mate, (dk, dv, dak, dav))
    dk, dv, dak, dav = beside(True, True, q_far, do_far, stats_far, sums)

    total = gate_part
    for axis in ("ctx", "dp"):
        size = lax.axis_size(axis)
        step_bit = 1
        while step_bit < size:
            total = total + lax.ppermute(total, axis, [(i, i ^ step_bit) for i in range(size)])
            step_bit *= 2

    return (
        dq.reshape(clips, rows, width),
        dk.reshape(clips, rows, width),
        dv.reshape(clips, rows, width),
        dak.reshape(clips, block, width),
        dav.reshape(clips, block, width),
        total.reshape(width),
    )


def solution(mesh):
    placed = P("dp", "ctx", None)
    return jax.shard_map(
        per_device,
        mesh=mesh,
        in_specs=(placed,) * 5 + (P(), placed, P(), P(), P()),
        out_specs=(placed,) * 5 + (P(),),
        check_vma=False,
    )
```

time: 343 us -> 128 us (0.37)
  the two profiles are of different devices: /device:TPU:1 before, /device:TPU:24 now
where the time goes in v1:
time: 128 us; the launch traced here: 127 us
  Pallas kernels  46.7 us (36%)
  starting transfers between devices  42.4 us (33%)
  waiting for transfers between devices  31.3 us (24%)
  local copies, waits for them, and re-layouts  4.01 us (3%)
  other arithmetic  1.42 us (1%)
    ppermute x7, starting transfers between devices, to_far(): return lax.ppermute(x, 'ctx', far_pairs)  31.1 us
    ppermute x8, waiting for transfers between devices, per_device(): lax.ppermute(total, axis, [(i, i ^ step_bit) for i in range(size)])  23.7 us
    pallas_call x2, Pallas kernels, beside(): pl.pallas_call(functools.partial(beside_kernel, far, last), grid=grid, in...  20.8 us
    pallas_call x1, Pallas kernels, per_device(): pl.pallas_call(own_kernel, grid=grid, in_specs=[SMEM] * 4 + [vspec] * 8 +...  17.7 us
    ppermute x8, starting transfers between devices, per_device(): lax.ppermute(total, axis, [(i, i ^ step_bit) for i in range(size)])  9.77 us
    pallas_call x1, Pallas kernels, per_device(): pl.pallas_call(gate_kernel, grid=grid, in_specs=[SMEM, SMEM] + [vspec] *...  8.27 us
    ppermute x7, waiting for transfers between devices, to_far(): return lax.ppermute(x, 'ctx', far_pairs)  7.59 us
    unnamed x24, local copies, waits for them, and re-layouts  4.01 us
  transfers between devices with their start and end apart: 22, of which 8 were waited for; matrix products, arithmetic and copies ran while one was open for 3% of the time, Pallas kernels for 29%

profile of v1, /device:TPU:24, one launch (start us, length us, event | category | flops | bytes accessed | tf_op | source)
XLA Modules:
  0.0 126.8 jit_solution(10984588715688331406)
XLA Ops:
  0.6 0.0 copy-start
  0.6 0.0 copy-start.1
  0.7 0.1 collective-permute-start
  0.8 8.0 %collective-permute-start.1 = (bf16[128,3072]{1,0:T(8,128)(2,1)}, bf16[128,3072]{1,0:T(8,128)(2,1)S(1)}, u32[]{:S(2)}, u32[]{:S(2)}) collective-permute-start(bf16[128,3072]{1,0:T(8,128)(2,1)} %bitcast.15), channel_id=1, source_target_pairs={{1,2},{2,1},{3,4},{4,3},{5,6},{6,5},{7,8},{8,7},{9,10},{10,9},{11,... | collective-permute-start | bytes 2359304 | tf_op jit(solution)/shard_map/ppermute | solution.py:286
  8.8 0.1 collective-permute-start.2
  8.9 0.5 collective-permute-start.4
  9.4 2.6 %collective-permute-start.5 = (bf16[16,3072]{1,0:T(8,128)(2,1)}, bf16[16,3072]{1,0:T(8,128)(2,1)S(1)}, u32[]{:S(2)}, u32[]{:S(2)}) collective-permute-start(bf16[16,3072]{1,0:T(8,128)(2,1)} %bitcast.33), channel_id=1, source_target_pairs={{1,2},{2,1},{3,4},{4,3},{5,6},{6,5},{7,8},{8,7},{9,10},{10,9},{11,... | collective-permute-start | bytes 294920 | tf_op jit(solution)/shard_map/ppermute | solution.py:286
  12.0 0.0 collective-permute-done.4.ak1
  12.0 0.0 copy-start.4
  12.1 0.1 collective-permute-start.6
  12.2 7.6 %collective-permute-done.5.ak2 = bf16[16,3072]{1,0:T(8,128)(2,1)S(1)} collective-permute-done((bf16[16,3072]{1,0:T(8,128)(2,1)}, bf16[16,3072]{1,0:T(8,128)(2,1)S(1)}, u32[]{:S(2)}, u32[]{:S(2)}) %collective-permute-start.5) | collective-permute-done | bytes 98336 | tf_op jit(solution)/shard_map/ppermute | solution.py:286
  19.7 5.7 %collective-permute-start.7 = (bf16[16,3072]{1,0:T(8,128)(2,1)}, bf16[16,3072]{1,0:T(8,128)(2,1)S(1)}, u32[]{:S(2)}, u32[]{:S(2)}) collective-permute-start(bf16[16,3072]{1,0:T(8,128)(2,1)} %bitcast.39), channel_id=1, source_target_pairs={{1,2},{2,1},{3,4},{4,3},{5,6},{6,5},{7,8},{8,7},{9,10},{10,9},{11,... | collective-permute-start | bytes 294920 | tf_op jit(solution)/shard_map/ppermute | solution.py:286
  25.5 0.0 collective-permute-done.6.av1
  25.5 1.9 %collective-permute-start.3 = (bf16[128,3072]{1,0:T(8,128)(2,1)}, bf16[128,3072]{1,0:T(8,128)(2,1)}, u32[]{:S(2)}, u32[]{:S(2)}) collective-permute-start(bf16[128,3072]{1,0:T(8,128)(2,1)} %bitcast.20), channel_id=1, source_target_pairs={{1,2},{2,1},{3,4},{4,3},{5,6},{6,5},{7,8},{8,7},{9,10},{10,9},{11,... | collective-permute-start | bytes 2359304 | tf_op jit(solution)/shard_map/ppermute | solution.py:286
  27.4 1.4 %copy.17.audio_list = s32[128,2]{1,0:T(8,128)} copy(s32[128,2]{0,1:T(2,128)} %param.19) | data formatting | bytes 2048 | tf_op args[9]
  28.8 0.0 collective-permute-done.7.av2
  28.9 0.6 copy-done.7
  29.5 8.3 %gate_terms.1 = f32[1,3072]{1,0:T(1,128)} custom-call(s32[1]{0:T(128)} %bitcast.position_ref, s32[128,2]{1,0:T(8,128)} %copy.17.audio_list, bf16[128,3072]{1,0:T(8,128)(2,1)} %bitcast.24, bf16[128,3072]{1,0:T(8,128)(2,1)} %bitcast.28, bf16[16,3072]{1,0:T(8,128)(2,1)} %bitcast.34, bf16[16,3072]{1,0:T(8,128)(2,1)} %copy-done.4, bf16[16,3072]{1,0:T(8,128)(2,1)} %copy-done.5, ...), custom_call_target="tpu_custom_call" | custom-call | flops 75497472 | bytes 2162688 | tf_op jit(solution)/shard_map/gate_terms/pallas_call | solution.py:312
  37.8 1.4 %collective-permute-done.14 = f32[1,3072]{1,0:T(1,128)S(1)} collective-permute-done((f32[1,3072]{1,0:T(1,128)}, f32[1,3072]{1,0:T(1,128)S(1)}, u32[]{:S(2)}, u32[]{:S(2)}) %collective-permute-start.14) | collective-permute-done | bytes 12320 | tf_op jit(solution)/shard_map/ppermute | solution.py:369
  39.1 0.7 add.24
  39.9 0.1 collective-permute-start.15
  40.0 3.7 %collective-permute-done.15 = f32[1,3072]{1,0:T(1,128)S(1)} collective-permute-done((f32[1,3072]{1,0:T(1,128)S(1)}, f32[1,3072]{1,0:T(1,128)S(1)}, u32[]{:S(2)}, u32[]{:S(2)}) %collective-permute-start.15) | collective-permute-done | bytes 12320 | tf_op jit(solution)/shard_map/ppermute | solution.py:369
  43.7 0.1 collective-permute-start.16
  43.8 4.6 %collective-permute-done.16 = f32[1,3072]{1,0:T(1,128)S(1)} collective-permute-done((f32[1,3072]{1,0:T(1,128)S(1)}, f32[1,3072]{1,0:T(1,128)S(1)}, u32[]{:S(2)}, u32[]{:S(2)}) %collective-permute-start.16) | collective-permute-done | bytes 12320 | tf_op jit(solution)/shard_map/ppermute | solution.py:369
  48.4 3.3 %collective-permute-start.17 = (f32[1,3072]{1,0:T(1,128)S(1)}, f32[1,3072]{1,0:T(1,128)S(1)}, u32[]{:S(2)}, u32[]{:S(2)}) collective-permute-start(f32[1,3072]{1,0:T(1,128)S(1)} %add.26), channel_id=1, source_target_pairs={{0,8},{1,9},{2,10},{3,11},{4,12},{5,13},{6,14},{7,15},{8,0},{9,1},... | collective-permute-start | bytes 36872 | tf_op jit(solution)/shard_map/ppermute | solution.py:369
  51.7 4.4 %collective-permute-done.17 = f32[1,3072]{1,0:T(1,128)S(1)} collective-permute-done((f32[1,3072]{1,0:T(1,128)S(1)}, f32[1,3072]{1,0:T(1,128)S(1)}, u32[]{:S(2)}, u32[]{:S(2)}) %collective-permute-start.17) | collective-permute-done | bytes 12320 | tf_op jit(solution)/shard_map/ppermute | solution.py:369
  56.1 0.5 collective-permute-start.18
  56.6 3.2 %collective-permute-done.18 = f32[1,3072]{1,0:T(1,128)S(1)} collective-permute-done((f32[1,3072]{1,0:T(1,128)S(1)}, f32[1,3072]{1,0:T(1,128)S(1)}, u32[]{:S(2)}, u32[]{:S(2)}) %collective-permute-start.18) | collective-permute-done | bytes 12320 | tf_op jit(solution)/shard_map/ppermute | solution.py:369
  59.9 1.0 collective-permute-start.19
  60.9 4.3 %collective-permute-done.19 = f32[1,3072]{1,0:T(1,128)S(1)} collective-permute-done((f32[1,3072]{1,0:T(1,128)S(1)}, f32[1,3072]{1,0:T(1,128)S(1)}, u32[]{:S(2)}, u32[]{:S(2)}) %collective-permute-start.19) | collective-permute-done | bytes 12320 | tf_op jit(solution)/shard_map/ppermute | solution.py:369
  65.2 1.6 %collective-permute-start.20 = (f32[1,3072]{1,0:T(1,128)S(1)}, f32[1,3072]{1,0:T(1,128)S(1)}, u32[]{:S(2)}, u32[]{:S(2)}) collective-permute-start(f32[1,3072]{1,0:T(1,128)S(1)} %add.29), channel_id=1, source_target_pairs={{0,64},{64,0},{128,192},{192,128},{1,65},{65,1},{129,193},{193,129... | collective-permute-start | bytes 36872 | tf_op jit(solution)/shard_map/ppermute | solution.py:369
  66.8 2.2 %collective-permute-done.20 = f32[1,3072]{1,0:T(1,128)S(1)} collective-permute-done((f32[1,3072]{1,0:T(1,128)S(1)}, f32[1,3072]{1,0:T(1,128)S(1)}, u32[]{:S(2)}, u32[]{:S(2)}) %collective-permute-start.20) | collective-permute-done | bytes 12320 | tf_op jit(solution)/shard_map/ppermute | solution.py:369
  69.0 0.0 collective-permute-start.11
  69.0 0.0 collective-permute-done.k1
  69.0 0.0 copy-start.2
  69.0 0.6 collective-permute-start.12
  69.6 5.4 %collective-permute-start.8 = (bf16[128,3072]{1,0:T(8,128)(2,1)S(1)}, bf16[128,3072]{1,0:T(8,128)(2,1)}, u32[]{:S(2)}, u32[]{:S(2)}) collective-permute-start(bf16[128,3072]{1,0:T(8,128)(2,1)S(1)} %bitcast.27), channel_id=1, source_target_pairs={{1,2},{2,1},{3,4},{4,3},{5,6},{6,5},{7,8},{8,7},{9,10},{10,9},{11,... | collective-permute-start | bytes 2359304 | tf_op jit(solution)/shard_map/ppermute | solution.py:286
  75.0 2.2 %collective-permute-start.9 = (bf16[128,3072]{1,0:T(8,128)(2,1)S(1)}, bf16[128,3072]{1,0:T(8,128)(2,1)}, u32[]{:S(2)}, u32[]{:S(2)}) collective-permute-start(bf16[128,3072]{1,0:T(8,128)(2,1)S(1)} %bitcast.31), channel_id=1, source_target_pairs={{1,2},{2,1},{3,4},{4,3},{5,6},{6,5},{7,8},{8,7},{9,10},{10,9},{11,... | collective-permute-start | bytes 2359304 | tf_op jit(solution)/shard_map/ppermute | solution.py:286
  77.3 0.7 copy.16.tile_list
  78.0 3.1 %collective-permute-start.21 = (f32[1,3072]{1,0:T(1,128)S(1)}, f32[1,3072]{1,0:T(1,128)S(1)}, u32[]{:S(2)}, u32[]{:S(2)}) collective-permute-start(f32[1,3072]{1,0:T(1,128)S(1)} %add.30), channel_id=1, source_target_pairs={{0,128},{64,192},{128,0},{192,64},{1,129},{65,193},{129,1},{193,65... | collective-permute-start | bytes 36872 | tf_op jit(solution)/shard_map/ppermute | solution.py:369
  81.1 17.7 %own_queries.1 = (bf16[128,3072]{1,0:T(8,128)(2,1)}, f32[128,3072]{1,0:T(8,128)}, f32[128,3072]{1,0:T(8,128)}, f32[16,3072]{1,0:T(8,128)}, f32[16,3072]{1,0:T(8,128)}, /*index=5*/f32[96,128]{1,0:T(8,128)}) custom-call(s32[1]{0:T(128)} %bitcast.position_ref, s32[128,4]{1,0:T(8,128)} %copy.16.tile_list, s32[128]{0:T(128)} %tile_count.5, ...), custom_call_target="tpu_custom_call" | custom-call | flops 1107296256 | bytes 6881280 | tf_op jit(solution)/shard_map/own_queries/pallas_call | solution.py:323
  98.8 0.1 collective-permute-start.13
  98.9 5.2 %collective-permute-start.10 = (f32[96,128]{1,0:T(8,128)}, f32[96,128]{1,0:T(8,128)S(1)}, u32[]{:S(2)}, u32[]{:S(2)}) collective-permute-start(f32[96,128]{1,0:T(8,128)} %get-tuple-element.21), channel_id=1, source_target_pairs={{1,2},{2,1},{3,4},{4,3},{5,6},{6,5},{7,8},{8,7},{9,10},{10,9},{11,... | collective-permute-start | bytes 147464 | tf_op jit(solution)/shard_map/ppermute | solution.py:286
  104.1 0.6 add.31
  104.7 0.6 copy-done.9
  105.4 10.6 %mate_queries.1 = (f32[128,3072]{1,0:T(8,128)}, f32[128,3072]{1,0:T(8,128)}, f32[16,3072]{1,0:T(8,128)}, f32[16,3072]{1,0:T(8,128)}) custom-call(s32[1]{0:T(128)} %bitcast.position_ref, s32[128,4]{1,0:T(8,128)} %copy.16.tile_list, s32[128]{0:T(128)} %tile_count.5, s32[128,2]{1,0:T(8,128)} %copy.17.audio_list, ...), custom_call_target="tpu_custom_call" | custom-call | flops 402653184 | bytes 6684672 | tf_op jit(solution)/shard_map/mate_queries/pallas_call | solution.py:344
  116.0 0.6 copy-done.8
  116.6 10.2 %far_queries.1 = (bf16[128,3072]{1,0:T(8,128)(2,1)}, bf16[128,3072]{1,0:T(8,128)(2,1)}, bf16[16,3072]{1,0:T(8,128)(2,1)}, bf16[16,3072]{1,0:T(8,128)(2,1)}) custom-call(s32[1]{0:T(128)} %bitcast.position_ref, s32[128,4]{1,0:T(8,128)} %copy.16.tile_list, s32[128]{0:T(128)} %tile_count.5, s32[128,2]{1,0:T(8,128)} %copy.17.audio_list, ...), custom_call_target="tpu_custom_call" | custom-call | flops 402653184 | bytes 6684672 | tf_op jit(solution)/shard_map/far_queries/pallas_call | solution.py:344
  (32 shorter events, 0.1 us)
Async XLA Ops:
  0.6 68.3 %copy-start = (bf16[1,128,3072]{2,1,0:T(8,128)(2,1)S(1)}, bf16[1,128,3072]{2,1,0:T(8,128)(2,1)}, u32[]{:S(2)}) copy-start(bf16[1,128,3072]{2,1,0:T(8,128)(2,1)} %param.10) | copy-start | bytes 2359300
  0.6 68.3 %copy-start.1 = (bf16[1,128,3072]{2,1,0:T(8,128)(2,1)S(1)}, bf16[1,128,3072]{2,1,0:T(8,128)(2,1)}, u32[]{:S(2)}) copy-start(bf16[1,128,3072]{2,1,0:T(8,128)(2,1)} %param.16) | copy-start | bytes 2359300
  0.7 76.6 %copy-start.10 = (s32[128,4]{0,1:T(4,128)S(1)}, s32[128,4]{0,1:T(4,128)}, u32[]{:S(2)}) copy-start(s32[128,4]{0,1:T(4,128)} %param.17) | copy-start | bytes 6148
  0.7 68.3 %collective-permute-start = (bf16[128,3072]{1,0:T(8,128)(2,1)}, bf16[128,3072]{1,0:T(8,128)(2,1)S(1)}, u32[]{:S(2)}, u32[]{:S(2)}) collective-permute-start(bf16[128,3072]{1,0:T(8,128)(2,1)} %bitcast.14), channel_id=1, source_target_pairs={{0,1},{1,0},{2,3},{3,2},{4,5},{5,4},{6,7},{7,6},{8,9},{9,8},{10,11... | collective-permute-start | bytes 2359304 | tf_op jit(solution)/shard_map/ppermute | solution.py:283
  0.8 68.8 %collective-permute-start.1 = (bf16[128,3072]{1,0:T(8,128)(2,1)}, bf16[128,3072]{1,0:T(8,128)(2,1)S(1)}, u32[]{:S(2)}, u32[]{:S(2)}) collective-permute-start(bf16[128,3072]{1,0:T(8,128)(2,1)} %bitcast.15), channel_id=1, source_target_pairs={{1,2},{2,1},{3,4},{4,3},{5,6},{6,5},{7,8},{8,7},{9,10},{10,9},{11,... | collective-permute-start | bytes 2359304 | tf_op jit(solution)/shard_map/ppermute | solution.py:286
  8.8 66.2 %collective-permute-start.2 = (bf16[128,3072]{1,0:T(8,128)(2,1)}, bf16[128,3072]{1,0:T(8,128)(2,1)}, u32[]{:S(2)}, u32[]{:S(2)}) collective-permute-start(bf16[128,3072]{1,0:T(8,128)(2,1)} %bitcast.19), channel_id=1, source_target_pairs={{0,1},{1,0},{2,3},{3,2},{4,5},{5,4},{6,7},{7,6},{8,9},{9,8},{10,11... | collective-permute-start | bytes 2359304 | tf_op jit(solution)/shard_map/ppermute | solution.py:283
  8.9 3.1 %collective-permute-start.4 = (bf16[16,3072]{1,0:T(8,128)(2,1)}, bf16[16,3072]{1,0:T(8,128)(2,1)S(1)}, u32[]{:S(2)}, u32[]{:S(2)}) collective-permute-start(bf16[16,3072]{1,0:T(8,128)(2,1)} %bitcast.32), channel_id=1, source_target_pairs={{0,1},{1,0},{2,3},{3,2},{4,5},{5,4},{6,7},{7,6},{8,9},{9,8},{10,11... | collective-permute-start | bytes 294920 | tf_op jit(solution)/shard_map/ppermute | solution.py:283
  9.4 10.3 %collective-permute-start.5 = (bf16[16,3072]{1,0:T(8,128)(2,1)}, bf16[16,3072]{1,0:T(8,128)(2,1)S(1)}, u32[]{:S(2)}, u32[]{:S(2)}) collective-permute-start(bf16[16,3072]{1,0:T(8,128)(2,1)} %bitcast.33), channel_id=1, source_target_pairs={{1,2},{2,1},{3,4},{4,3},{5,6},{6,5},{7,8},{8,7},{9,10},{10,9},{11,... | collective-permute-start | bytes 294920 | tf_op jit(solution)/shard_map/ppermute | solution.py:286
  12.0 16.8 %copy-start.4 = (bf16[16,3072]{1,0:T(8,128)(2,1)}, bf16[16,3072]{1,0:T(8,128)(2,1)S(1)}, u32[]{:S(2)}) copy-start(bf16[16,3072]{1,0:T(8,128)(2,1)S(1)} %collective-permute-done.4.ak1) | copy-start | bytes 294916
  12.1 13.4 %collective-permute-start.6 = (bf16[16,3072]{1,0:T(8,128)(2,1)}, bf16[16,3072]{1,0:T(8,128)(2,1)S(1)}, u32[]{:S(2)}, u32[]{:S(2)}) collective-permute-start(bf16[16,3072]{1,0:T(8,128)(2,1)} %bitcast.38), channel_id=1, source_target_pairs={{0,1},{1,0},{2,3},{3,2},{4,5},{5,4},{6,7},{7,6},{8,9},{9,8},{10,11... | collective-permute-start | bytes 294920 | tf_op jit(solution)/shard_map/ppermute | solution.py:283
  19.7 9.1 %copy-start.5 = (bf16[16,3072]{1,0:T(8,128)(2,1)}, bf16[16,3072]{1,0:T(8,128)(2,1)S(1)}, u32[]{:S(2)}) copy-start(bf16[16,3072]{1,0:T(8,128)(2,1)S(1)} %collective-permute-done.5.ak2) | copy-start | bytes 294916
  19.7 9.1 %collective-permute-start.7 = (bf16[16,3072]{1,0:T(8,128)(2,1)}, bf16[16,3072]{1,0:T(8,128)(2,1)S(1)}, u32[]{:S(2)}, u32[]{:S(2)}) collective-permute-start(bf16[16,3072]{1,0:T(8,128)(2,1)} %bitcast.39), channel_id=1, source_target_pairs={{1,2},{2,1},{3,4},{4,3},{5,6},{6,5},{7,8},{8,7},{9,10},{10,9},{11,... | collective-permute-start | bytes 294920 | tf_op jit(solution)/shard_map/ppermute | solution.py:286
  25.5 3.4 %copy-start.6 = (bf16[16,3072]{1,0:T(8,128)(2,1)}, bf16[16,3072]{1,0:T(8,128)(2,1)S(1)}, u32[]{:S(2)}) copy-start(bf16[16,3072]{1,0:T(8,128)(2,1)S(1)} %collective-permute-done.6.av1) | copy-start | bytes 294916
  25.5 52.5 %collective-permute-start.3 = (bf16[128,3072]{1,0:T(8,128)(2,1)}, bf16[128,3072]{1,0:T(8,128)(2,1)}, u32[]{:S(2)}, u32[]{:S(2)}) collective-permute-start(bf16[128,3072]{1,0:T(8,128)(2,1)} %bitcast.20), channel_id=1, source_target_pairs={{1,2},{2,1},{3,4},{4,3},{5,6},{6,5},{7,8},{8,7},{9,10},{10,9},{11,... | collective-permute-start | bytes 2359304 | tf_op jit(solution)/shard_map/ppermute | solution.py:286
  28.8 0.6 copy-start.7
  37.8 1.4 %collective-permute-start.14 = (f32[1,3072]{1,0:T(1,128)}, f32[1,3072]{1,0:T(1,128)S(1)}, u32[]{:S(2)}, u32[]{:S(2)}) collective-permute-start(f32[1,3072]{1,0:T(1,128)} %gate_terms.1), channel_id=1, source_target_pairs={{0,1},{1,0},{2,3},{3,2},{4,5},{5,4},{6,7},{7,6},{8,9},{9,8},{10,11... | collective-permute-start | bytes 36872 | tf_op jit(solution)/shard_map/ppermute | solution.py:369
  39.9 3.8 %collective-permute-start.15 = (f32[1,3072]{1,0:T(1,128)S(1)}, f32[1,3072]{1,0:T(1,128)S(1)}, u32[]{:S(2)}, u32[]{:S(2)}) collective-permute-start(f32[1,3072]{1,0:T(1,128)S(1)} %add.24), channel_id=1, source_target_pairs={{0,2},{1,3},{2,0},{3,1},{4,6},{5,7},{6,4},{7,5},{8,10},{9,11},{10,... | collective-permute-start | bytes 36872 | tf_op jit(solution)/shard_map/ppermute | solution.py:369
  43.7 4.7 %collective-permute-start.16 = (f32[1,3072]{1,0:T(1,128)S(1)}, f32[1,3072]{1,0:T(1,128)S(1)}, u32[]{:S(2)}, u32[]{:S(2)}) collective-permute-start(f32[1,3072]{1,0:T(1,128)S(1)} %add.25), channel_id=1, source_target_pairs={{0,4},{1,5},{2,6},{3,7},{4,0},{5,1},{6,2},{7,3},{8,12},{9,13},{10,... | collective-permute-start | bytes 36872 | tf_op jit(solution)/shard_map/ppermute | solution.py:369
  48.4 7.7 %collective-permute-start.17 = (f32[1,3072]{1,0:T(1,128)S(1)}, f32[1,3072]{1,0:T(1,128)S(1)}, u32[]{:S(2)}, u32[]{:S(2)}) collective-permute-start(f32[1,3072]{1,0:T(1,128)S(1)} %add.26), channel_id=1, source_target_pairs={{0,8},{1,9},{2,10},{3,11},{4,12},{5,13},{6,14},{7,15},{8,0},{9,1},... | collective-permute-start | bytes 36872 | tf_op jit(solution)/shard_map/ppermute | solution.py:369
  56.1 3.8 %collective-permute-start.18 = (f32[1,3072]{1,0:T(1,128)S(1)}, f32[1,3072]{1,0:T(1,128)S(1)}, u32[]{:S(2)}, u32[]{:S(2)}) collective-permute-start(f32[1,3072]{1,0:T(1,128)S(1)} %add.27), channel_id=1, source_target_pairs={{0,16},{1,17},{2,18},{3,19},{4,20},{5,21},{6,22},{7,23},{8,24},{9,... | collective-permute-start | bytes 36872 | tf_op jit(solution)/shard_map/ppermute | solution.py:369
  59.9 5.3 %collective-permute-start.19 = (f32[1,3072]{1,0:T(1,128)S(1)}, f32[1,3072]{1,0:T(1,128)S(1)}, u32[]{:S(2)}, u32[]{:S(2)}) collective-permute-start(f32[1,3072]{1,0:T(1,128)S(1)} %add.28), channel_id=1, source_target_pairs={{0,32},{1,33},{2,34},{3,35},{4,36},{5,37},{6,38},{7,39},{8,40},{9,... | collective-permute-start | bytes 36872 | tf_op jit(solution)/shard_map/ppermute | solution.py:369
  65.2 3.8 %collective-permute-start.20 = (f32[1,3072]{1,0:T(1,128)S(1)}, f32[1,3072]{1,0:T(1,128)S(1)}, u32[]{:S(2)}, u32[]{:S(2)}) collective-permute-start(f32[1,3072]{1,0:T(1,128)S(1)} %add.29), channel_id=1, source_target_pairs={{0,64},{64,0},{128,192},{192,128},{1,65},{65,1},{129,193},{193,129... | collective-permute-start | bytes 36872 | tf_op jit(solution)/shard_map/ppermute | solution.py:369
  69.0 30.0 %collective-permute-start.11 = (bf16[128,3072]{1,0:T(8,128)(2,1)S(1)}, bf16[128,3072]{1,0:T(8,128)(2,1)}, u32[]{:S(2)}, u32[]{:S(2)}) collective-permute-start(bf16[128,3072]{1,0:T(8,128)(2,1)S(1)} %bitcast.26), channel_id=1, source_target_pairs={{0,1},{1,0},{2,3},{3,2},{4,5},{5,4},{6,7},{7,6},{8,9},{9,8},{10,11... | collective-permute-start | bytes 2359304 | tf_op jit(solution)/shard_map/ppermute | solution.py:283
  69.0 12.2 %copy-start.2 = (bf16[128,3072]{1,0:T(8,128)(2,1)}, bf16[128,3072]{1,0:T(8,128)(2,1)S(1)}, u32[]{:S(2)}) copy-start(bf16[128,3072]{1,0:T(8,128)(2,1)S(1)} %collective-permute-done.k1) | copy-start | bytes 2359300
  69.0 35.7 %collective-permute-start.12 = (bf16[128,3072]{1,0:T(8,128)(2,1)S(1)}, bf16[128,3072]{1,0:T(8,128)(2,1)}, u32[]{:S(2)}, u32[]{:S(2)}) collective-permute-start(bf16[128,3072]{1,0:T(8,128)(2,1)S(1)} %bitcast.30), channel_id=1, source_target_pairs={{0,1},{1,0},{2,3},{3,2},{4,5},{5,4},{6,7},{7,6},{8,9},{9,8},{10,11... | collective-permute-start | bytes 2359304 | tf_op jit(solution)/shard_map/ppermute | solution.py:283
  69.6 11.6 %copy-start.3 = (bf16[128,3072]{1,0:T(8,128)(2,1)}, bf16[128,3072]{1,0:T(8,128)(2,1)S(1)}, u32[]{:S(2)}) copy-start(bf16[128,3072]{1,0:T(8,128)(2,1)S(1)} %collective-permute-done.1.k2) | copy-start | bytes 2359300
  69.6 46.4 %collective-permute-start.8 = (bf16[128,3072]{1,0:T(8,128)(2,1)S(1)}, bf16[128,3072]{1,0:T(8,128)(2,1)}, u32[]{:S(2)}, u32[]{:S(2)}) collective-permute-start(bf16[128,3072]{1,0:T(8,128)(2,1)S(1)} %bitcast.27), channel_id=1, source_target_pairs={{1,2},{2,1},{3,4},{4,3},{5,6},{6,5},{7,8},{8,7},{9,10},{10,9},{11,... | collective-permute-start | bytes 2359304 | tf_op jit(solution)/shard_map/ppermute | solution.py:286
  75.0 40.9 %collective-permute-start.9 = (bf16[128,3072]{1,0:T(8,128)(2,1)S(1)}, bf16[128,3072]{1,0:T(8,128)(2,1)}, u32[]{:S(2)}, u32[]{:S(2)}) collective-permute-start(bf16[128,3072]{1,0:T(8,128)(2,1)S(1)} %bitcast.31), channel_id=1, source_target_pairs={{1,2},{2,1},{3,4},{4,3},{5,6},{6,5},{7,8},{8,7},{9,10},{10,9},{11,... | collective-permute-start | bytes 2359304 | tf_op jit(solution)/shard_map/ppermute | solution.py:286
  78.0 20.8 %collective-permute-start.21 = (f32[1,3072]{1,0:T(1,128)S(1)}, f32[1,3072]{1,0:T(1,128)S(1)}, u32[]{:S(2)}, u32[]{:S(2)}) collective-permute-start(f32[1,3072]{1,0:T(1,128)S(1)} %add.30), channel_id=1, source_target_pairs={{0,128},{64,192},{128,0},{192,64},{1,129},{65,193},{129,1},{193,65... | collective-permute-start | bytes 36872 | tf_op jit(solution)/shard_map/ppermute | solution.py:369
  98.8 5.9 %collective-permute-start.13 = (f32[96,128]{1,0:T(8,128)}, f32[96,128]{1,0:T(8,128)S(1)}, u32[]{:S(2)}, u32[]{:S(2)}) collective-permute-start(f32[96,128]{1,0:T(8,128)} %get-tuple-element.21), channel_id=1, source_target_pairs={{0,1},{1,0},{2,3},{3,2},{4,5},{5,4},{6,7},{7,6},{8,9},{9,8},{10,11... | collective-permute-start | bytes 147464 | tf_op jit(solution)/shard_map/ppermute | solution.py:283
  98.9 17.0 %collective-permute-start.10 = (f32[96,128]{1,0:T(8,128)}, f32[96,128]{1,0:T(8,128)S(1)}, u32[]{:S(2)}, u32[]{:S(2)}) collective-permute-start(f32[96,128]{1,0:T(8,128)} %get-tuple-element.21), channel_id=1, source_target_pairs={{1,2},{2,1},{3,4},{4,3},{5,6},{6,5},{7,8},{8,7},{9,10},{10,9},{11,... | collective-permute-start | bytes 147464 | tf_op jit(solution)/shard_map/ppermute | solution.py:286
  104.7 0.6 copy-start.9
  116.0 0.6 copy-start.8

commit v2 on v1

v2 whole, which is shorter than its diff:
```python
import math

import jax
import jax.numpy as jnp
from jax import lax
from jax.experimental import pallas as pl
from jax.experimental.pallas import tpu as pltpu
from jax.sharding import PartitionSpec as P

HEAD_DIM = 128
TILE = 64
SCALE = 1.0 / math.sqrt(HEAD_DIM)
SCORE_FACTOR = SCALE * math.log2(math.e)
NEG_INF = float("-inf")


def dot_t(a, b):
    return lax.dot_general(a, b, (((1,), (1,)), ((), ())), preferred_element_type=jnp.float32)


def dot(a, b):
    return lax.dot_general(a, b, (((1,), (0,)), ((), ())), preferred_element_type=jnp.float32)


def dot_lead(a, b):
    return lax.dot_general(a, b, (((0,), (0,)), ((), ())), preferred_element_type=jnp.float32)


def mate_of(position):
    return position + 1 - 2 * lax.rem(position, 2)


def far_of(position):
    return position - 1 + 2 * lax.rem(position, 2)


def tile_bias(list_ref, count_ref, row_tile, key_tile):
    slots, tiles = list_ref.shape
    row = jnp.clip(row_tile, 0, tiles - 1)
    inside = row == row_tile
    hit = jnp.bool_(False)
    for j in range(slots):
        hit = hit | ((list_ref[j, row] == key_tile) & (j < count_ref[row]))
    return jnp.where(hit & inside, 0.0, NEG_INF).astype(jnp.float32)


def block_bias(list_ref, row_tile, block):
    slots, tiles = list_ref.shape
    row = jnp.clip(row_tile, 0, tiles - 1)
    inside = row == row_tile
    hit = jnp.bool_(False)
    for j in range(slots):
        hit = hit | (list_ref[j, row] == block)
    return jnp.where(hit & inside, 0.0, NEG_INF).astype(jnp.float32)


def lanes_of(first, second):
    lane = lax.broadcasted_iota(jnp.int32, (1, 2 * TILE), 1)
    return jnp.where(lane < TILE, first, second)


def own_video_rows(list_ref, count_ref, position):
    rows = []
    for holder in (position, mate_of(position), far_of(position)):
        for w in range(2):
            key_tile = 2 * holder + w
            rows.append(
                lanes_of(
                    tile_bias(list_ref, count_ref, 2 * position, key_tile),
                    tile_bias(list_ref, count_ref, 2 * position + 1, key_tile),
                )
            )
    return rows


def own_audio_rows(list_ref, position):
    rows = []
    for block in (position, mate_of(position), far_of(position)):
        rows.append(
            lanes_of(
                block_bias(list_ref, 2 * position, block),
                block_bias(list_ref, 2 * position + 1, block),
            )
        )
    return rows


def masked(scores, rows, height):
    return jnp.concatenate(
        [scores[i * height : (i + 1) * height] * SCORE_FACTOR + row for i, row in enumerate(rows)],
        axis=0,
    )


def softmax_cols(scores):
    top = jnp.max(scores, axis=0, keepdims=True)
    grown = jnp.exp2(scores - top)
    total = jnp.sum(grown, axis=0, keepdims=True)
    return grown * (1.0 / total), top + jnp.log2(total)


def head_cols(ref):
    return [slice(i, i + HEAD_DIM) for i in range(0, ref.shape[1], HEAD_DIM)]


def rows_at(refs, first, count, cols):
    return jnp.concatenate([ref[first : first + count, cols] for ref in refs], axis=0)


def gated_by(gate, cotangent):
    return (gate * cotangent.astype(jnp.float32)).astype(jnp.bfloat16)


def gate_kernel(position_ref, audio_list, q_ref, do_ref, a0, a1, a2, gate_out):
    rows = own_audio_rows(audio_list, position_ref[0])
    block = a0.shape[0] // 2
    heads = head_cols(q_ref)
    raw = [dot_t(rows_at((a0, a1, a2), 0, block, c), q_ref[:, c]) for c in heads]
    weights = [softmax_cols(masked(r, rows, block))[0].astype(jnp.bfloat16) for r in raw]
    spread = [dot(w, do_ref[:, c]) for w, c in zip(weights, heads)]
    for t, c in zip(spread, heads):
        values = rows_at((a0, a1, a2), block, block, c).astype(jnp.float32)
        gate_out[:, c] = jnp.sum(t * values, axis=0, keepdims=True)


def own_kernel(
    position_ref,
    tile_list,
    tile_count,
    audio_list,
    q_ref,
    do_ref,
    kv0,
    kv1,
    kv2,
    a0,
    a1,
    a2,
    gate_ref,
    dq_out,
    own_out,
    mate_k_out,
    mate_v_out,
    stat_out,
):
    position = position_ref[0]
    video_rows = own_video_rows(tile_list, tile_count, position)
    audio_rows = own_audio_rows(audio_list, position)
    own = kv0.shape[0] // 2
    window = 3 * own
    block = a0.shape[0] // 2
    video, audio = (kv0, kv1, kv2), (a0, a1, a2)
    heads = head_cols(q_ref)
    products = []
    for c in heads:
        q = q_ref[:, c]
        do = do_ref[:, c]
        keys = jnp.concatenate([rows_at(video, 0, own, c), rows_at(audio, 0, block, c)], axis=0)
        raw = dot_t(keys, q)
        video_dp = dot_t(rows_at(video, own, own, c), do)
        cross_dp = dot_t(rows_at(audio, block, block, c), gated_by(gate_ref[:, c], do))
        products.append((raw, video_dp, cross_dp))
    grads = []
    for h, (raw, video_dp, cross_dp) in enumerate(products):
        video_prob, video_total = softmax_cols(masked(raw[:window], video_rows, TILE))
        cross_prob, cross_total = softmax_cols(masked(raw[window:], audio_rows, block))
        video_weights = video_prob.astype(jnp.bfloat16)
        cross_weights = cross_prob.astype(jnp.bfloat16)
        video_delta = jnp.sum(video_weights.astype(jnp.float32) * video_dp, axis=0, keepdims=True)
        cross_delta = jnp.sum(cross_weights.astype(jnp.float32) * cross_dp, axis=0, keepdims=True)
        video_ds = (video_prob * (video_dp - video_delta)).astype(jnp.bfloat16)
        cross_ds = (cross_prob * (cross_dp - cross_delta)).astype(jnp.bfloat16)
        stat_out[4 * h : 4 * h + 4, :] = jnp.concatenate(
            [video_total, video_delta, cross_total, cross_delta], axis=0
        )
        grads.append((video_ds, cross_ds, video_weights[: 2 * own], cross_weights[: 2 * block]))
    for c, (video_ds, cross_ds, video_weights, cross_weights) in zip(heads, grads):
        q = q_ref[:, c]
        do = do_ref[:, c]
        keys = jnp.concatenate([rows_at(video, 0, own, c), rows_at(audio, 0, block, c)], axis=0)
        both_ds = jnp.concatenate([video_ds, cross_ds], axis=0)
        dq_out[:, c] = (dot_lead(both_ds, keys) * SCALE).astype(jnp.bfloat16)
        dk = dot(video_ds[: 2 * own], q)
        dv = dot(video_weights, do)
        dak = dot(cross_ds[: 2 * block], q)
        dav = dot(cross_weights, gated_by(gate_ref[:, c], do))
        own_out[:own, c] = dk[:own]
        own_out[own : 2 * own, c] = dv[:own]
        own_out[2 * own : 2 * own + block, c] = dak[:block]
        own_out[2 * own + block :, c] = dav[:block]
        mate_k_out[:own, c] = dk[own:].astype(jnp.bfloat16)
        mate_k_out[own:, c] = dak[block:].astype(jnp.bfloat16)
        mate_v_out[:own, c] = dv[own:].astype(jnp.bfloat16)
        mate_v_out[own:, c] = dav[block:].astype(jnp.bfloat16)


def far_kernel(
    position_ref,
    tile_list,
    tile_count,
    audio_list,
    qo_ref,
    stat_ref,
    kv_ref,
    a_ref,
    gate_ref,
    own_in,
    mate_k_in,
    mate_v_in,
    dk_out,
    dv_out,
    dak_out,
    dav_out,
):
    position = position_ref[0]
    beside = far_of(position)
    video_rows = [
        lanes_of(
            tile_bias(tile_list, tile_count, 2 * beside, 2 * position + w),
            tile_bias(tile_list, tile_count, 2 * beside + 1, 2 * position + w),
        )
        for w in range(2)
    ]
    audio_row = lanes_of(
        block_bias(audio_list, 2 * beside, position),
        block_bias(audio_list, 2 * beside + 1, position),
    )
    own = kv_ref.shape[0] // 2
    block = a_ref.shape[0] // 2
    heads = head_cols(kv_ref)
    products = []
    for c in heads:
        q = qo_ref[:own, c]
        do = qo_ref[own:, c]
        keys = jnp.concatenate([kv_ref[:own, c], a_ref[:block, c]], axis=0)
        products.append(
            (
                dot_t(keys, q),
                dot_t(kv_ref[own:, c], do),
                dot_t(a_ref[block:, c], gated_by(gate_ref[:, c], do)),
            )
        )
    grads = []
    for h, (raw, video_dp, cross_dp) in enumerate(products):
        stats = stat_ref[4 * h : 4 * h + 4, :]
        video_prob = jnp.exp2(masked(raw[:own], video_rows, TILE) - stats[0:1])
        cross_prob = jnp.exp2(raw[own:] * SCORE_FACTOR + audio_row - stats[2:3])
        video_ds = (video_prob * (video_dp - stats[1:2])).astype(jnp.bfloat16)
        cross_ds = (cross_prob * (cross_dp - stats[3:4])).astype(jnp.bfloat16)
        grads.append(
            (
                jnp.concatenate([video_ds, cross_ds], axis=0),
                video_prob.astype(jnp.bfloat16),
                cross_prob.astype(jnp.bfloat16),
            )
        )
    for c, (both_ds, video_weights, cross_weights) in zip(heads, grads):
        q = qo_ref[:own, c]
        do = qo_ref[own:, c]
        from_q = dot(both_ds, q)
        from_do = dot(video_weights, do)
        from_gated = dot(cross_weights, gated_by(gate_ref[:, c], do))
        mate_k = mate_k_in[:, c].astype(jnp.float32)
        mate_v = mate_v_in[:, c].astype(jnp.float32)
        sums = own_in[:, c]
        audio = sums[2 * own :]
        dk_out[:, c] = ((sums[:own] + mate_k[:own] + from_q[:own]) * SCALE).astype(dk_out.dtype)
        dv_out[:, c] = (sums[own : 2 * own] + mate_v[:own] + from_do).astype(dv_out.dtype)
        dak_out[:, c] = ((audio[:block] + mate_k[own:] + from_q[own:]) * SCALE).astype(dak_out.dtype)
        dav_out[:, c] = (audio[block:] + mate_v[own:] + from_gated).astype(dav_out.dtype)


def heads_per_step(heads, most):
    return max(g for g in range(1, most + 1) if heads % g == 0)


def flipped(part, axis, bit):
    size = lax.axis_size(axis)
    flips = [f for f in (bit, 2 * bit, 3 * bit) if f < size]
    return [part] + [lax.ppermute(part, axis, [(i, i ^ f) for i in range(size)]) for f in flips]


def joined(parts):
    if len(parts) < 4:
        return sum(parts[1:], parts[0])
    return (parts[0] + parts[1]) + (parts[2] + parts[3])


def after(first, then):
    return lax.optimization_barrier((first, then))


SMEM = pl.BlockSpec(memory_space=pltpu.SMEM)


def cols_spec(rows, width):
    return pl.BlockSpec((rows, width), lambda i: (0, i))


def cost(flops, arrays):
    return pl.CostEstimate(
        flops=flops,
        bytes_accessed=0,
        transcendentals=0,
    )


def per_device(
    video_query,
    video_key,
    video_value,
    audio_key,
    audio_value,
    cross_gate,
    out_cotangent,
    tile_list,
    tile_count,
    audio_list,
):
    clips, rows, width = video_query.shape
    block = audio_key.shape[1]
    heads = width // HEAD_DIM
    count = lax.axis_size("ctx")
    position = lax.axis_index("ctx").astype(jnp.int32).reshape(1)
    mate_pairs = [(i, i ^ 1) for i in range(count)]
    far_pairs = [(i + s, i + 1 - s) for i in range(1, count - 1, 2) for s in range(2)]

    def to_mate(x):
        return lax.ppermute(x, "ctx", mate_pairs)

    def to_far(x):
        return lax.ppermute(x, "ctx", far_pairs)

    q, k, v, do = (x.reshape(rows, width) for x in (video_query, video_key, video_value, out_cotangent))
    ak, av = (x.reshape(block, width) for x in (audio_key, audio_value))
    gate = cross_gate.reshape(1, width)
    tile_list, audio_list = tile_list.T, audio_list.T

    a = jnp.concatenate([ak, av], axis=0)
    a_far, a_mate = to_far(a), to_mate(a)
    kv = jnp.concatenate([k, v], axis=0)
    kv_far, kv_mate = to_far(kv), to_mate(kv)

    f32, bf16 = jnp.float32, jnp.bfloat16

    def specs(group):
        step = group * HEAD_DIM
        return (
            (heads // group,),
            cols_spec(2 * rows, step),
            cols_spec(rows, step),
            cols_spec(2 * block, step),
            cols_spec(block, step),
            cols_spec(1, step),
            pl.BlockSpec((4 * group, rows), lambda i: (i, 0)),
        )

    def array(n, dtype):
        return jax.ShapeDtypeStruct((n, width), dtype)

    params = pltpu.CompilerParams(vmem_limit_bytes=24 * 2**20)

    grid, pair, vspec, apair, aspec, gspec, sspec = specs(heads_per_step(heads, 12))
    gate_args = (q, do, a, a_mate, a_far)
    gate_part = pl.pallas_call(
        gate_kernel,
        grid=grid,
        in_specs=[SMEM, SMEM] + [vspec] * 2 + [apair] * 3,
        out_specs=gspec,
        out_shape=array(1, f32),
        cost_estimate=cost(20_000_000_000, gate_args),
        compiler_params=params,
        name="gate_terms",
    )(position, audio_list, *gate_args)

    total = joined(flipped(gate_part, "dp", 1))
    parts = flipped(total, "ctx", 16)
    kv_far, parts = after(kv_far, parts)
    total, q_next = after(joined(parts), q)
    qo_far = to_far(jnp.concatenate([q_next, do], axis=0))

    grid, pair, vspec, apair, aspec, gspec, sspec = specs(heads_per_step(heads, 8))
    sums_spec = cols_spec(2 * (rows + block), vspec.block_shape[1])
    half_spec = cols_spec(rows + block, vspec.block_shape[1])
    own_args = (q, do, kv, kv_mate, kv_far, a, a_mate, a_far)
    dq, own_sums, mate_k, mate_v, stats = pl.pallas_call(
        own_kernel,
        grid=grid,
        in_specs=[SMEM] * 4 + [vspec] * 2 + [pair] * 3 + [apair] * 3 + [gspec],
        out_specs=[vspec, sums_spec, half_spec, half_spec, sspec],
        out_shape=[
            array(rows, bf16),
            array(2 * (rows + block), f32),
            array(rows + block, bf16),
            array(rows + block, bf16),
            jax.ShapeDtypeStruct((4 * heads, rows), f32),
        ],
        cost_estimate=cost(0, own_args),
        compiler_params=params,
        name="own_queries",
    )(position, tile_list, tile_count, audio_list, *own_args, gate)

    stats_far = to_far(stats)
    mate_k, mate_v = to_mate(mate_k), to_mate(mate_v)
    (mate_k, mate_v), total = after((mate_k, mate_v), total)
    parts = flipped(total, "ctx", 1)
    (qo_far, stats_far), parts = after((qo_far, stats_far), parts)
    total = joined(flipped(joined(parts), "ctx", 4))

    far_args = (qo_far, stats_far, kv, a, gate, own_sums, mate_k, mate_v)
    dk, dv, dak, dav = pl.pallas_call(
        far_kernel,
        grid=grid,
        in_specs=[SMEM] * 4 + [pair, sspec, pair, apair, gspec, sums_spec, half_spec, half_spec],
        out_specs=[vspec, vspec, aspec, aspec],
        out_shape=[array(rows, bf16), array(rows, bf16), array(block, bf16), array(block, bf16)],
        cost_estimate=cost(5_000_000_000, far_args),
        compiler_params=params,
        name="far_queries",
    )(position, tile_list, tile_count, audio_list, *far_args)

    return (
        dq.reshape(clips, rows, width),
        dk.reshape(clips, rows, width),
        dv.reshape(clips, rows, width),
        dak.reshape(clips, block, width),
        dav.reshape(clips, block, width),
        total.reshape(width),
    )


def solution(mesh):
    placed = P("dp", "ctx", None)
    return jax.shard_map(
        per_device,
        mesh=mesh,
        in_specs=(placed,) * 5 + (P(), placed, P(), P(), P()),
        out_specs=(placed,) * 5 + (P(),),
        check_vma=False,
    )
```

time: 128 us -> 73.8 us (0.58)
  the two profiles are of different devices: /device:TPU:24 before, /device:TPU:1 now
where the time goes in v2:
time: 73.8 us; the launch traced here: 73.5 us
  starting transfers between devices  37.6 us (51%)
  Pallas kernels  15.9 us (22%)
  waiting for transfers between devices  15.8 us (21%)
  other arithmetic  3.34 us (5%)
  between operations  0.9 us (1%)
    ppermute x12, starting transfers between devices, flipped(): lax.ppermute(part, axis, [(i, i ^ f) for i in range(size)])  16.3 us
    ppermute x4, starting transfers between devices, to_far(): return lax.ppermute(x, 'ctx', far_pairs)  11.1 us
    ppermute x12, waiting for transfers between devices, flipped(): lax.ppermute(part, axis, [(i, i ^ f) for i in range(size)])  10.5 us
    ppermute x4, starting transfers between devices, to_mate(): return lax.ppermute(x, 'ctx', mate_pairs)  10.1 us
    pallas_call x1, Pallas kernels, per_device(): pl.pallas_call(own_kernel, grid=grid, in_specs=[SMEM] * 4 + [vspec] * 2 +...  8.93 us
    ppermute x4, waiting for transfers between devices, to_far(): return lax.ppermute(x, 'ctx', far_pairs)  5.22 us
    pallas_call x1, Pallas kernels, per_device(): pl.pallas_call(far_kernel, grid=grid, in_specs=[SMEM] * 4 + [pair, sspec,...  4.71 us
    pallas_call x1, Pallas kernels, per_device(): pl.pallas_call(gate_kernel, grid=grid, in_specs=[SMEM, SMEM] + [vspec] *...  2.23 us
  transfers between devices with their start and end apart: 20, of which 5 were waited for; matrix products, arithmetic and copies ran while one was open for 2% of the time, Pallas kernels for 22%

profile of v2, /device:TPU:1, one launch (start us, length us, event | category | flops | bytes accessed | tf_op | source)
XLA Modules:
  0.0 73.5 jit_solution(8903963680516533834)
XLA Ops:
  0.6 1.0 %pad_maximum_fusion.2.a0.a_ref = bf16[32,3072]{1,0:T(8,128)(2,1)S(1)} fusion(bf16[16,3072]{1,0:T(8,128)(2,1)} %bitcast.31, bf16[16,3072]{1,0:T(8,128)(2,1)} %bitcast.32), kind=kLoop, calls=%fused_computation.2 | loop fusion | flops 393216 | bytes 393216 | tf_op jit(solution)/shard_map/concatenate | solution.py:339
  1.6 3.3 %collective-permute-start.2 = (bf16[32,3072]{1,0:T(8,128)(2,1)S(1)}, bf16[32,3072]{1,0:T(8,128)(2,1)S(1)}, u32[]{:S(2)}, u32[]{:S(2)}) collective-permute-start(bf16[32,3072]{1,0:T(8,128)(2,1)S(1)} %pad_maximum_fusion.2.a0.a_ref), channel_id=1, source_target_pairs={{0,1},{1,0},{2,3},{3,2},{4,5},{5,4},{6,7},{7,6},{8,9},{9,8},{10,11... | collective-permute-start | bytes 589832 | tf_op jit(solution)/shard_map/ppermute | solution.py:329
  4.9 1.9 %collective-permute-start.3 = (bf16[32,3072]{1,0:T(8,128)(2,1)S(1)}, bf16[32,3072]{1,0:T(8,128)(2,1)}, u32[]{:S(2)}, u32[]{:S(2)}) collective-permute-start(bf16[32,3072]{1,0:T(8,128)(2,1)S(1)} %pad_maximum_fusion.2.a0.a_ref), channel_id=1, source_target_pairs={{1,2},{2,1},{3,4},{4,3},{5,6},{6,5},{7,8},{8,7},{9,10},{10,9},{11,... | collective-permute-start | bytes 589832 | tf_op jit(solution)/shard_map/ppermute | solution.py:332
  6.8 0.0 copy-start
  6.8 0.0 copy-start.1
  6.9 0.0 copy-start.4
  6.9 1.6 %pad_maximum_fusion.kv0.kv_ref = bf16[256,3072]{1,0:T(8,128)(2,1)S(1)} fusion(bf16[128,3072]{1,0:T(8,128)(2,1)} %bitcast.29, bf16[128,3072]{1,0:T(8,128)(2,1)} %bitcast.30), kind=kLoop, calls=%fused_computation | loop fusion | flops 3145728 | bytes 3145728 | tf_op jit(solution)/shard_map/concatenate | solution.py:341
  8.5 3.6 %collective-permute-start.1 = (bf16[256,3072]{1,0:T(8,128)(2,1)S(1)}, bf16[256,3072]{1,0:T(8,128)(2,1)}, u32[]{:S(2)}, u32[]{:S(2)}) collective-permute-start(bf16[256,3072]{1,0:T(8,128)(2,1)S(1)} %pad_maximum_fusion.kv0.kv_ref), channel_id=1, source_target_pairs={{1,2},{2,1},{3,4},{4,3},{5,6},{6,5},{7,8},{8,7},{9,10},{10,9},{11,... | collective-permute-start | bytes 4718600 | tf_op jit(solution)/shard_map/ppermute | solution.py:332
  12.1 0.0 collective-permute-done.2.a1
  12.1 0.0 collective-permute-done.3.a2
  12.2 2.2 %gate_terms.1 = f32[1,3072]{1,0:T(1,128)S(1)} custom-call(s32[1]{0:T(128)} %bitcast.position_ref, s32[2,128]{1,0:T(2,128)S(1)} %bitcast.26, bf16[128,3072]{1,0:T(8,128)(2,1)S(1)} %bitcast.16, bf16[128,3072]{1,0:T(8,128)(2,1)S(1)} %bitcast.19, bf16[32,3072]{1,0:T(8,128)(2,1)S(1)} %pad_maximum_fusion.2.a0.a_ref, ...), custom_call_target="tpu_custom_call" | custom-call | flops 20000000000 | tf_op jit(solution)/shard_map/gate_terms/pallas_call | solution.py:365
  14.4 0.1 collective-permute-start.4
  14.5 1.9 %collective-permute-start.5 = (f32[1,3072]{1,0:T(1,128)S(1)}, f32[1,3072]{1,0:T(1,128)S(1)}, u32[]{:S(2)}, u32[]{:S(2)}) collective-permute-start(f32[1,3072]{1,0:T(1,128)S(1)} %gate_terms.1), channel_id=1, source_target_pairs={{0,128},{64,192},{128,0},{192,64},{1,129},{65,193},{129,1},{193,65... | collective-permute-start | bytes 36872 | tf_op jit(solution)/shard_map/ppermute | solution.py:280
  16.4 1.9 %collective-permute-start.6 = (f32[1,3072]{1,0:T(1,128)S(1)}, f32[1,3072]{1,0:T(1,128)S(1)}, u32[]{:S(2)}, u32[]{:S(2)}) collective-permute-start(f32[1,3072]{1,0:T(1,128)S(1)} %gate_terms.1), channel_id=1, source_target_pairs={{0,192},{64,128},{128,64},{192,0},{1,193},{65,129},{129,65},{193,1... | collective-permute-start | bytes 36872 | tf_op jit(solution)/shard_map/ppermute | solution.py:280
  18.4 0.0 collective-permute-done.4
  18.4 0.3 collective-permute-done.5
  18.7 1.5 %collective-permute-done.6 = f32[1,3072]{1,0:T(1,128)S(1)} collective-permute-done((f32[1,3072]{1,0:T(1,128)S(1)}, f32[1,3072]{1,0:T(1,128)S(1)}, u32[]{:S(2)}, u32[]{:S(2)}) %collective-permute-start.6) | collective-permute-done | bytes 12320 | tf_op jit(solution)/shard_map/ppermute | solution.py:280
  20.2 1.8 %collective-permute-start.7 = (f32[1,3072]{1,0:T(1,128)S(1)}, f32[1,3072]{1,0:T(1,128)S(1)}, u32[]{:S(2)}, u32[]{:S(2)}) collective-permute-start(f32[1,3072]{1,0:T(1,128)S(1)} %add_add_fusion.3), channel_id=1, source_target_pairs={{0,16},{1,17},{2,18},{3,19},{4,20},{5,21},{6,22},{7,23},{8,24},{9,... | collective-permute-start | bytes 36872 | tf_op jit(solution)/shard_map/ppermute | solution.py:280
  22.0 2.6 %collective-permute-start.8 = (f32[1,3072]{1,0:T(1,128)S(1)}, f32[1,3072]{1,0:T(1,128)S(1)}, u32[]{:S(2)}, u32[]{:S(2)}) collective-permute-start(f32[1,3072]{1,0:T(1,128)S(1)} %add_add_fusion.3), channel_id=1, source_target_pairs={{0,32},{1,33},{2,34},{3,35},{4,36},{5,37},{6,38},{7,39},{8,40},{9,... | collective-permute-start | bytes 36872 | tf_op jit(solution)/shard_map/ppermute | solution.py:280
  24.6 6.3 %collective-permute-start = (bf16[256,3072]{1,0:T(8,128)(2,1)S(1)}, bf16[256,3072]{1,0:T(8,128)(2,1)S(1)}, u32[]{:S(2)}, u32[]{:S(2)}) collective-permute-start(bf16[256,3072]{1,0:T(8,128)(2,1)S(1)} %pad_maximum_fusion.kv0.kv_ref), channel_id=1, source_target_pairs={{0,1},{1,0},{2,3},{3,2},{4,5},{5,4},{6,7},{7,6},{8,9},{9,8},{10,11... | collective-permute-start | bytes 4718600 | tf_op jit(solution)/shard_map/ppermute | solution.py:329
  30.9 0.0 collective-permute-done.7
  30.9 8.3 %collective-permute-done.8 = f32[1,3072]{1,0:T(1,128)S(1)} collective-permute-done((f32[1,3072]{1,0:T(1,128)S(1)}, f32[1,3072]{1,0:T(1,128)S(1)}, u32[]{:S(2)}, u32[]{:S(2)}) %collective-permute-start.8) | collective-permute-done | bytes 12320 | tf_op jit(solution)/shard_map/ppermute | solution.py:280
  39.2 0.0 copy-start.2
  39.2 0.0 copy-start.3
  39.3 0.0 copy-start.5
  39.3 0.1 pad_maximum_fusion.1
  39.4 1.9 %collective-permute-start.10 = (bf16[256,3072]{1,0:T(8,128)(2,1)S(1)}, bf16[256,3072]{1,0:T(8,128)(2,1)S(1)}, u32[]{:S(2)}, u32[]{:S(2)}) collective-permute-start(bf16[256,3072]{1,0:T(8,128)(2,1)S(1)} %pad_maximum_fusion.1), channel_id=1, source_target_pairs={{1,2},{2,1},{3,4},{4,3},{5,6},{6,5},{7,8},{8,7},{9,10},{10,9},{11,... | collective-permute-start | bytes 4718600 | tf_op jit(solution)/shard_map/ppermute | solution.py:332
  41.3 0.0 collective-permute-done.kv1
  41.3 8.9 %own_queries.1 = (bf16[128,3072]{1,0:T(8,128)(2,1)}, f32[288,3072]{1,0:T(8,128)S(1)}, bf16[144,3072]{1,0:T(8,128)(2,1)S(1)}, bf16[144,3072]{1,0:T(8,128)(2,1)S(1)}, f32[96,128]{1,0:T(8,128)S(1)}) custom-call(s32[1]{0:T(128)} %bitcast.position_ref, s32[4,128]{1,0:T(4,128)S(1)} %bitcast.24, s32[128]{0:T(128)S(1)} %copy-done.5, s32[2,128]{1,0:T(2,128)S(1)} %bitcast.27, ...), custom_call_target="tpu_custom_call" | custom-call | tf_op jit(solution)/shard_map/own_queries/pallas_call | solution.py:386
  50.3 0.0 collective-permute-start.12
  50.3 0.5 collective-permute-start.13
  50.8 3.6 %collective-permute-start.11 = (f32[96,128]{1,0:T(8,128)S(1)}, f32[96,128]{1,0:T(8,128)S(1)}, u32[]{:S(2)}, u32[]{:S(2)}) collective-permute-start(f32[96,128]{1,0:T(8,128)S(1)} %get-tuple-element.38), channel_id=1, source_target_pairs={{1,2},{2,1},{3,4},{4,3},{5,6},{6,5},{7,8},{8,7},{9,10},{10,9},{11,... | collective-permute-start | bytes 147464 | tf_op jit(solution)/shard_map/ppermute | solution.py:332
  54.4 0.0 collective-permute-done.12.mate_k_in
  54.4 0.0 collective-permute-done.13.mate_v_in
  54.5 0.1 collective-permute-start.14
  54.6 1.3 %collective-permute-start.15 = (f32[1,3072]{1,0:T(1,128)S(1)}, f32[1,3072]{1,0:T(1,128)S(1)}, u32[]{:S(2)}, u32[]{:S(2)}) collective-permute-start(f32[1,3072]{1,0:T(1,128)S(1)} %add_add_fusion.2), channel_id=1, source_target_pairs={{0,2},{1,3},{2,0},{3,1},{4,6},{5,7},{6,4},{7,5},{8,10},{9,11},{10,... | collective-permute-start | bytes 36872 | tf_op jit(solution)/shard_map/ppermute | solution.py:280
  55.8 0.9 %collective-permute-start.16 = (f32[1,3072]{1,0:T(1,128)S(1)}, f32[1,3072]{1,0:T(1,128)S(1)}, u32[]{:S(2)}, u32[]{:S(2)}) collective-permute-start(f32[1,3072]{1,0:T(1,128)S(1)} %add_add_fusion.2), channel_id=1, source_target_pairs={{0,3},{1,2},{2,1},{3,0},{4,7},{5,6},{6,5},{7,4},{8,11},{9,10},{10,... | collective-permute-start | bytes 36872 | tf_op jit(solution)/shard_map/ppermute | solution.py:280
  56.7 5.2 %collective-permute-done.11.stat_ref = f32[96,128]{1,0:T(8,128)S(1)} collective-permute-done((f32[96,128]{1,0:T(8,128)S(1)}, f32[96,128]{1,0:T(8,128)S(1)}, u32[]{:S(2)}, u32[]{:S(2)}) %collective-permute-start.11) | collective-permute-done | bytes 49184 | tf_op jit(solution)/shard_map/ppermute | solution.py:332
  61.9 0.0 collective-permute-done.14
  61.9 0.0 collective-permute-done.15
  61.9 0.4 collective-permute-done.16
  62.3 0.0 collective-permute-done.10.qo_ref
  62.4 0.1 collective-permute-start.17
  62.5 0.1 collective-permute-start.18
  62.6 5.5 %collective-permute-start.19 = (f32[1,3072]{1,0:T(1,128)S(1)}, f32[1,3072]{1,0:T(1,128)S(1)}, u32[]{:S(2)}, u32[]{:S(2)}) collective-permute-start(f32[1,3072]{1,0:T(1,128)S(1)} %add_add_fusion.1), channel_id=1, source_target_pairs={{0,12},{1,13},{2,14},{3,15},{4,8},{5,9},{6,10},{7,11},{8,4},{9,5},... | collective-permute-start | bytes 36872 | tf_op jit(solution)/shard_map/ppermute | solution.py:280
  68.1 4.7 %far_queries.1 = (bf16[128,3072]{1,0:T(8,128)(2,1)}, bf16[128,3072]{1,0:T(8,128)(2,1)}, bf16[16,3072]{1,0:T(8,128)(2,1)}, bf16[16,3072]{1,0:T(8,128)(2,1)}) custom-call(s32[1]{0:T(128)} %bitcast.position_ref, s32[4,128]{1,0:T(4,128)S(1)} %bitcast.25, s32[128]{0:T(128)S(1)} %copy-done.5, s32[2,128]{1,0:T(2,128)S(1)} %bitcast.28, ...), custom_call_target="tpu_custom_call" | custom-call | flops 5000000000 | tf_op jit(solution)/shard_map/far_queries/pallas_call | solution.py:411
  72.8 0.0 collective-permute-done.18
  72.8 0.6 add_add_fusion
  (14 shorter events, 0.1 us)
Async XLA Ops:
  1.6 10.5 %collective-permute-start.2 = (bf16[32,3072]{1,0:T(8,128)(2,1)S(1)}, bf16[32,3072]{1,0:T(8,128)(2,1)S(1)}, u32[]{:S(2)}, u32[]{:S(2)}) collective-permute-start(bf16[32,3072]{1,0:T(8,128)(2,1)S(1)} %pad_maximum_fusion.2.a0.a_ref), channel_id=1, source_target_pairs={{0,1},{1,0},{2,3},{3,2},{4,5},{5,4},{6,7},{7,6},{8,9},{9,8},{10,11... | collective-permute-start | bytes 589832 | tf_op jit(solution)/shard_map/ppermute | solution.py:329
  4.9 7.2 %collective-permute-start.3 = (bf16[32,3072]{1,0:T(8,128)(2,1)S(1)}, bf16[32,3072]{1,0:T(8,128)(2,1)}, u32[]{:S(2)}, u32[]{:S(2)}) collective-permute-start(bf16[32,3072]{1,0:T(8,128)(2,1)S(1)} %pad_maximum_fusion.2.a0.a_ref), channel_id=1, source_target_pairs={{1,2},{2,1},{3,4},{4,3},{5,6},{6,5},{7,8},{8,7},{9,10},{10,9},{11,... | collective-permute-start | bytes 589832 | tf_op jit(solution)/shard_map/ppermute | solution.py:332
  6.8 5.3 %copy-start = (bf16[1,128,3072]{2,1,0:T(8,128)(2,1)S(1)}, bf16[1,128,3072]{2,1,0:T(8,128)(2,1)}, u32[]{:S(2)}) copy-start(bf16[1,128,3072]{2,1,0:T(8,128)(2,1)} %param.10) | copy-start | bytes 2359300
  6.8 5.3 %copy-start.1 = (bf16[1,128,3072]{2,1,0:T(8,128)(2,1)S(1)}, bf16[1,128,3072]{2,1,0:T(8,128)(2,1)}, u32[]{:S(2)}) copy-start(bf16[1,128,3072]{2,1,0:T(8,128)(2,1)} %param.16) | copy-start | bytes 2359300
  6.9 5.3 %copy-start.4 = (s32[128,2]{0,1:T(2,128)S(1)}, s32[128,2]{0,1:T(2,128)}, u32[]{:S(2)}) copy-start(s32[128,2]{0,1:T(2,128)} %param.19) | copy-start | bytes 3076
  8.5 30.7 %collective-permute-start.1 = (bf16[256,3072]{1,0:T(8,128)(2,1)S(1)}, bf16[256,3072]{1,0:T(8,128)(2,1)}, u32[]{:S(2)}, u32[]{:S(2)}) collective-permute-start(bf16[256,3072]{1,0:T(8,128)(2,1)S(1)} %pad_maximum_fusion.kv0.kv_ref), channel_id=1, source_target_pairs={{1,2},{2,1},{3,4},{4,3},{5,6},{6,5},{7,8},{8,7},{9,10},{10,9},{11,... | collective-permute-start | bytes 4718600 | tf_op jit(solution)/shard_map/ppermute | solution.py:332
  14.4 3.9 %collective-permute-start.4 = (f32[1,3072]{1,0:T(1,128)S(1)}, f32[1,3072]{1,0:T(1,128)S(1)}, u32[]{:S(2)}, u32[]{:S(2)}) collective-permute-start(f32[1,3072]{1,0:T(1,128)S(1)} %gate_terms.1), channel_id=1, source_target_pairs={{0,64},{64,0},{128,192},{192,128},{1,65},{65,1},{129,193},{193,129... | collective-permute-start | bytes 36872 | tf_op jit(solution)/shard_map/ppermute | solution.py:280
  14.5 4.1 %collective-permute-start.5 = (f32[1,3072]{1,0:T(1,128)S(1)}, f32[1,3072]{1,0:T(1,128)S(1)}, u32[]{:S(2)}, u32[]{:S(2)}) collective-permute-start(f32[1,3072]{1,0:T(1,128)S(1)} %gate_terms.1), channel_id=1, source_target_pairs={{0,128},{64,192},{128,0},{192,64},{1,129},{65,193},{129,1},{193,65... | collective-permute-start | bytes 36872 | tf_op jit(solution)/shard_map/ppermute | solution.py:280
  16.4 3.8 %collective-permute-start.6 = (f32[1,3072]{1,0:T(1,128)S(1)}, f32[1,3072]{1,0:T(1,128)S(1)}, u32[]{:S(2)}, u32[]{:S(2)}) collective-permute-start(f32[1,3072]{1,0:T(1,128)S(1)} %gate_terms.1), channel_id=1, source_target_pairs={{0,192},{64,128},{128,64},{192,0},{1,193},{65,129},{129,65},{193,1... | collective-permute-start | bytes 36872 | tf_op jit(solution)/shard_map/ppermute | solution.py:280
  20.2 10.7 %collective-permute-start.7 = (f32[1,3072]{1,0:T(1,128)S(1)}, f32[1,3072]{1,0:T(1,128)S(1)}, u32[]{:S(2)}, u32[]{:S(2)}) collective-permute-start(f32[1,3072]{1,0:T(1,128)S(1)} %add_add_fusion.3), channel_id=1, source_target_pairs={{0,16},{1,17},{2,18},{3,19},{4,20},{5,21},{6,22},{7,23},{8,24},{9,... | collective-permute-start | bytes 36872 | tf_op jit(solution)/shard_map/ppermute | solution.py:280
  22.0 17.2 %collective-permute-start.8 = (f32[1,3072]{1,0:T(1,128)S(1)}, f32[1,3072]{1,0:T(1,128)S(1)}, u32[]{:S(2)}, u32[]{:S(2)}) collective-permute-start(f32[1,3072]{1,0:T(1,128)S(1)} %add_add_fusion.3), channel_id=1, source_target_pairs={{0,32},{1,33},{2,34},{3,35},{4,36},{5,37},{6,38},{7,39},{8,40},{9,... | collective-permute-start | bytes 36872 | tf_op jit(solution)/shard_map/ppermute | solution.py:280
  24.6 14.6 %collective-permute-start.9 = (f32[1,3072]{1,0:T(1,128)S(1)}, f32[1,3072]{1,0:T(1,128)S(1)}, u32[]{:S(2)}, u32[]{:S(2)}) collective-permute-start(f32[1,3072]{1,0:T(1,128)S(1)} %add_add_fusion.3), channel_id=1, source_target_pairs={{0,48},{1,49},{2,50},{3,51},{4,52},{5,53},{6,54},{7,55},{8,56},{9,... | collective-permute-start | bytes 36872 | tf_op jit(solution)/shard_map/ppermute | solution.py:280
  24.6 16.7 %collective-permute-start = (bf16[256,3072]{1,0:T(8,128)(2,1)S(1)}, bf16[256,3072]{1,0:T(8,128)(2,1)S(1)}, u32[]{:S(2)}, u32[]{:S(2)}) collective-permute-start(bf16[256,3072]{1,0:T(8,128)(2,1)S(1)} %pad_maximum_fusion.kv0.kv_ref), channel_id=1, source_target_pairs={{0,1},{1,0},{2,3},{3,2},{4,5},{5,4},{6,7},{7,6},{8,9},{9,8},{10,11... | collective-permute-start | bytes 4718600 | tf_op jit(solution)/shard_map/ppermute | solution.py:329
  39.2 2.1 %copy-start.2 = (f32[3072]{0:T(1024)S(1)}, f32[3072]{0:T(1024)}, u32[]{:S(2)}) copy-start(f32[3072]{0:T(1024)} %param.15) | copy-start | bytes 36868
  39.2 2.1 %copy-start.3 = (s32[128,4]{0,1:T(4,128)S(1)}, s32[128,4]{0,1:T(4,128)}, u32[]{:S(2)}) copy-start(s32[128,4]{0,1:T(4,128)} %param.17) | copy-start | bytes 6148
  39.3 2.1 %copy-start.5 = (s32[128]{0:T(128)S(1)}, s32[128]{0:T(128)}, u32[]{:S(2)}) copy-start(s32[128]{0:T(128)} %tile_count.3) | copy-start | bytes 1540
  39.4 23.0 %collective-permute-start.10 = (bf16[256,3072]{1,0:T(8,128)(2,1)S(1)}, bf16[256,3072]{1,0:T(8,128)(2,1)S(1)}, u32[]{:S(2)}, u32[]{:S(2)}) collective-permute-start(bf16[256,3072]{1,0:T(8,128)(2,1)S(1)} %pad_maximum_fusion.1), channel_id=1, source_target_pairs={{1,2},{2,1},{3,4},{4,3},{5,6},{6,5},{7,8},{8,7},{9,10},{10,9},{11,... | collective-permute-start | bytes 4718600 | tf_op jit(solution)/shard_map/ppermute | solution.py:332
  50.3 4.2 %collective-permute-start.12 = (bf16[144,3072]{1,0:T(8,128)(2,1)S(1)}, bf16[144,3072]{1,0:T(8,128)(2,1)S(1)}, u32[]{:S(2)}, u32[]{:S(2)}) collective-permute-start(bf16[144,3072]{1,0:T(8,128)(2,1)S(1)} %get-tuple-element.39), channel_id=1, source_target_pairs={{0,1},{1,0},{2,3},{3,2},{4,5},{5,4},{6,7},{7,6},{8,9},{9,8},{10,11... | collective-permute-start | bytes 2654216 | tf_op jit(solution)/shard_map/ppermute | solution.py:329
  50.3 4.2 %collective-permute-start.13 = (bf16[144,3072]{1,0:T(8,128)(2,1)S(1)}, bf16[144,3072]{1,0:T(8,128)(2,1)S(1)}, u32[]{:S(2)}, u32[]{:S(2)}) collective-permute-start(bf16[144,3072]{1,0:T(8,128)(2,1)S(1)} %get-tuple-element.40), channel_id=1, source_target_pairs={{0,1},{1,0},{2,3},{3,2},{4,5},{5,4},{6,7},{7,6},{8,9},{9,8},{10,11... | collective-permute-start | bytes 2654216 | tf_op jit(solution)/shard_map/ppermute | solution.py:329
  50.8 11.1 %collective-permute-start.11 = (f32[96,128]{1,0:T(8,128)S(1)}, f32[96,128]{1,0:T(8,128)S(1)}, u32[]{:S(2)}, u32[]{:S(2)}) collective-permute-start(f32[96,128]{1,0:T(8,128)S(1)} %get-tuple-element.38), channel_id=1, source_target_pairs={{1,2},{2,1},{3,4},{4,3},{5,6},{6,5},{7,8},{8,7},{9,10},{10,9},{11,... | collective-permute-start | bytes 147464 | tf_op jit(solution)/shard_map/ppermute | solution.py:332
  54.5 7.4 %collective-permute-start.14 = (f32[1,3072]{1,0:T(1,128)S(1)}, f32[1,3072]{1,0:T(1,128)S(1)}, u32[]{:S(2)}, u32[]{:S(2)}) collective-permute-start(f32[1,3072]{1,0:T(1,128)S(1)} %add_add_fusion.2), channel_id=1, source_target_pairs={{0,1},{1,0},{2,3},{3,2},{4,5},{5,4},{6,7},{7,6},{8,9},{9,8},{10,11... | collective-permute-start | bytes 36872 | tf_op jit(solution)/shard_map/ppermute | solution.py:280
  54.6 7.4 %collective-permute-start.15 = (f32[1,3072]{1,0:T(1,128)S(1)}, f32[1,3072]{1,0:T(1,128)S(1)}, u32[]{:S(2)}, u32[]{:S(2)}) collective-permute-start(f32[1,3072]{1,0:T(1,128)S(1)} %add_add_fusion.2), channel_id=1, source_target_pairs={{0,2},{1,3},{2,0},{3,1},{4,6},{5,7},{6,4},{7,5},{8,10},{9,11},{10,... | collective-permute-start | bytes 36872 | tf_op jit(solution)/shard_map/ppermute | solution.py:280
  55.8 6.5 %collective-permute-start.16 = (f32[1,3072]{1,0:T(1,128)S(1)}, f32[1,3072]{1,0:T(1,128)S(1)}, u32[]{:S(2)}, u32[]{:S(2)}) collective-permute-start(f32[1,3072]{1,0:T(1,128)S(1)} %add_add_fusion.2), channel_id=1, source_target_pairs={{0,3},{1,2},{2,1},{3,0},{4,7},{5,6},{6,5},{7,4},{8,11},{9,10},{10,... | collective-permute-start | bytes 36872 | tf_op jit(solution)/shard_map/ppermute | solution.py:280
  62.4 10.5 %collective-permute-start.17 = (f32[1,3072]{1,0:T(1,128)S(1)}, f32[1,3072]{1,0:T(1,128)S(1)}, u32[]{:S(2)}, u32[]{:S(2)}) collective-permute-start(f32[1,3072]{1,0:T(1,128)S(1)} %add_add_fusion.1), channel_id=1, source_target_pairs={{0,4},{1,5},{2,6},{3,7},{4,0},{5,1},{6,2},{7,3},{8,12},{9,13},{10,... | collective-permute-start | bytes 36872 | tf_op jit(solution)/shard_map/ppermute | solution.py:280
  62.5 10.4 %collective-permute-start.18 = (f32[1,3072]{1,0:T(1,128)S(1)}, f32[1,3072]{1,0:T(1,128)S(1)}, u32[]{:S(2)}, u32[]{:S(2)}) collective-permute-start(f32[1,3072]{1,0:T(1,128)S(1)} %add_add_fusion.1), channel_id=1, source_target_pairs={{0,8},{1,9},{2,10},{3,11},{4,12},{5,13},{6,14},{7,15},{8,0},{9,1},... | collective-permute-start | bytes 36872 | tf_op jit(solution)/shard_map/ppermute | solution.py:280
  62.6 10.3 %collective-permute-start.19 = (f32[1,3072]{1,0:T(1,128)S(1)}, f32[1,3072]{1,0:T(1,128)S(1)}, u32[]{:S(2)}, u32[]{:S(2)}) collective-permute-start(f32[1,3072]{1,0:T(1,128)S(1)} %add_add_fusion.1), channel_id=1, source_target_pairs={{0,12},{1,13},{2,14},{3,15},{4,8},{5,9},{6,10},{7,11},{8,4},{9,5},... | collective-permute-start | bytes 36872 | tf_op jit(solution)/shard_map/ppermute | solution.py:280

commit v3 on v2

--- a/solution.py
+++ b/solution.py
@@ -274,10 +274,18 @@
     return max(g for g in range(1, most + 1) if heads % g == 0)
 
 
-def flipped(part, axis, bit):
+def flipped(part, axis, bit, bits=2):
     size = lax.axis_size(axis)
-    flips = [f for f in (bit, 2 * bit, 3 * bit) if f < size]
+    flips = [f * bit for f in range(1, 2**bits) if f * bit < size]
     return [part] + [lax.ppermute(part, axis, [(i, i ^ f) for i in range(size)]) for f in flips]
+
+
+def flipped_apart(part):
+    size = lax.axis_size("ctx")
+    return [
+        lax.ppermute(part, "ctx", [(i, i ^ (step + 8 * (i % 2))) for i in range(size)])
+        for step in (0, 2, 4, 6)
+    ]
 
 
 def joined(parts):
@@ -337,8 +345,9 @@
     tile_list, audio_list = tile_list.T, audio_list.T
 
     a = jnp.concatenate([ak, av], axis=0)
+    kv = jnp.concatenate([k, v], axis=0)
+    kv, a = after(kv, a)
     a_far, a_mate = to_far(a), to_mate(a)
-    kv = jnp.concatenate([k, v], axis=0)
     kv_far, kv_mate = to_far(kv), to_mate(kv)
 
     f32, bf16 = jnp.float32, jnp.bfloat16
@@ -373,10 +382,12 @@
         name="gate_terms",
     )(position, audio_list, *gate_args)
 
-    total = joined(flipped(gate_part, "dp", 1))
-    parts = flipped(total, "ctx", 16)
+    total = joined(flipped(joined(flipped(gate_part, "ctx", 1, 1)), "dp", 1))
+    kv_mate, total = after(kv_mate, total)
+    parts = flipped_apart(total)
+    (kv_far, total), q_next = after((kv_far, total), q)
     kv_far, parts = after(kv_far, parts)
-    total, q_next = after(joined(parts), q)
+    total = joined(flipped(joined(parts), "ctx", 1, 1))
     qo_far = to_far(jnp.concatenate([q_next, do], axis=0))
 
     grid, pair, vspec, apair, aspec, gspec, sspec = specs(heads_per_step(heads, 8))
@@ -395,7 +406,7 @@
             array(rows + block, bf16),
             jax.ShapeDtypeStruct((4 * heads, rows), f32),
         ],
-        cost_estimate=cost(0, own_args),
+        cost_estimate=cost(20_000_000_000, own_args),
         compiler_params=params,
         name="own_queries",
     )(position, tile_list, tile_count, audio_list, *own_args, gate)
@@ -403,9 +414,7 @@
     stats_far = to_far(stats)
     mate_k, mate_v = to_mate(mate_k), to_mate(mate_v)
     (mate_k, mate_v), total = after((mate_k, mate_v), total)
-    parts = flipped(total, "ctx", 1)
-    (qo_far, stats_far), parts = after((qo_far, stats_far), parts)
-    total = joined(flipped(joined(parts), "ctx", 4))
+    parts = flipped(total, "ctx", 16)
 
     far_args = (qo_far, stats_far, kv, a, gate, own_sums, mate_k, mate_v)
     dk, dv, dak, dav = pl.pallas_call(
@@ -419,6 +428,9 @@
         name="far_queries",
     )(position, tile_list, tile_count, audio_list, *far_args)
 
+    dak, parts = after(dak, parts)
+    total = joined(parts)
+
     return (
         dq.reshape(clips, rows, width),
         dk.reshape(clips, rows, width),

time: 73.8 us -> 66.3 us (0.90)
  waiting for transfers between devices: 15.8 us -> 6.41 us
  starting transfers between devices: 37.6 us -> 39.6 us
  other arithmetic: 3.34 us -> 2.42 us
    ppermute x0 -> x4, starting transfers between devices: none -> 14.7 us  [flipped_apart(): lax.ppermute(part, 'ctx', [(i, i ^ step + 8 * (i % 2)) for i in range(siz...]
    ppermute x12 -> x8, starting transfers between devices: 16.3 us -> 8.68 us  [flipped(): lax.ppermute(part, axis, [(i, i ^ f) for i in range(size)])]
    ppermute x4, starting transfers between devices: 10.1 us -> 3.93 us  [to_mate(): return lax.ppermute(x, 'ctx', mate_pairs)]
    ppermute x12 -> x8, waiting for transfers between devices: 10.5 us -> 4.6 us  [flipped(): lax.ppermute(part, axis, [(i, i ^ f) for i in range(size)])]
    ppermute x4, waiting for transfers between devices: 5.22 us -> 1.33 us  [to_far(): return lax.ppermute(x, 'ctx', far_pairs)]
    ppermute x4, starting transfers between devices: 11.1 us -> 12.3 us  [to_far(): return lax.ppermute(x, 'ctx', far_pairs)]
    concatenate x1, other arithmetic: 0.96 us -> 0.02 us  [per_device(): a = jnp.concatenate([ak, av], axis=0)]
  transfers between devices with their start and end apart: 20 -> 20, of which waited for: 5 -> 6; matrix products, arithmetic and copies ran while one was open for 2% -> 0% of each run, Pallas kernels for 22% -> 24%
where the time goes in v3:
time: 66.3 us; the launch traced here: 65.4 us
  starting transfers between devices  39.6 us (60%)
  Pallas kernels  16 us (24%)
  waiting for transfers between devices  6.41 us (10%)
  other arithmetic  2.42 us (4%)
  between operations  0.93 us (1%)
    ppermute x4, starting transfers between devices, flipped_apart(): lax.ppermute(part, 'ctx', [(i, i ^ step + 8 * (i % 2)) for i in range(siz...  14.7 us
    ppermute x4, starting transfers between devices, to_far(): return lax.ppermute(x, 'ctx', far_pairs)  12.3 us
    pallas_call x1, Pallas kernels, per_device(): pl.pallas_call(own_kernel, grid=grid, in_specs=[SMEM] * 4 + [vspec] * 2 +...  9.03 us
    ppermute x8, starting transfers between devices, flipped(): lax.ppermute(part, axis, [(i, i ^ f) for i in range(size)])  8.68 us
    pallas_call x1, Pallas kernels, per_device(): pl.pallas_call(far_kernel, grid=grid, in_specs=[SMEM] * 4 + [pair, sspec,...  4.74 us
    ppermute x8, waiting for transfers between devices, flipped(): lax.ppermute(part, axis, [(i, i ^ f) for i in range(size)])  4.6 us
    ppermute x4, starting transfers between devices, to_mate(): return lax.ppermute(x, 'ctx', mate_pairs)  3.93 us
    pallas_call x1, Pallas kernels, per_device(): pl.pallas_call(gate_kernel, grid=grid, in_specs=[SMEM, SMEM] + [vspec] *...  2.22 us
  transfers between devices with their start and end apart: 20, of which 6 were waited for; matrix products, arithmetic and copies ran while one was open for 0% of the time, Pallas kernels for 24%

profile of v3, /device:TPU:1, one launch (start us, length us, event | category | flops | bytes accessed | tf_op | source)
XLA Modules:
  0.0 65.4 jit_solution(13083566659643134285)
XLA Ops:
  0.7 1.6 %pad_maximum_fusion.kv0.kv_ref = bf16[256,3072]{1,0:T(8,128)(2,1)S(1)} fusion(bf16[128,3072]{1,0:T(8,128)(2,1)} %bitcast.29, bf16[128,3072]{1,0:T(8,128)(2,1)} %bitcast.30), kind=kLoop, calls=%fused_computation | loop fusion | flops 3145728 | bytes 3145728 | tf_op jit(solution)/shard_map/concatenate | solution.py:348
  2.3 3.3 %collective-permute-start.1 = (bf16[32,3072]{1,0:T(8,128)(2,1)S(1)}, bf16[32,3072]{1,0:T(8,128)(2,1)S(1)}, u32[]{:S(2)}, u32[]{:S(2)}) collective-permute-start(bf16[32,3072]{1,0:T(8,128)(2,1)S(1)} %pad_maximum_fusion.2.a0.a_ref), channel_id=1, source_target_pairs={{0,1},{1,0},{2,3},{3,2},{4,5},{5,4},{6,7},{7,6},{8,9},{9,8},{10,11... | collective-permute-start | bytes 589832 | tf_op jit(solution)/shard_map/ppermute | solution.py:337
  5.7 1.9 %collective-permute-start.2 = (bf16[32,3072]{1,0:T(8,128)(2,1)S(1)}, bf16[32,3072]{1,0:T(8,128)(2,1)}, u32[]{:S(2)}, u32[]{:S(2)}) collective-permute-start(bf16[32,3072]{1,0:T(8,128)(2,1)S(1)} %pad_maximum_fusion.2.a0.a_ref), channel_id=1, source_target_pairs={{1,2},{2,1},{3,4},{4,3},{5,6},{6,5},{7,8},{8,7},{9,10},{10,9},{11,... | collective-permute-start | bytes 589832 | tf_op jit(solution)/shard_map/ppermute | solution.py:340
  7.6 0.1 collective-permute-start
  7.7 3.7 %collective-permute-start.7 = (bf16[256,3072]{1,0:T(8,128)(2,1)S(1)}, bf16[256,3072]{1,0:T(8,128)(2,1)}, u32[]{:S(2)}, u32[]{:S(2)}) collective-permute-start(bf16[256,3072]{1,0:T(8,128)(2,1)S(1)} %pad_maximum_fusion.kv0.kv_ref), channel_id=1, source_target_pairs={{1,2},{2,1},{3,4},{4,3},{5,6},{6,5},{7,8},{8,7},{9,10},{10,9},{11,... | collective-permute-start | bytes 4718600 | tf_op jit(solution)/shard_map/ppermute | solution.py:340
  11.4 0.0 collective-permute-done.1.a1
  11.4 1.3 %collective-permute-done.2.a2 = bf16[32,3072]{1,0:T(8,128)(2,1)} collective-permute-done((bf16[32,3072]{1,0:T(8,128)(2,1)S(1)}, bf16[32,3072]{1,0:T(8,128)(2,1)}, u32[]{:S(2)}, u32[]{:S(2)}) %collective-permute-start.2) | collective-permute-done | bytes 196640 | tf_op jit(solution)/shard_map/ppermute | solution.py:340
  12.8 2.2 %gate_terms.1 = f32[1,3072]{1,0:T(1,128)S(1)} custom-call(s32[1]{0:T(128)} %bitcast.position_ref, s32[2,128]{1,0:T(2,128)S(1)} %bitcast.26, bf16[128,3072]{1,0:T(8,128)(2,1)S(1)} %bitcast.16, bf16[128,3072]{1,0:T(8,128)(2,1)S(1)} %bitcast.19, bf16[32,3072]{1,0:T(8,128)(2,1)S(1)} %pad_maximum_fusion.2.a0.a_ref, ...), custom_call_target="tpu_custom_call" | custom-call | flops 20000000000 | tf_op jit(solution)/shard_map/gate_terms/pallas_call | solution.py:374
  15.0 0.1 collective-permute-start.3
  15.1 1.2 %collective-permute-done.3 = f32[1,3072]{1,0:T(1,128)S(1)} collective-permute-done((f32[1,3072]{1,0:T(1,128)S(1)}, f32[1,3072]{1,0:T(1,128)S(1)}, u32[]{:S(2)}, u32[]{:S(2)}) %collective-permute-start.3) | collective-permute-done | bytes 12320 | tf_op jit(solution)/shard_map/ppermute | solution.py:280
  16.3 0.1 collective-permute-start.4
  16.4 2.4 %collective-permute-start.5 = (f32[1,3072]{1,0:T(1,128)S(1)}, f32[1,3072]{1,0:T(1,128)S(1)}, u32[]{:S(2)}, u32[]{:S(2)}) collective-permute-start(f32[1,3072]{1,0:T(1,128)S(1)} %add.33), channel_id=1, source_target_pairs={{0,128},{64,192},{128,0},{192,64},{1,129},{65,193},{129,1},{193,65... | collective-permute-start | bytes 36872 | tf_op jit(solution)/shard_map/ppermute | solution.py:280
  18.7 1.5 %collective-permute-start.6 = (f32[1,3072]{1,0:T(1,128)S(1)}, f32[1,3072]{1,0:T(1,128)S(1)}, u32[]{:S(2)}, u32[]{:S(2)}) collective-permute-start(f32[1,3072]{1,0:T(1,128)S(1)} %add.33), channel_id=1, source_target_pairs={{0,192},{64,128},{128,64},{192,0},{1,193},{65,129},{129,65},{193,1... | collective-permute-start | bytes 36872 | tf_op jit(solution)/shard_map/ppermute | solution.py:280
  20.2 0.0 collective-permute-done.4
  20.2 0.3 collective-permute-done.5
  20.6 1.9 %collective-permute-done.6 = f32[1,3072]{1,0:T(1,128)S(1)} collective-permute-done((f32[1,3072]{1,0:T(1,128)S(1)}, f32[1,3072]{1,0:T(1,128)S(1)}, u32[]{:S(2)}, u32[]{:S(2)}) %collective-permute-start.6) | collective-permute-done | bytes 12320 | tf_op jit(solution)/shard_map/ppermute | solution.py:280
  22.5 0.0 copy-start.2
  22.5 0.0 copy-start.3
  22.5 0.0 copy-start.5
  22.5 0.0 collective-permute-done.kv1
  22.5 5.7 %collective-permute-start.10 = (f32[1,3072]{1,0:T(1,128)S(1)}, f32[1,3072]{1,0:T(1,128)S(1)}, u32[]{:S(2)}, u32[]{:S(2)}) collective-permute-start(f32[1,3072]{1,0:T(1,128)S(1)} %add_add_fusion.2), channel_id=1, source_target_pairs={{0,4},{1,13},{2,6},{3,15},{4,0},{5,9},{6,2},{7,11},{8,12},{9,5},{1... | collective-permute-start | bytes 36872 | tf_op jit(solution)/shard_map/ppermute | solution.py:286
  28.2 1.8 %collective-permute-start.11 = (f32[1,3072]{1,0:T(1,128)S(1)}, f32[1,3072]{1,0:T(1,128)S(1)}, u32[]{:S(2)}, u32[]{:S(2)}) collective-permute-start(f32[1,3072]{1,0:T(1,128)S(1)} %add_add_fusion.2), channel_id=1, source_target_pairs={{0,6},{1,15},{2,4},{3,13},{4,2},{5,11},{6,0},{7,9},{8,14},{9,7},{1... | collective-permute-start | bytes 36872 | tf_op jit(solution)/shard_map/ppermute | solution.py:286
  30.0 4.2 %collective-permute-start.8 = (f32[1,3072]{1,0:T(1,128)S(1)}, f32[1,3072]{1,0:T(1,128)S(1)}, u32[]{:S(2)}, u32[]{:S(2)}) collective-permute-start(f32[1,3072]{1,0:T(1,128)S(1)} %add_add_fusion.2), channel_id=1, source_target_pairs={{0,0},{1,9},{2,2},{3,11},{4,4},{5,13},{6,6},{7,15},{8,8},{9,1},{10... | collective-permute-start | bytes 36872 | tf_op jit(solution)/shard_map/ppermute | solution.py:286
  34.1 3.1 %collective-permute-start.9 = (f32[1,3072]{1,0:T(1,128)S(1)}, f32[1,3072]{1,0:T(1,128)S(1)}, u32[]{:S(2)}, u32[]{:S(2)}) collective-permute-start(f32[1,3072]{1,0:T(1,128)S(1)} %add_add_fusion.2), channel_id=1, source_target_pairs={{0,2},{1,11},{2,0},{3,9},{4,6},{5,15},{6,4},{7,13},{8,10},{9,3},{1... | collective-permute-start | bytes 36872 | tf_op jit(solution)/shard_map/ppermute | solution.py:286
  37.2 0.0 collective-permute-done.7.kv2
  37.3 0.1 pad_maximum_fusion.1
  37.4 1.9 %collective-permute-start.12 = (bf16[256,3072]{1,0:T(8,128)(2,1)S(1)}, bf16[256,3072]{1,0:T(8,128)(2,1)S(1)}, u32[]{:S(2)}, u32[]{:S(2)}) collective-permute-start(bf16[256,3072]{1,0:T(8,128)(2,1)S(1)} %pad_maximum_fusion.1), channel_id=1, source_target_pairs={{1,2},{2,1},{3,4},{4,3},{5,6},{6,5},{7,8},{8,7},{9,10},{10,9},{11,... | collective-permute-start | bytes 4718600 | tf_op jit(solution)/shard_map/ppermute | solution.py:340
  39.3 0.0 collective-permute-done.10
  39.3 0.0 collective-permute-done.11
  39.3 0.0 collective-permute-done.8
  39.3 0.5 collective-permute-done.9
  39.8 9.0 %own_queries.1 = (bf16[128,3072]{1,0:T(8,128)(2,1)}, f32[288,3072]{1,0:T(8,128)S(1)}, bf16[144,3072]{1,0:T(8,128)(2,1)S(1)}, bf16[144,3072]{1,0:T(8,128)(2,1)S(1)}, f32[96,128]{1,0:T(8,128)S(1)}) custom-call(s32[1]{0:T(128)} %bitcast.position_ref, s32[4,128]{1,0:T(4,128)S(1)} %bitcast.24, s32[128]{0:T(128)S(1)} %copy-done.5, s32[2,128]{1,0:T(2,128)S(1)} %bitcast.27, ...), custom_call_target="tpu_custom_call" | custom-call | flops 20000000000 | tf_op jit(solution)/shard_map/own_queries/pallas_call | solution.py:397
  48.8 0.0 collective-permute-start.14
  48.8 0.5 collective-permute-start.15
  49.3 4.7 %collective-permute-start.13 = (f32[96,128]{1,0:T(8,128)S(1)}, f32[96,128]{1,0:T(8,128)S(1)}, u32[]{:S(2)}, u32[]{:S(2)}) collective-permute-start(f32[96,128]{1,0:T(8,128)S(1)} %get-tuple-element.42), channel_id=1, source_target_pairs={{1,2},{2,1},{3,4},{4,3},{5,6},{6,5},{7,8},{8,7},{9,10},{10,9},{11,... | collective-permute-start | bytes 147464 | tf_op jit(solution)/shard_map/ppermute | solution.py:340
  54.1 0.1 collective-permute-start.16
  54.2 1.2 %collective-permute-done.16 = f32[1,3072]{1,0:T(1,128)S(1)} collective-permute-done((f32[1,3072]{1,0:T(1,128)S(1)}, f32[1,3072]{1,0:T(1,128)S(1)}, u32[]{:S(2)}, u32[]{:S(2)}) %collective-permute-start.16) | collective-permute-done | bytes 12320 | tf_op jit(solution)/shard_map/ppermute | solution.py:280
  55.4 0.0 collective-permute-done.15.mate_v_in
  55.4 1.6 %collective-permute-start.17 = (f32[1,3072]{1,0:T(1,128)S(1)}, f32[1,3072]{1,0:T(1,128)S(1)}, u32[]{:S(2)}, u32[]{:S(2)}) collective-permute-start(f32[1,3072]{1,0:T(1,128)S(1)} %add.40), channel_id=1, source_target_pairs={{0,16},{1,17},{2,18},{3,19},{4,20},{5,21},{6,22},{7,23},{8,24},{9,... | collective-permute-start | bytes 36872 | tf_op jit(solution)/shard_map/ppermute | solution.py:280
  57.0 2.9 %collective-permute-start.18 = (f32[1,3072]{1,0:T(1,128)S(1)}, f32[1,3072]{1,0:T(1,128)S(1)}, u32[]{:S(2)}, u32[]{:S(2)}) collective-permute-start(f32[1,3072]{1,0:T(1,128)S(1)} %add.40), channel_id=1, source_target_pairs={{0,32},{1,33},{2,34},{3,35},{4,36},{5,37},{6,38},{7,39},{8,40},{9,... | collective-permute-start | bytes 36872 | tf_op jit(solution)/shard_map/ppermute | solution.py:280
  59.9 0.0 collective-permute-start.19
  60.0 0.0 collective-permute-done.13.stat_ref
  60.0 0.0 collective-permute-done.12.qo_ref
  60.0 4.7 %far_queries.1 = (bf16[128,3072]{1,0:T(8,128)(2,1)}, bf16[128,3072]{1,0:T(8,128)(2,1)}, bf16[16,3072]{1,0:T(8,128)(2,1)}, bf16[16,3072]{1,0:T(8,128)(2,1)}) custom-call(s32[1]{0:T(128)} %bitcast.position_ref, s32[4,128]{1,0:T(4,128)S(1)} %bitcast.25, s32[128]{0:T(128)S(1)} %copy-done.5, s32[2,128]{1,0:T(2,128)S(1)} %bitcast.28, ...), custom_call_target="tpu_custom_call" | custom-call | flops 5000000000 | tf_op jit(solution)/shard_map/far_queries/pallas_call | solution.py:420
  64.7 0.0 collective-permute-done.17
  64.7 0.0 collective-permute-done.18
  64.7 0.0 collective-permute-done.19
  64.7 0.6 add_add_fusion
  (19 shorter events, 0.1 us)
Async XLA Ops:
  0.6 1.7 %copy-start.6 = (bf16[1,16,3072]{2,1,0:T(8,128)(2,1)S(1)}, bf16[1,16,3072]{2,1,0:T(8,128)(2,1)}, u32[]{:S(2)}) copy-start(bf16[1,16,3072]{2,1,0:T(8,128)(2,1)} %param.14) | copy-start | bytes 294916
  0.6 1.7 %copy-start.7 = (bf16[1,16,3072]{2,1,0:T(8,128)(2,1)S(1)}, bf16[1,16,3072]{2,1,0:T(8,128)(2,1)}, u32[]{:S(2)}) copy-start(bf16[1,16,3072]{2,1,0:T(8,128)(2,1)} %param.13) | copy-start | bytes 294916
  0.7 12.1 %copy-start = (bf16[1,128,3072]{2,1,0:T(8,128)(2,1)S(1)}, bf16[1,128,3072]{2,1,0:T(8,128)(2,1)}, u32[]{:S(2)}) copy-start(bf16[1,128,3072]{2,1,0:T(8,128)(2,1)} %param.10) | copy-start | bytes 2359300
  0.7 12.1 %copy-start.1 = (bf16[1,128,3072]{2,1,0:T(8,128)(2,1)S(1)}, bf16[1,128,3072]{2,1,0:T(8,128)(2,1)}, u32[]{:S(2)}) copy-start(bf16[1,128,3072]{2,1,0:T(8,128)(2,1)} %param.16) | copy-start | bytes 2359300
  0.7 12.1 %copy-start.4 = (s32[128,2]{0,1:T(2,128)S(1)}, s32[128,2]{0,1:T(2,128)}, u32[]{:S(2)}) copy-start(s32[128,2]{0,1:T(2,128)} %param.19) | copy-start | bytes 3076
  2.3 9.1 %collective-permute-start.1 = (bf16[32,3072]{1,0:T(8,128)(2,1)S(1)}, bf16[32,3072]{1,0:T(8,128)(2,1)S(1)}, u32[]{:S(2)}, u32[]{:S(2)}) collective-permute-start(bf16[32,3072]{1,0:T(8,128)(2,1)S(1)} %pad_maximum_fusion.2.a0.a_ref), channel_id=1, source_target_pairs={{0,1},{1,0},{2,3},{3,2},{4,5},{5,4},{6,7},{7,6},{8,9},{9,8},{10,11... | collective-permute-start | bytes 589832 | tf_op jit(solution)/shard_map/ppermute | solution.py:337
  5.7 7.1 %collective-permute-start.2 = (bf16[32,3072]{1,0:T(8,128)(2,1)S(1)}, bf16[32,3072]{1,0:T(8,128)(2,1)}, u32[]{:S(2)}, u32[]{:S(2)}) collective-permute-start(bf16[32,3072]{1,0:T(8,128)(2,1)S(1)} %pad_maximum_fusion.2.a0.a_ref), channel_id=1, source_target_pairs={{1,2},{2,1},{3,4},{4,3},{5,6},{6,5},{7,8},{8,7},{9,10},{10,9},{11,... | collective-permute-start | bytes 589832 | tf_op jit(solution)/shard_map/ppermute | solution.py:340
  7.6 15.0 %collective-permute-start = (bf16[256,3072]{1,0:T(8,128)(2,1)S(1)}, bf16[256,3072]{1,0:T(8,128)(2,1)}, u32[]{:S(2)}, u32[]{:S(2)}) collective-permute-start(bf16[256,3072]{1,0:T(8,128)(2,1)S(1)} %pad_maximum_fusion.kv0.kv_ref), channel_id=1, source_target_pairs={{0,1},{1,0},{2,3},{3,2},{4,5},{5,4},{6,7},{7,6},{8,9},{9,8},{10,11... | collective-permute-start | bytes 4718600 | tf_op jit(solution)/shard_map/ppermute | solution.py:337
  7.7 29.6 %collective-permute-start.7 = (bf16[256,3072]{1,0:T(8,128)(2,1)S(1)}, bf16[256,3072]{1,0:T(8,128)(2,1)}, u32[]{:S(2)}, u32[]{:S(2)}) collective-permute-start(bf16[256,3072]{1,0:T(8,128)(2,1)S(1)} %pad_maximum_fusion.kv0.kv_ref), channel_id=1, source_target_pairs={{1,2},{2,1},{3,4},{4,3},{5,6},{6,5},{7,8},{8,7},{9,10},{10,9},{11,... | collective-permute-start | bytes 4718600 | tf_op jit(solution)/shard_map/ppermute | solution.py:340
  15.0 1.3 %collective-permute-start.3 = (f32[1,3072]{1,0:T(1,128)S(1)}, f32[1,3072]{1,0:T(1,128)S(1)}, u32[]{:S(2)}, u32[]{:S(2)}) collective-permute-start(f32[1,3072]{1,0:T(1,128)S(1)} %gate_terms.1), channel_id=1, source_target_pairs={{0,1},{1,0},{2,3},{3,2},{4,5},{5,4},{6,7},{7,6},{8,9},{9,8},{10,11... | collective-permute-start | bytes 36872 | tf_op jit(solution)/shard_map/ppermute | solution.py:280
  16.3 3.9 %collective-permute-start.4 = (f32[1,3072]{1,0:T(1,128)S(1)}, f32[1,3072]{1,0:T(1,128)S(1)}, u32[]{:S(2)}, u32[]{:S(2)}) collective-permute-start(f32[1,3072]{1,0:T(1,128)S(1)} %add.33), channel_id=1, source_target_pairs={{0,64},{64,0},{128,192},{192,128},{1,65},{65,1},{129,193},{193,129... | collective-permute-start | bytes 36872 | tf_op jit(solution)/shard_map/ppermute | solution.py:280
  16.4 4.2 %collective-permute-start.5 = (f32[1,3072]{1,0:T(1,128)S(1)}, f32[1,3072]{1,0:T(1,128)S(1)}, u32[]{:S(2)}, u32[]{:S(2)}) collective-permute-start(f32[1,3072]{1,0:T(1,128)S(1)} %add.33), channel_id=1, source_target_pairs={{0,128},{64,192},{128,0},{192,64},{1,129},{65,193},{129,1},{193,65... | collective-permute-start | bytes 36872 | tf_op jit(solution)/shard_map/ppermute | solution.py:280
  18.7 3.8 %collective-permute-start.6 = (f32[1,3072]{1,0:T(1,128)S(1)}, f32[1,3072]{1,0:T(1,128)S(1)}, u32[]{:S(2)}, u32[]{:S(2)}) collective-permute-start(f32[1,3072]{1,0:T(1,128)S(1)} %add.33), channel_id=1, source_target_pairs={{0,192},{64,128},{128,64},{192,0},{1,193},{65,129},{129,65},{193,1... | collective-permute-start | bytes 36872 | tf_op jit(solution)/shard_map/ppermute | solution.py:280
  22.5 17.3 %copy-start.2 = (f32[3072]{0:T(1024)S(1)}, f32[3072]{0:T(1024)}, u32[]{:S(2)}) copy-start(f32[3072]{0:T(1024)} %param.15) | copy-start | bytes 36868
  22.5 17.3 %copy-start.3 = (s32[128,4]{0,1:T(4,128)S(1)}, s32[128,4]{0,1:T(4,128)}, u32[]{:S(2)}) copy-start(s32[128,4]{0,1:T(4,128)} %param.17) | copy-start | bytes 6148
  22.5 17.3 %copy-start.5 = (s32[128]{0:T(128)S(1)}, s32[128]{0:T(128)}, u32[]{:S(2)}) copy-start(s32[128]{0:T(128)} %tile_count.3) | copy-start | bytes 1540
  22.5 16.7 %collective-permute-start.10 = (f32[1,3072]{1,0:T(1,128)S(1)}, f32[1,3072]{1,0:T(1,128)S(1)}, u32[]{:S(2)}, u32[]{:S(2)}) collective-permute-start(f32[1,3072]{1,0:T(1,128)S(1)} %add_add_fusion.2), channel_id=1, source_target_pairs={{0,4},{1,13},{2,6},{3,15},{4,0},{5,9},{6,2},{7,11},{8,12},{9,5},{1... | collective-permute-start | bytes 36872 | tf_op jit(solution)/shard_map/ppermute | solution.py:286
  28.2 11.1 %collective-permute-start.11 = (f32[1,3072]{1,0:T(1,128)S(1)}, f32[1,3072]{1,0:T(1,128)S(1)}, u32[]{:S(2)}, u32[]{:S(2)}) collective-permute-start(f32[1,3072]{1,0:T(1,128)S(1)} %add_add_fusion.2), channel_id=1, source_target_pairs={{0,6},{1,15},{2,4},{3,13},{4,2},{5,11},{6,0},{7,9},{8,14},{9,7},{1... | collective-permute-start | bytes 36872 | tf_op jit(solution)/shard_map/ppermute | solution.py:286
  30.0 9.3 %collective-permute-start.8 = (f32[1,3072]{1,0:T(1,128)S(1)}, f32[1,3072]{1,0:T(1,128)S(1)}, u32[]{:S(2)}, u32[]{:S(2)}) collective-permute-start(f32[1,3072]{1,0:T(1,128)S(1)} %add_add_fusion.2), channel_id=1, source_target_pairs={{0,0},{1,9},{2,2},{3,11},{4,4},{5,13},{6,6},{7,15},{8,8},{9,1},{10... | collective-permute-start | bytes 36872 | tf_op jit(solution)/shard_map/ppermute | solution.py:286
  34.1 5.6 %collective-permute-start.9 = (f32[1,3072]{1,0:T(1,128)S(1)}, f32[1,3072]{1,0:T(1,128)S(1)}, u32[]{:S(2)}, u32[]{:S(2)}) collective-permute-start(f32[1,3072]{1,0:T(1,128)S(1)} %add_add_fusion.2), channel_id=1, source_target_pairs={{0,2},{1,11},{2,0},{3,9},{4,6},{5,15},{6,4},{7,13},{8,10},{9,3},{1... | collective-permute-start | bytes 36872 | tf_op jit(solution)/shard_map/ppermute | solution.py:286
  37.4 22.6 %collective-permute-start.12 = (bf16[256,3072]{1,0:T(8,128)(2,1)S(1)}, bf16[256,3072]{1,0:T(8,128)(2,1)S(1)}, u32[]{:S(2)}, u32[]{:S(2)}) collective-permute-start(bf16[256,3072]{1,0:T(8,128)(2,1)S(1)} %pad_maximum_fusion.1), channel_id=1, source_target_pairs={{1,2},{2,1},{3,4},{4,3},{5,6},{6,5},{7,8},{8,7},{9,10},{10,9},{11,... | collective-permute-start | bytes 4718600 | tf_op jit(solution)/shard_map/ppermute | solution.py:340
  48.8 6.5 %collective-permute-start.14 = (bf16[144,3072]{1,0:T(8,128)(2,1)S(1)}, bf16[144,3072]{1,0:T(8,128)(2,1)S(1)}, u32[]{:S(2)}, u32[]{:S(2)}) collective-permute-start(bf16[144,3072]{1,0:T(8,128)(2,1)S(1)} %get-tuple-element.44), channel_id=1, source_target_pairs={{0,1},{1,0},{2,3},{3,2},{4,5},{5,4},{6,7},{7,6},{8,9},{9,8},{10,11... | collective-permute-start | bytes 2654216 | tf_op jit(solution)/shard_map/ppermute | solution.py:337
  48.8 6.6 %collective-permute-start.15 = (bf16[144,3072]{1,0:T(8,128)(2,1)S(1)}, bf16[144,3072]{1,0:T(8,128)(2,1)S(1)}, u32[]{:S(2)}, u32[]{:S(2)}) collective-permute-start(bf16[144,3072]{1,0:T(8,128)(2,1)S(1)} %get-tuple-element.45), channel_id=1, source_target_pairs={{0,1},{1,0},{2,3},{3,2},{4,5},{5,4},{6,7},{7,6},{8,9},{9,8},{10,11... | collective-permute-start | bytes 2654216 | tf_op jit(solution)/shard_map/ppermute | solution.py:337
  49.3 10.6 %collective-permute-start.13 = (f32[96,128]{1,0:T(8,128)S(1)}, f32[96,128]{1,0:T(8,128)S(1)}, u32[]{:S(2)}, u32[]{:S(2)}) collective-permute-start(f32[96,128]{1,0:T(8,128)S(1)} %get-tuple-element.42), channel_id=1, source_target_pairs={{1,2},{2,1},{3,4},{4,3},{5,6},{6,5},{7,8},{8,7},{9,10},{10,9},{11,... | collective-permute-start | bytes 147464 | tf_op jit(solution)/shard_map/ppermute | solution.py:340
  54.1 1.3 %collective-permute-start.16 = (f32[1,3072]{1,0:T(1,128)S(1)}, f32[1,3072]{1,0:T(1,128)S(1)}, u32[]{:S(2)}, u32[]{:S(2)}) collective-permute-start(f32[1,3072]{1,0:T(1,128)S(1)} %add_add_fusion.1), channel_id=1, source_target_pairs={{0,1},{1,0},{2,3},{3,2},{4,5},{5,4},{6,7},{7,6},{8,9},{9,8},{10,11... | collective-permute-start | bytes 36872 | tf_op jit(solution)/shard_map/ppermute | solution.py:280
  55.4 9.3 %collective-permute-start.17 = (f32[1,3072]{1,0:T(1,128)S(1)}, f32[1,3072]{1,0:T(1,128)S(1)}, u32[]{:S(2)}, u32[]{:S(2)}) collective-permute-start(f32[1,3072]{1,0:T(1,128)S(1)} %add.40), channel_id=1, source_target_pairs={{0,16},{1,17},{2,18},{3,19},{4,20},{5,21},{6,22},{7,23},{8,24},{9,... | collective-permute-start | bytes 36872 | tf_op jit(solution)/shard_map/ppermute | solution.py:280
  57.0 7.7 %collective-permute-start.18 = (f32[1,3072]{1,0:T(1,128)S(1)}, f32[1,3072]{1,0:T(1,128)S(1)}, u32[]{:S(2)}, u32[]{:S(2)}) collective-permute-start(f32[1,3072]{1,0:T(1,128)S(1)} %add.40), channel_id=1, source_target_pairs={{0,32},{1,33},{2,34},{3,35},{4,36},{5,37},{6,38},{7,39},{8,40},{9,... | collective-permute-start | bytes 36872 | tf_op jit(solution)/shard_map/ppermute | solution.py:280
  59.9 4.8 %collective-permute-start.19 = (f32[1,3072]{1,0:T(1,128)S(1)}, f32[1,3072]{1,0:T(1,128)S(1)}, u32[]{:S(2)}, u32[]{:S(2)}) collective-permute-start(f32[1,3072]{1,0:T(1,128)S(1)} %add.40), channel_id=1, source_target_pairs={{0,48},{1,49},{2,50},{3,51},{4,52},{5,53},{6,54},{7,55},{8,56},{9,... | collective-permute-start | bytes 36872 | tf_op jit(solution)/shard_map/ppermute | solution.py:280

commit v4 on v3

--- a/solution.py
+++ b/solution.py
@@ -24,6 +24,15 @@
 
 def dot_lead(a, b):
     return lax.dot_general(a, b, (((0,), (0,)), ((), ())), preferred_element_type=jnp.float32)
+
+
+def far_place(clip, index, clips, count, ends_apart):
+    other = index + 1 if index % 2 else index - 1
+    if 0 <= other < count:
+        return clip * count + other
+    if clips % 2 == 0 and not ends_apart:
+        return (clip ^ 1) * count + index
+    return clip * count + other % count
 
 
 def mate_of(position):
@@ -331,13 +340,18 @@
     count = lax.axis_size("ctx")
     position = lax.axis_index("ctx").astype(jnp.int32).reshape(1)
     mate_pairs = [(i, i ^ 1) for i in range(count)]
-    far_pairs = [(i + s, i + 1 - s) for i in range(1, count - 1, 2) for s in range(2)]
+    clip_places = lax.axis_size("dp")
 
     def to_mate(x):
         return lax.ppermute(x, "ctx", mate_pairs)
 
-    def to_far(x):
-        return lax.ppermute(x, "ctx", far_pairs)
+    def to_far(x, ends_apart):
+        pairs = [
+            (c * count + i, far_place(c, i, clip_places, count, ends_apart))
+            for c in range(clip_places)
+            for i in range(count)
+        ]
+        return lax.ppermute(x, ("dp", "ctx"), pairs)
 
     q, k, v, do = (x.reshape(rows, width) for x in (video_query, video_key, video_value, out_cotangent))
     ak, av = (x.reshape(block, width) for x in (audio_key, audio_value))
@@ -347,8 +361,8 @@
     a = jnp.concatenate([ak, av], axis=0)
     kv = jnp.concatenate([k, v], axis=0)
     kv, a = after(kv, a)
-    a_far, a_mate = to_far(a), to_mate(a)
-    kv_far, kv_mate = to_far(kv), to_mate(kv)
+    a_far, a_mate = to_far(a, False), to_mate(a)
+    kv_far, kv_mate = to_far(kv, False), to_mate(kv)
 
     f32, bf16 = jnp.float32, jnp.bfloat16
 
@@ -369,7 +383,7 @@
 
     params = pltpu.CompilerParams(vmem_limit_bytes=24 * 2**20)
 
-    grid, pair, vspec, apair, aspec, gspec, sspec = specs(heads_per_step(heads, 12))
+    grid, pair, vspec, apair, aspec, gspec, sspec = specs(heads_per_step(heads, 24))
     gate_args = (q, do, a, a_mate, a_far)
     gate_part = pl.pallas_call(
         gate_kernel,
@@ -382,13 +396,13 @@
         name="gate_terms",
     )(position, audio_list, *gate_args)
 
-    total = joined(flipped(joined(flipped(gate_part, "ctx", 1, 1)), "dp", 1))
+    total = joined(flipped(gate_part, "ctx", 1, 1))
     kv_mate, total = after(kv_mate, total)
     parts = flipped_apart(total)
-    (kv_far, total), q_next = after((kv_far, total), q)
     kv_far, parts = after(kv_far, parts)
-    total = joined(flipped(joined(parts), "ctx", 1, 1))
-    qo_far = to_far(jnp.concatenate([q_next, do], axis=0))
+    parts, q_next = after(parts, q)
+    qo_far = to_far(jnp.concatenate([q_next, do], axis=0), True)
+    parts = flipped(joined(parts), "dp", 1)
 
     grid, pair, vspec, apair, aspec, gspec, sspec = specs(heads_per_step(heads, 8))
     sums_spec = cols_spec(2 * (rows + block), vspec.block_shape[1])
@@ -406,13 +420,15 @@
             array(rows + block, bf16),
             jax.ShapeDtypeStruct((4 * heads, rows), f32),
         ],
-        cost_estimate=cost(20_000_000_000, own_args),
+        cost_estimate=cost(0_000_000_000, own_args),
         compiler_params=params,
         name="own_queries",
     )(position, tile_list, tile_count, audio_list, *own_args, gate)
 
-    stats_far = to_far(stats)
+    (stats, mate_k, mate_v), parts = after((stats, mate_k, mate_v), parts)
+    stats_far = to_far(stats, True)
     mate_k, mate_v = to_mate(mate_k), to_mate(mate_v)
+    total = joined(flipped(joined(parts), "ctx", 1, 1))
     (mate_k, mate_v), total = after((mate_k, mate_v), total)
     parts = flipped(total, "ctx", 16)
 

time: 66.3 us -> 62.6 us (0.944); the launches traced: 65.4 us -> 62.5 us
  starting transfers between devices: 39.6 us -> 33.5 us
  waiting for transfers between devices: 6.41 us -> 10.1 us
    ppermute x4, starting transfers between devices: 12.3 us -> 2.04 us  [to_far(): return lax.ppermute(x, ('dp', 'ctx'), pairs)]
    ppermute x4, waiting for transfers between devices: 0.47 us -> 3.84 us  [flipped_apart(): lax.ppermute(part, 'ctx', [(i, i ^ step + 8 * (i % 2)) for i in range(siz...]
    ppermute x8, starting transfers between devices: 8.68 us -> 12 us  [flipped(): lax.ppermute(part, axis, [(i, i ^ f) for i in range(size)])]
    ppermute x4, waiting for transfers between devices: 1.33 us -> 4.58 us  [to_far(): return lax.ppermute(x, ('dp', 'ctx'), pairs)]
    ppermute x8, waiting for transfers between devices: 4.6 us -> 1.68 us  [flipped(): lax.ppermute(part, axis, [(i, i ^ f) for i in range(size)])]
    ppermute x4, starting transfers between devices: 3.93 us -> 6.46 us  [to_mate(): return lax.ppermute(x, 'ctx', mate_pairs)]
    ppermute x4, starting transfers between devices: 14.7 us -> 13 us  [flipped_apart(): lax.ppermute(part, 'ctx', [(i, i ^ step + 8 * (i % 2)) for i in range(siz...]
  transfers between devices with their start and end apart: 20 -> 20, of which waited for: 6 -> 6; matrix products, arithmetic and copies ran while one was open for 0% -> 0% of each run, Pallas kernels for 24% -> 25%
where the time goes in v4:
time: 62.6 us; the launch traced here: 62.5 us
  starting transfers between devices  33.5 us (54%)
  Pallas kernels  15.6 us (25%)
  waiting for transfers between devices  10.1 us (16%)
  other arithmetic  2.42 us (4%)
  between operations  0.85 us (1%)
    ppermute x4, starting transfers between devices, flipped_apart(): lax.ppermute(part, 'ctx', [(i, i ^ step + 8 * (i % 2)) for i in range(siz...  13 us
    ppermute x8, starting transfers between devices, flipped(): lax.ppermute(part, axis, [(i, i ^ f) for i in range(size)])  12 us
    pallas_call x1, Pallas kernels, per_device(): pl.pallas_call(own_kernel, grid=grid, in_specs=[SMEM] * 4 + [vspec] * 2 +...  9.02 us
    ppermute x4, starting transfers between devices, to_mate(): return lax.ppermute(x, 'ctx', mate_pairs)  6.46 us
    pallas_call x1, Pallas kernels, per_device(): pl.pallas_call(far_kernel, grid=grid, in_specs=[SMEM] * 4 + [pair, sspec,...  4.73 us
    ppermute x4, waiting for transfers between devices, to_far(): return lax.ppermute(x, ('dp', 'ctx'), pairs)  4.58 us
    ppermute x4, waiting for transfers between devices, flipped_apart(): lax.ppermute(part, 'ctx', [(i, i ^ step + 8 * (i % 2)) for i in range(siz...  3.84 us
    ppermute x4, starting transfers between devices, to_far(): return lax.ppermute(x, ('dp', 'ctx'), pairs)  2.04 us
  transfers between devices with their start and end apart: 20, of which 6 were waited for; matrix products, arithmetic and copies ran while one was open for 0% of the time, Pallas kernels for 25%

profile of v4, /device:TPU:1, one launch (start us, length us, event | category | flops | bytes accessed | tf_op | source)
XLA Modules:
  0.0 62.5 jit_solution(18290943369012210517)
XLA Ops:
  0.7 1.6 %pad_maximum_fusion.kv0.kv_ref = bf16[256,3072]{1,0:T(8,128)(2,1)S(1)} fusion(bf16[128,3072]{1,0:T(8,128)(2,1)} %bitcast.29, bf16[128,3072]{1,0:T(8,128)(2,1)} %bitcast.30), kind=kLoop, calls=%fused_computation | loop fusion | flops 3145728 | bytes 3145728 | tf_op jit(solution)/shard_map/concatenate | solution.py:362
  2.3 3.3 %collective-permute-start.1 = (bf16[32,3072]{1,0:T(8,128)(2,1)S(1)}, bf16[32,3072]{1,0:T(8,128)(2,1)S(1)}, u32[]{:S(2)}, u32[]{:S(2)}) collective-permute-start(bf16[32,3072]{1,0:T(8,128)(2,1)S(1)} %pad_maximum_fusion.2.a0.a_ref), channel_id=1, source_target_pairs={{0,1},{1,0},{2,3},{3,2},{4,5},{5,4},{6,7},{7,6},{8,9},{9,8},{10,11... | collective-permute-start | bytes 589832 | tf_op jit(solution)/shard_map/ppermute | solution.py:346
  5.7 0.0 collective-permute-start.2
  5.7 0.2 collective-permute-start
  5.9 1.7 %collective-permute-start.4 = (bf16[256,3072]{1,0:T(8,128)(2,1)S(1)}, bf16[256,3072]{1,0:T(8,128)(2,1)}, u32[]{:S(2)}, u32[]{:S(2)}) collective-permute-start(bf16[256,3072]{1,0:T(8,128)(2,1)S(1)} %pad_maximum_fusion.kv0.kv_ref), channel_id=1, source_target_pairs={{0,64},{1,2},{2,1},{3,4},{4,3},{5,6},{6,5},{7,8},{8,7},{9,10},{10,... | collective-permute-start | bytes 4718600 | tf_op jit(solution)/shard_map/ppermute | solution.py:354
  7.6 0.0 collective-permute-done.1.a1
  7.6 3.6 %collective-permute-done.2.a2 = bf16[32,3072]{1,0:T(8,128)(2,1)} collective-permute-done((bf16[32,3072]{1,0:T(8,128)(2,1)S(1)}, bf16[32,3072]{1,0:T(8,128)(2,1)}, u32[]{:S(2)}, u32[]{:S(2)}) %collective-permute-start.2) | collective-permute-done | bytes 196640 | tf_op jit(solution)/shard_map/ppermute | solution.py:354
  11.2 1.8 %gate_terms.1 = f32[1,3072]{1,0:T(1,128)S(1)} custom-call(s32[1]{0:T(128)} %bitcast.position_ref, s32[2,128]{1,0:T(2,128)S(1)} %bitcast.26, bf16[128,3072]{1,0:T(8,128)(2,1)S(1)} %bitcast.16, bf16[128,3072]{1,0:T(8,128)(2,1)S(1)} %bitcast.19, bf16[32,3072]{1,0:T(8,128)(2,1)S(1)} %pad_maximum_fusion.2.a0.a_ref, ...), custom_call_target="tpu_custom_call" | custom-call | flops 20000000000 | tf_op jit(solution)/shard_map/gate_terms/pallas_call | solution.py:388
  13.0 0.5 collective-permute-start.3
  13.5 0.8 %collective-permute-done.3 = f32[1,3072]{1,0:T(1,128)S(1)} collective-permute-done((f32[1,3072]{1,0:T(1,128)S(1)}, f32[1,3072]{1,0:T(1,128)S(1)}, u32[]{:S(2)}, u32[]{:S(2)}) %collective-permute-start.3) | collective-permute-done | bytes 12320 | tf_op jit(solution)/shard_map/ppermute | solution.py:289
  14.3 0.0 copy-start.2
  14.3 0.0 copy-start.3
  14.3 0.0 copy-start.5
  14.3 0.0 collective-permute-done.kv1
  14.4 7.7 %collective-permute-start.5 = (f32[1,3072]{1,0:T(1,128)S(1)}, f32[1,3072]{1,0:T(1,128)S(1)}, u32[]{:S(2)}, u32[]{:S(2)}) collective-permute-start(f32[1,3072]{1,0:T(1,128)S(1)} %add.33), channel_id=1, source_target_pairs={{0,0},{1,9},{2,2},{3,11},{4,4},{5,13},{6,6},{7,15},{8,8},{9,1},{10... | collective-permute-start | bytes 36872 | tf_op jit(solution)/shard_map/ppermute | solution.py:295
  22.1 0.1 collective-permute-start.6
  22.2 5.2 %collective-permute-start.7 = (f32[1,3072]{1,0:T(1,128)S(1)}, f32[1,3072]{1,0:T(1,128)S(1)}, u32[]{:S(2)}, u32[]{:S(2)}) collective-permute-start(f32[1,3072]{1,0:T(1,128)S(1)} %add.33), channel_id=1, source_target_pairs={{0,4},{1,13},{2,6},{3,15},{4,0},{5,9},{6,2},{7,11},{8,12},{9,5},{1... | collective-permute-start | bytes 36872 | tf_op jit(solution)/shard_map/ppermute | solution.py:295
  27.4 0.0 collective-permute-start.8
  27.4 1.0 %collective-permute-done.4.kv2 = bf16[256,3072]{1,0:T(8,128)(2,1)} collective-permute-done((bf16[256,3072]{1,0:T(8,128)(2,1)S(1)}, bf16[256,3072]{1,0:T(8,128)(2,1)}, u32[]{:S(2)}, u32[]{:S(2)}) %collective-permute-start.4) | collective-permute-done | bytes 1572896 | tf_op jit(solution)/shard_map/ppermute | solution.py:354
  28.4 3.6 %collective-permute-done.5 = f32[1,3072]{1,0:T(1,128)S(1)} collective-permute-done((f32[1,3072]{1,0:T(1,128)S(1)}, f32[1,3072]{1,0:T(1,128)S(1)}, u32[]{:S(2)}, u32[]{:S(2)}) %collective-permute-start.5) | collective-permute-done | bytes 12320 | tf_op jit(solution)/shard_map/ppermute | solution.py:295
  32.0 0.0 collective-permute-done.6
  32.0 0.0 collective-permute-done.7
  32.0 0.2 collective-permute-done.8
  32.2 0.1 pad_maximum_fusion.1
  32.3 0.1 collective-permute-start.9
  32.5 1.3 %collective-permute-start.10 = (f32[1,3072]{1,0:T(1,128)S(1)}, f32[1,3072]{1,0:T(1,128)S(1)}, u32[]{:S(2)}, u32[]{:S(2)}) collective-permute-start(f32[1,3072]{1,0:T(1,128)S(1)} %add_add_fusion.2), channel_id=1, source_target_pairs={{0,64},{64,0},{128,192},{192,128},{1,65},{65,1},{129,193},{193,129... | collective-permute-start | bytes 36872 | tf_op jit(solution)/shard_map/ppermute | solution.py:289
  33.7 2.5 %collective-permute-start.11 = (f32[1,3072]{1,0:T(1,128)S(1)}, f32[1,3072]{1,0:T(1,128)S(1)}, u32[]{:S(2)}, u32[]{:S(2)}) collective-permute-start(f32[1,3072]{1,0:T(1,128)S(1)} %add_add_fusion.2), channel_id=1, source_target_pairs={{0,128},{64,192},{128,0},{192,64},{1,129},{65,193},{129,1},{193,65... | collective-permute-start | bytes 36872 | tf_op jit(solution)/shard_map/ppermute | solution.py:289
  36.2 0.2 collective-permute-start.12
  36.4 9.0 %own_queries.1 = (bf16[128,3072]{1,0:T(8,128)(2,1)}, f32[288,3072]{1,0:T(8,128)S(1)}, bf16[144,3072]{1,0:T(8,128)(2,1)S(1)}, bf16[144,3072]{1,0:T(8,128)(2,1)S(1)}, f32[96,128]{1,0:T(8,128)S(1)}) custom-call(s32[1]{0:T(128)} %bitcast.position_ref, s32[4,128]{1,0:T(4,128)S(1)} %bitcast.24, s32[128]{0:T(128)S(1)} %copy-done.5, s32[2,128]{1,0:T(2,128)S(1)} %bitcast.27, ...), custom_call_target="tpu_custom_call" | custom-call | tf_op jit(solution)/shard_map/own_queries/pallas_call | solution.py:411
  45.4 0.0 collective-permute-done.10
  45.4 0.0 collective-permute-done.11
  45.4 0.0 collective-permute-done.12
  45.4 2.8 %collective-permute-start.14 = (bf16[144,3072]{1,0:T(8,128)(2,1)S(1)}, bf16[144,3072]{1,0:T(8,128)(2,1)S(1)}, u32[]{:S(2)}, u32[]{:S(2)}) collective-permute-start(bf16[144,3072]{1,0:T(8,128)(2,1)S(1)} %get-tuple-element.64), channel_id=1, source_target_pairs={{0,1},{1,0},{2,3},{3,2},{4,5},{5,4},{6,7},{7,6},{8,9},{9,8},{10,11... | collective-permute-start | bytes 2654216 | tf_op jit(solution)/shard_map/ppermute | solution.py:346
  48.3 0.1 collective-permute-start.15
  48.4 0.2 collective-permute-start.13
  48.6 3.6 %collective-permute-start.16 = (f32[1,3072]{1,0:T(1,128)S(1)}, f32[1,3072]{1,0:T(1,128)S(1)}, u32[]{:S(2)}, u32[]{:S(2)}) collective-permute-start(f32[1,3072]{1,0:T(1,128)S(1)} %add_add_fusion.1), channel_id=1, source_target_pairs={{0,1},{1,0},{2,3},{3,2},{4,5},{5,4},{6,7},{7,6},{8,9},{9,8},{10,11... | collective-permute-start | bytes 36872 | tf_op jit(solution)/shard_map/ppermute | solution.py:289
  52.2 0.8 %collective-permute-done.16 = f32[1,3072]{1,0:T(1,128)S(1)} collective-permute-done((f32[1,3072]{1,0:T(1,128)S(1)}, f32[1,3072]{1,0:T(1,128)S(1)}, u32[]{:S(2)}, u32[]{:S(2)}) %collective-permute-start.16) | collective-permute-done | bytes 12320 | tf_op jit(solution)/shard_map/ppermute | solution.py:289
  53.1 0.0 collective-permute-done.14.mate_k_in
  53.1 0.0 collective-permute-done.15.mate_v_in
  53.1 0.8 %collective-permute-start.17 = (f32[1,3072]{1,0:T(1,128)S(1)}, f32[1,3072]{1,0:T(1,128)S(1)}, u32[]{:S(2)}, u32[]{:S(2)}) collective-permute-start(f32[1,3072]{1,0:T(1,128)S(1)} %add.40), channel_id=1, source_target_pairs={{0,16},{1,17},{2,18},{3,19},{4,20},{5,21},{6,22},{7,23},{8,24},{9,... | collective-permute-start | bytes 36872 | tf_op jit(solution)/shard_map/ppermute | solution.py:289
  53.9 2.9 %collective-permute-start.18 = (f32[1,3072]{1,0:T(1,128)S(1)}, f32[1,3072]{1,0:T(1,128)S(1)}, u32[]{:S(2)}, u32[]{:S(2)}) collective-permute-start(f32[1,3072]{1,0:T(1,128)S(1)} %add.40), channel_id=1, source_target_pairs={{0,32},{1,33},{2,34},{3,35},{4,36},{5,37},{6,38},{7,39},{8,40},{9,... | collective-permute-start | bytes 36872 | tf_op jit(solution)/shard_map/ppermute | solution.py:289
  56.8 0.2 collective-permute-start.19
  57.1 0.0 collective-permute-done.13.stat_ref
  57.1 0.0 collective-permute-done.9.qo_ref
  57.1 4.7 %far_queries.1 = (bf16[128,3072]{1,0:T(8,128)(2,1)}, bf16[128,3072]{1,0:T(8,128)(2,1)}, bf16[16,3072]{1,0:T(8,128)(2,1)}, bf16[16,3072]{1,0:T(8,128)(2,1)}) custom-call(s32[1]{0:T(128)} %bitcast.position_ref, s32[4,128]{1,0:T(4,128)S(1)} %bitcast.25, s32[128]{0:T(128)S(1)} %copy-done.5, s32[2,128]{1,0:T(2,128)S(1)} %bitcast.28, ...), custom_call_target="tpu_custom_call" | custom-call | flops 5000000000 | tf_op jit(solution)/shard_map/far_queries/pallas_call | solution.py:436
  61.8 0.0 collective-permute-done.17
  61.8 0.0 collective-permute-done.18
  61.8 0.6 %add_add_fusion = f32[1,3072]{1,0:T(1,128)} fusion(f32[1,3072]{1,0:T(1,128)S(1)} %collective-permute-done.18, f32[1,3072]{1,0:T(1,128)S(1)} %collective-permute-done.19, f32[1,3072]{1,0:T(1,128)S(1)} %add.40, f32[1,3072]{1,0:T(1,128)S(1)} %collective-permute-done.17), kind=kLoop, calls=%fused_computation.3 | loop fusion | flops 9216 | bytes 61440 | tf_op jit(solution)/shard_map/add | solution.py:303
  (19 shorter events, 0.1 us)
Async XLA Ops:
  0.6 1.7 %copy-start.6 = (bf16[1,16,3072]{2,1,0:T(8,128)(2,1)S(1)}, bf16[1,16,3072]{2,1,0:T(8,128)(2,1)}, u32[]{:S(2)}) copy-start(bf16[1,16,3072]{2,1,0:T(8,128)(2,1)} %param.14) | copy-start | bytes 294916
  0.6 1.7 %copy-start.7 = (bf16[1,16,3072]{2,1,0:T(8,128)(2,1)S(1)}, bf16[1,16,3072]{2,1,0:T(8,128)(2,1)}, u32[]{:S(2)}) copy-start(bf16[1,16,3072]{2,1,0:T(8,128)(2,1)} %param.13) | copy-start | bytes 294916
  0.7 10.5 %copy-start = (bf16[1,128,3072]{2,1,0:T(8,128)(2,1)S(1)}, bf16[1,128,3072]{2,1,0:T(8,128)(2,1)}, u32[]{:S(2)}) copy-start(bf16[1,128,3072]{2,1,0:T(8,128)(2,1)} %param.10) | copy-start | bytes 2359300
  0.7 10.5 %copy-start.1 = (bf16[1,128,3072]{2,1,0:T(8,128)(2,1)S(1)}, bf16[1,128,3072]{2,1,0:T(8,128)(2,1)}, u32[]{:S(2)}) copy-start(bf16[1,128,3072]{2,1,0:T(8,128)(2,1)} %param.16) | copy-start | bytes 2359300
  0.7 10.5 %copy-start.4 = (s32[128,2]{0,1:T(2,128)S(1)}, s32[128,2]{0,1:T(2,128)}, u32[]{:S(2)}) copy-start(s32[128,2]{0,1:T(2,128)} %param.19) | copy-start | bytes 3076
  2.3 5.3 %collective-permute-start.1 = (bf16[32,3072]{1,0:T(8,128)(2,1)S(1)}, bf16[32,3072]{1,0:T(8,128)(2,1)S(1)}, u32[]{:S(2)}, u32[]{:S(2)}) collective-permute-start(bf16[32,3072]{1,0:T(8,128)(2,1)S(1)} %pad_maximum_fusion.2.a0.a_ref), channel_id=1, source_target_pairs={{0,1},{1,0},{2,3},{3,2},{4,5},{5,4},{6,7},{7,6},{8,9},{9,8},{10,11... | collective-permute-start | bytes 589832 | tf_op jit(solution)/shard_map/ppermute | solution.py:346
  5.7 5.5 %collective-permute-start.2 = (bf16[32,3072]{1,0:T(8,128)(2,1)S(1)}, bf16[32,3072]{1,0:T(8,128)(2,1)}, u32[]{:S(2)}, u32[]{:S(2)}) collective-permute-start(bf16[32,3072]{1,0:T(8,128)(2,1)S(1)} %pad_maximum_fusion.2.a0.a_ref), channel_id=1, source_target_pairs={{0,64},{1,2},{2,1},{3,4},{4,3},{5,6},{6,5},{7,8},{8,7},{9,10},{10,... | collective-permute-start | bytes 589832 | tf_op jit(solution)/shard_map/ppermute | solution.py:354
  5.7 8.7 %collective-permute-start = (bf16[256,3072]{1,0:T(8,128)(2,1)S(1)}, bf16[256,3072]{1,0:T(8,128)(2,1)}, u32[]{:S(2)}, u32[]{:S(2)}) collective-permute-start(bf16[256,3072]{1,0:T(8,128)(2,1)S(1)} %pad_maximum_fusion.kv0.kv_ref), channel_id=1, source_target_pairs={{0,1},{1,0},{2,3},{3,2},{4,5},{5,4},{6,7},{7,6},{8,9},{9,8},{10,11... | collective-permute-start | bytes 4718600 | tf_op jit(solution)/shard_map/ppermute | solution.py:346
  5.9 22.5 %collective-permute-start.4 = (bf16[256,3072]{1,0:T(8,128)(2,1)S(1)}, bf16[256,3072]{1,0:T(8,128)(2,1)}, u32[]{:S(2)}, u32[]{:S(2)}) collective-permute-start(bf16[256,3072]{1,0:T(8,128)(2,1)S(1)} %pad_maximum_fusion.kv0.kv_ref), channel_id=1, source_target_pairs={{0,64},{1,2},{2,1},{3,4},{4,3},{5,6},{6,5},{7,8},{8,7},{9,10},{10,... | collective-permute-start | bytes 4718600 | tf_op jit(solution)/shard_map/ppermute | solution.py:354
  13.0 1.3 %collective-permute-start.3 = (f32[1,3072]{1,0:T(1,128)S(1)}, f32[1,3072]{1,0:T(1,128)S(1)}, u32[]{:S(2)}, u32[]{:S(2)}) collective-permute-start(f32[1,3072]{1,0:T(1,128)S(1)} %gate_terms.1), channel_id=1, source_target_pairs={{0,1},{1,0},{2,3},{3,2},{4,5},{5,4},{6,7},{7,6},{8,9},{9,8},{10,11... | collective-permute-start | bytes 36872 | tf_op jit(solution)/shard_map/ppermute | solution.py:289
  14.3 22.1 %copy-start.2 = (f32[3072]{0:T(1024)S(1)}, f32[3072]{0:T(1024)}, u32[]{:S(2)}) copy-start(f32[3072]{0:T(1024)} %param.15) | copy-start | bytes 36868
  14.3 22.1 %copy-start.3 = (s32[128,4]{0,1:T(4,128)S(1)}, s32[128,4]{0,1:T(4,128)}, u32[]{:S(2)}) copy-start(s32[128,4]{0,1:T(4,128)} %param.17) | copy-start | bytes 6148
  14.3 22.1 %copy-start.5 = (s32[128]{0:T(128)S(1)}, s32[128]{0:T(128)}, u32[]{:S(2)}) copy-start(s32[128]{0:T(128)} %tile_count.3) | copy-start | bytes 1540
  14.4 17.6 %collective-permute-start.5 = (f32[1,3072]{1,0:T(1,128)S(1)}, f32[1,3072]{1,0:T(1,128)S(1)}, u32[]{:S(2)}, u32[]{:S(2)}) collective-permute-start(f32[1,3072]{1,0:T(1,128)S(1)} %add.33), channel_id=1, source_target_pairs={{0,0},{1,9},{2,2},{3,11},{4,4},{5,13},{6,6},{7,15},{8,8},{9,1},{10... | collective-permute-start | bytes 36872 | tf_op jit(solution)/shard_map/ppermute | solution.py:295
  22.1 9.9 %collective-permute-start.6 = (f32[1,3072]{1,0:T(1,128)S(1)}, f32[1,3072]{1,0:T(1,128)S(1)}, u32[]{:S(2)}, u32[]{:S(2)}) collective-permute-start(f32[1,3072]{1,0:T(1,128)S(1)} %add.33), channel_id=1, source_target_pairs={{0,2},{1,11},{2,0},{3,9},{4,6},{5,15},{6,4},{7,13},{8,10},{9,3},{1... | collective-permute-start | bytes 36872 | tf_op jit(solution)/shard_map/ppermute | solution.py:295
  22.2 9.8 %collective-permute-start.7 = (f32[1,3072]{1,0:T(1,128)S(1)}, f32[1,3072]{1,0:T(1,128)S(1)}, u32[]{:S(2)}, u32[]{:S(2)}) collective-permute-start(f32[1,3072]{1,0:T(1,128)S(1)} %add.33), channel_id=1, source_target_pairs={{0,4},{1,13},{2,6},{3,15},{4,0},{5,9},{6,2},{7,11},{8,12},{9,5},{1... | collective-permute-start | bytes 36872 | tf_op jit(solution)/shard_map/ppermute | solution.py:295
  27.4 4.9 %collective-permute-start.8 = (f32[1,3072]{1,0:T(1,128)S(1)}, f32[1,3072]{1,0:T(1,128)S(1)}, u32[]{:S(2)}, u32[]{:S(2)}) collective-permute-start(f32[1,3072]{1,0:T(1,128)S(1)} %add.33), channel_id=1, source_target_pairs={{0,6},{1,15},{2,4},{3,13},{4,2},{5,11},{6,0},{7,9},{8,14},{9,7},{1... | collective-permute-start | bytes 36872 | tf_op jit(solution)/shard_map/ppermute | solution.py:295
  32.3 24.8 %collective-permute-start.9 = (bf16[256,3072]{1,0:T(8,128)(2,1)S(1)}, bf16[256,3072]{1,0:T(8,128)(2,1)S(1)}, u32[]{:S(2)}, u32[]{:S(2)}) collective-permute-start(bf16[256,3072]{1,0:T(8,128)(2,1)S(1)} %pad_maximum_fusion.1), channel_id=1, source_target_pairs={{0,63},{1,2},{2,1},{3,4},{4,3},{5,6},{6,5},{7,8},{8,7},{9,10},{10,... | collective-permute-start | bytes 4718600 | tf_op jit(solution)/shard_map/ppermute | solution.py:354
  32.5 13.0 %collective-permute-start.10 = (f32[1,3072]{1,0:T(1,128)S(1)}, f32[1,3072]{1,0:T(1,128)S(1)}, u32[]{:S(2)}, u32[]{:S(2)}) collective-permute-start(f32[1,3072]{1,0:T(1,128)S(1)} %add_add_fusion.2), channel_id=1, source_target_pairs={{0,64},{64,0},{128,192},{192,128},{1,65},{65,1},{129,193},{193,129... | collective-permute-start | bytes 36872 | tf_op jit(solution)/shard_map/ppermute | solution.py:289
  33.7 11.7 %collective-permute-start.11 = (f32[1,3072]{1,0:T(1,128)S(1)}, f32[1,3072]{1,0:T(1,128)S(1)}, u32[]{:S(2)}, u32[]{:S(2)}) collective-permute-start(f32[1,3072]{1,0:T(1,128)S(1)} %add_add_fusion.2), channel_id=1, source_target_pairs={{0,128},{64,192},{128,0},{192,64},{1,129},{65,193},{129,1},{193,65... | collective-permute-start | bytes 36872 | tf_op jit(solution)/shard_map/ppermute | solution.py:289
  36.2 9.2 %collective-permute-start.12 = (f32[1,3072]{1,0:T(1,128)S(1)}, f32[1,3072]{1,0:T(1,128)S(1)}, u32[]{:S(2)}, u32[]{:S(2)}) collective-permute-start(f32[1,3072]{1,0:T(1,128)S(1)} %add_add_fusion.2), channel_id=1, source_target_pairs={{0,192},{64,128},{128,64},{192,0},{1,193},{65,129},{129,65},{193,1... | collective-permute-start | bytes 36872 | tf_op jit(solution)/shard_map/ppermute | solution.py:289
  45.4 7.7 %collective-permute-start.14 = (bf16[144,3072]{1,0:T(8,128)(2,1)S(1)}, bf16[144,3072]{1,0:T(8,128)(2,1)S(1)}, u32[]{:S(2)}, u32[]{:S(2)}) collective-permute-start(bf16[144,3072]{1,0:T(8,128)(2,1)S(1)} %get-tuple-element.64), channel_id=1, source_target_pairs={{0,1},{1,0},{2,3},{3,2},{4,5},{5,4},{6,7},{7,6},{8,9},{9,8},{10,11... | collective-permute-start | bytes 2654216 | tf_op jit(solution)/shard_map/ppermute | solution.py:346
  48.3 4.8 %collective-permute-start.15 = (bf16[144,3072]{1,0:T(8,128)(2,1)S(1)}, bf16[144,3072]{1,0:T(8,128)(2,1)S(1)}, u32[]{:S(2)}, u32[]{:S(2)}) collective-permute-start(bf16[144,3072]{1,0:T(8,128)(2,1)S(1)} %get-tuple-element.65), channel_id=1, source_target_pairs={{0,1},{1,0},{2,3},{3,2},{4,5},{5,4},{6,7},{7,6},{8,9},{9,8},{10,11... | collective-permute-start | bytes 2654216 | tf_op jit(solution)/shard_map/ppermute | solution.py:346
  48.4 8.7 %collective-permute-start.13 = (f32[96,128]{1,0:T(8,128)S(1)}, f32[96,128]{1,0:T(8,128)S(1)}, u32[]{:S(2)}, u32[]{:S(2)}) collective-permute-start(f32[96,128]{1,0:T(8,128)S(1)} %get-tuple-element.62), channel_id=1, source_target_pairs={{0,63},{1,2},{2,1},{3,4},{4,3},{5,6},{6,5},{7,8},{8,7},{9,10},{10,... | collective-permute-start | bytes 147464 | tf_op jit(solution)/shard_map/ppermute | solution.py:354
  48.6 4.5 %collective-permute-start.16 = (f32[1,3072]{1,0:T(1,128)S(1)}, f32[1,3072]{1,0:T(1,128)S(1)}, u32[]{:S(2)}, u32[]{:S(2)}) collective-permute-start(f32[1,3072]{1,0:T(1,128)S(1)} %add_add_fusion.1), channel_id=1, source_target_pairs={{0,1},{1,0},{2,3},{3,2},{4,5},{5,4},{6,7},{7,6},{8,9},{9,8},{10,11... | collective-permute-start | bytes 36872 | tf_op jit(solution)/shard_map/ppermute | solution.py:289
  53.1 8.7 %collective-permute-start.17 = (f32[1,3072]{1,0:T(1,128)S(1)}, f32[1,3072]{1,0:T(1,128)S(1)}, u32[]{:S(2)}, u32[]{:S(2)}) collective-permute-start(f32[1,3072]{1,0:T(1,128)S(1)} %add.40), channel_id=1, source_target_pairs={{0,16},{1,17},{2,18},{3,19},{4,20},{5,21},{6,22},{7,23},{8,24},{9,... | collective-permute-start | bytes 36872 | tf_op jit(solution)/shard_map/ppermute | solution.py:289
  53.9 7.9 %collective-permute-start.18 = (f32[1,3072]{1,0:T(1,128)S(1)}, f32[1,3072]{1,0:T(1,128)S(1)}, u32[]{:S(2)}, u32[]{:S(2)}) collective-permute-start(f32[1,3072]{1,0:T(1,128)S(1)} %add.40), channel_id=1, source_target_pairs={{0,32},{1,33},{2,34},{3,35},{4,36},{5,37},{6,38},{7,39},{8,40},{9,... | collective-permute-start | bytes 36872 | tf_op jit(solution)/shard_map/ppermute | solution.py:289
  56.8 5.0 %collective-permute-start.19 = (f32[1,3072]{1,0:T(1,128)S(1)}, f32[1,3072]{1,0:T(1,128)S(1)}, u32[]{:S(2)}, u32[]{:S(2)}) collective-permute-start(f32[1,3072]{1,0:T(1,128)S(1)} %add.40), channel_id=1, source_target_pairs={{0,48},{1,49},{2,50},{3,51},{4,52},{5,53},{6,54},{7,55},{8,56},{9,... | collective-permute-start | bytes 36872 | tf_op jit(solution)/shard_map/ppermute | solution.py:289

commit v5 on v4

--- a/solution.py
+++ b/solution.py
@@ -381,7 +381,7 @@
     def array(n, dtype):
         return jax.ShapeDtypeStruct((n, width), dtype)
 
-    params = pltpu.CompilerParams(vmem_limit_bytes=24 * 2**20)
+    params = pltpu.CompilerParams(vmem_limit_bytes=32 * 2**20)
 
     grid, pair, vspec, apair, aspec, gspec, sspec = specs(heads_per_step(heads, 24))
     gate_args = (q, do, a, a_mate, a_far)
@@ -404,7 +404,7 @@
     qo_far = to_far(jnp.concatenate([q_next, do], axis=0), True)
     parts = flipped(joined(parts), "dp", 1)
 
-    grid, pair, vspec, apair, aspec, gspec, sspec = specs(heads_per_step(heads, 8))
+    grid, pair, vspec, apair, aspec, gspec, sspec = specs(heads_per_step(heads, 12))
     sums_spec = cols_spec(2 * (rows + block), vspec.block_shape[1])
     half_spec = cols_spec(rows + block, vspec.block_shape[1])
     own_args = (q, do, kv, kv_mate, kv_far, a, a_mate, a_far)

time: 62.6 us -> 61.6 us (0.984)
  Pallas kernels: 15.6 us -> 14.5 us
    pallas_call x1, Pallas kernels: 9.02 us -> 8.25 us  [per_device(): pl.pallas_call(own_kernel, grid=grid, in_specs=[SMEM] * 4 + [vspec] * 2 +...]
  transfers between devices with their start and end apart: 20 -> 20, of which waited for: 6 -> 6; matrix products, arithmetic and copies ran while one was open for 0% -> 0% of each run, Pallas kernels for 25% -> 24%
where the time goes in v5:
time: 61.6 us; the launch traced here: 61.4 us
  starting transfers between devices  33.5 us (54%)
  Pallas kernels  14.5 us (24%)
  waiting for transfers between devices  10.1 us (16%)
  other arithmetic  2.42 us (4%)
  between operations  0.85 us (1%)
    ppermute x4, starting transfers between devices, flipped_apart(): lax.ppermute(part, 'ctx', [(i, i ^ step + 8 * (i % 2)) for i in range(siz...  13 us
    ppermute x8, starting transfers between devices, flipped(): lax.ppermute(part, axis, [(i, i ^ f) for i in range(size)])  12 us
    pallas_call x1, Pallas kernels, per_device(): pl.pallas_call(own_kernel, grid=grid, in_specs=[SMEM] * 4 + [vspec] * 2 +...  8.25 us
    ppermute x4, starting transfers between devices, to_mate(): return lax.ppermute(x, 'ctx', mate_pairs)  6.65 us
    ppermute x4, waiting for transfers between devices, to_far(): return lax.ppermute(x, ('dp', 'ctx'), pairs)  4.58 us
    pallas_call x1, Pallas kernels, per_device(): pl.pallas_call(far_kernel, grid=grid, in_specs=[SMEM] * 4 + [pair, sspec,...  4.46 us
    ppermute x4, waiting for transfers between devices, flipped_apart(): lax.ppermute(part, 'ctx', [(i, i ^ step + 8 * (i % 2)) for i in range(siz...  3.84 us
    ppermute x4, starting transfers between devices, to_far(): return lax.ppermute(x, ('dp', 'ctx'), pairs)  1.86 us
  transfers between devices with their start and end apart: 20, of which 6 were waited for; matrix products, arithmetic and copies ran while one was open for 0% of the time, Pallas kernels for 24%

profile of v5, /device:TPU:1, one launch (start us, length us, event | category | flops | bytes accessed | tf_op | source)
XLA Modules:
  0.0 61.4 jit_solution(2929964673365273573)
XLA Ops:
  0.7 1.6 %pad_maximum_fusion.kv0.kv_ref = bf16[256,3072]{1,0:T(8,128)(2,1)S(1)} fusion(bf16[128,3072]{1,0:T(8,128)(2,1)} %bitcast.29, bf16[128,3072]{1,0:T(8,128)(2,1)} %bitcast.30), kind=kLoop, calls=%fused_computation | loop fusion | flops 3145728 | bytes 3145728 | tf_op jit(solution)/shard_map/concatenate | solution.py:362
  2.3 3.3 %collective-permute-start.1 = (bf16[32,3072]{1,0:T(8,128)(2,1)S(1)}, bf16[32,3072]{1,0:T(8,128)(2,1)S(1)}, u32[]{:S(2)}, u32[]{:S(2)}) collective-permute-start(bf16[32,3072]{1,0:T(8,128)(2,1)S(1)} %pad_maximum_fusion.2.a0.a_ref), channel_id=1, source_target_pairs={{0,1},{1,0},{2,3},{3,2},{4,5},{5,4},{6,7},{7,6},{8,9},{9,8},{10,11... | collective-permute-start | bytes 589832 | tf_op jit(solution)/shard_map/ppermute | solution.py:346
  5.7 0.0 collective-permute-start.2
  5.7 0.2 collective-permute-start
  5.9 1.7 %collective-permute-start.4 = (bf16[256,3072]{1,0:T(8,128)(2,1)S(1)}, bf16[256,3072]{1,0:T(8,128)(2,1)}, u32[]{:S(2)}, u32[]{:S(2)}) collective-permute-start(bf16[256,3072]{1,0:T(8,128)(2,1)S(1)} %pad_maximum_fusion.kv0.kv_ref), channel_id=1, source_target_pairs={{0,64},{1,2},{2,1},{3,4},{4,3},{5,6},{6,5},{7,8},{8,7},{9,10},{10,... | collective-permute-start | bytes 4718600 | tf_op jit(solution)/shard_map/ppermute | solution.py:354
  7.6 0.0 collective-permute-done.1.a1
  7.6 3.6 %collective-permute-done.2.a2 = bf16[32,3072]{1,0:T(8,128)(2,1)} collective-permute-done((bf16[32,3072]{1,0:T(8,128)(2,1)S(1)}, bf16[32,3072]{1,0:T(8,128)(2,1)}, u32[]{:S(2)}, u32[]{:S(2)}) %collective-permute-start.2) | collective-permute-done | bytes 196640 | tf_op jit(solution)/shard_map/ppermute | solution.py:354
  11.2 1.8 %gate_terms.1 = f32[1,3072]{1,0:T(1,128)S(1)} custom-call(s32[1]{0:T(128)} %bitcast.position_ref, s32[2,128]{1,0:T(2,128)S(1)} %bitcast.26, bf16[128,3072]{1,0:T(8,128)(2,1)S(1)} %bitcast.16, bf16[128,3072]{1,0:T(8,128)(2,1)S(1)} %bitcast.19, bf16[32,3072]{1,0:T(8,128)(2,1)S(1)} %pad_maximum_fusion.2.a0.a_ref, ...), custom_call_target="tpu_custom_call" | custom-call | flops 20000000000 | tf_op jit(solution)/shard_map/gate_terms/pallas_call | solution.py:388
  13.0 0.5 collective-permute-start.3
  13.5 0.8 %collective-permute-done.3 = f32[1,3072]{1,0:T(1,128)S(1)} collective-permute-done((f32[1,3072]{1,0:T(1,128)S(1)}, f32[1,3072]{1,0:T(1,128)S(1)}, u32[]{:S(2)}, u32[]{:S(2)}) %collective-permute-start.3) | collective-permute-done | bytes 12320 | tf_op jit(solution)/shard_map/ppermute | solution.py:289
  14.3 0.0 copy-start.2
  14.3 0.0 copy-start.3
  14.3 0.0 copy-start.5
  14.3 0.0 collective-permute-done.kv1
  14.4 7.7 %collective-permute-start.5 = (f32[1,3072]{1,0:T(1,128)S(1)}, f32[1,3072]{1,0:T(1,128)S(1)}, u32[]{:S(2)}, u32[]{:S(2)}) collective-permute-start(f32[1,3072]{1,0:T(1,128)S(1)} %add.33), channel_id=1, source_target_pairs={{0,0},{1,9},{2,2},{3,11},{4,4},{5,13},{6,6},{7,15},{8,8},{9,1},{10... | collective-permute-start | bytes 36872 | tf_op jit(solution)/shard_map/ppermute | solution.py:295
  22.1 0.1 collective-permute-start.6
  22.2 5.2 %collective-permute-start.7 = (f32[1,3072]{1,0:T(1,128)S(1)}, f32[1,3072]{1,0:T(1,128)S(1)}, u32[]{:S(2)}, u32[]{:S(2)}) collective-permute-start(f32[1,3072]{1,0:T(1,128)S(1)} %add.33), channel_id=1, source_target_pairs={{0,4},{1,13},{2,6},{3,15},{4,0},{5,9},{6,2},{7,11},{8,12},{9,5},{1... | collective-permute-start | bytes 36872 | tf_op jit(solution)/shard_map/ppermute | solution.py:295
  27.4 0.0 collective-permute-start.8
  27.4 1.0 %collective-permute-done.4.kv2 = bf16[256,3072]{1,0:T(8,128)(2,1)} collective-permute-done((bf16[256,3072]{1,0:T(8,128)(2,1)S(1)}, bf16[256,3072]{1,0:T(8,128)(2,1)}, u32[]{:S(2)}, u32[]{:S(2)}) %collective-permute-start.4) | collective-permute-done | bytes 1572896 | tf_op jit(solution)/shard_map/ppermute | solution.py:354
  28.4 3.6 %collective-permute-done.5 = f32[1,3072]{1,0:T(1,128)S(1)} collective-permute-done((f32[1,3072]{1,0:T(1,128)S(1)}, f32[1,3072]{1,0:T(1,128)S(1)}, u32[]{:S(2)}, u32[]{:S(2)}) %collective-permute-start.5) | collective-permute-done | bytes 12320 | tf_op jit(solution)/shard_map/ppermute | solution.py:295
  32.0 0.0 collective-permute-done.6
  32.0 0.0 collective-permute-done.7
  32.0 0.2 collective-permute-done.8
  32.2 0.1 pad_maximum_fusion.1
  32.3 0.1 collective-permute-start.9
  32.5 1.3 %collective-permute-start.10 = (f32[1,3072]{1,0:T(1,128)S(1)}, f32[1,3072]{1,0:T(1,128)S(1)}, u32[]{:S(2)}, u32[]{:S(2)}) collective-permute-start(f32[1,3072]{1,0:T(1,128)S(1)} %add_add_fusion.2), channel_id=1, source_target_pairs={{0,64},{64,0},{128,192},{192,128},{1,65},{65,1},{129,193},{193,129... | collective-permute-start | bytes 36872 | tf_op jit(solution)/shard_map/ppermute | solution.py:289
  33.7 2.5 %collective-permute-start.11 = (f32[1,3072]{1,0:T(1,128)S(1)}, f32[1,3072]{1,0:T(1,128)S(1)}, u32[]{:S(2)}, u32[]{:S(2)}) collective-permute-start(f32[1,3072]{1,0:T(1,128)S(1)} %add_add_fusion.2), channel_id=1, source_target_pairs={{0,128},{64,192},{128,0},{192,64},{1,129},{65,193},{129,1},{193,65... | collective-permute-start | bytes 36872 | tf_op jit(solution)/shard_map/ppermute | solution.py:289
  36.2 0.2 collective-permute-start.12
  36.4 8.2 %own_queries.1 = (bf16[128,3072]{1,0:T(8,128)(2,1)}, f32[288,3072]{1,0:T(8,128)S(1)}, bf16[144,3072]{1,0:T(8,128)(2,1)S(1)}, bf16[144,3072]{1,0:T(8,128)(2,1)S(1)}, f32[96,128]{1,0:T(8,128)S(1)}) custom-call(s32[1]{0:T(128)} %bitcast.position_ref, s32[4,128]{1,0:T(4,128)S(1)} %bitcast.24, s32[128]{0:T(128)S(1)} %copy-done.5, s32[2,128]{1,0:T(2,128)S(1)} %bitcast.27, ...), custom_call_target="tpu_custom_call" | custom-call | tf_op jit(solution)/shard_map/own_queries/pallas_call | solution.py:411
  44.7 0.0 collective-permute-done.10
  44.7 0.0 collective-permute-done.11
  44.7 0.0 collective-permute-done.12
  44.7 2.8 %collective-permute-start.14 = (bf16[144,3072]{1,0:T(8,128)(2,1)S(1)}, bf16[144,3072]{1,0:T(8,128)(2,1)S(1)}, u32[]{:S(2)}, u32[]{:S(2)}) collective-permute-start(bf16[144,3072]{1,0:T(8,128)(2,1)S(1)} %get-tuple-element.64), channel_id=1, source_target_pairs={{0,1},{1,0},{2,3},{3,2},{4,5},{5,4},{6,7},{7,6},{8,9},{9,8},{10,11... | collective-permute-start | bytes 2654216 | tf_op jit(solution)/shard_map/ppermute | solution.py:346
  47.5 0.3 collective-permute-start.15
  47.8 0.0 collective-permute-start.13
  47.9 3.6 %collective-permute-start.16 = (f32[1,3072]{1,0:T(1,128)S(1)}, f32[1,3072]{1,0:T(1,128)S(1)}, u32[]{:S(2)}, u32[]{:S(2)}) collective-permute-start(f32[1,3072]{1,0:T(1,128)S(1)} %add_add_fusion.1), channel_id=1, source_target_pairs={{0,1},{1,0},{2,3},{3,2},{4,5},{5,4},{6,7},{7,6},{8,9},{9,8},{10,11... | collective-permute-start | bytes 36872 | tf_op jit(solution)/shard_map/ppermute | solution.py:289
  51.5 0.8 %collective-permute-done.16 = f32[1,3072]{1,0:T(1,128)S(1)} collective-permute-done((f32[1,3072]{1,0:T(1,128)S(1)}, f32[1,3072]{1,0:T(1,128)S(1)}, u32[]{:S(2)}, u32[]{:S(2)}) %collective-permute-start.16) | collective-permute-done | bytes 12320 | tf_op jit(solution)/shard_map/ppermute | solution.py:289
  52.3 0.0 collective-permute-done.14.mate_k_in
  52.3 0.0 collective-permute-done.15.mate_v_in
  52.4 0.8 %collective-permute-start.17 = (f32[1,3072]{1,0:T(1,128)S(1)}, f32[1,3072]{1,0:T(1,128)S(1)}, u32[]{:S(2)}, u32[]{:S(2)}) collective-permute-start(f32[1,3072]{1,0:T(1,128)S(1)} %add.40), channel_id=1, source_target_pairs={{0,16},{1,17},{2,18},{3,19},{4,20},{5,21},{6,22},{7,23},{8,24},{9,... | collective-permute-start | bytes 36872 | tf_op jit(solution)/shard_map/ppermute | solution.py:289
  53.1 2.9 %collective-permute-start.18 = (f32[1,3072]{1,0:T(1,128)S(1)}, f32[1,3072]{1,0:T(1,128)S(1)}, u32[]{:S(2)}, u32[]{:S(2)}) collective-permute-start(f32[1,3072]{1,0:T(1,128)S(1)} %add.40), channel_id=1, source_target_pairs={{0,32},{1,33},{2,34},{3,35},{4,36},{5,37},{6,38},{7,39},{8,40},{9,... | collective-permute-start | bytes 36872 | tf_op jit(solution)/shard_map/ppermute | solution.py:289
  56.1 0.2 collective-permute-start.19
  56.3 0.0 collective-permute-done.13.stat_ref
  56.3 0.0 collective-permute-done.9.qo_ref
  56.3 4.5 %far_queries.1 = (bf16[128,3072]{1,0:T(8,128)(2,1)}, bf16[128,3072]{1,0:T(8,128)(2,1)}, bf16[16,3072]{1,0:T(8,128)(2,1)}, bf16[16,3072]{1,0:T(8,128)(2,1)}) custom-call(s32[1]{0:T(128)} %bitcast.position_ref, s32[4,128]{1,0:T(4,128)S(1)} %bitcast.25, s32[128]{0:T(128)S(1)} %copy-done.5, s32[2,128]{1,0:T(2,128)S(1)} %bitcast.28, ...), custom_call_target="tpu_custom_call" | custom-call | flops 5000000000 | tf_op jit(solution)/shard_map/far_queries/pallas_call | solution.py:436
  60.8 0.0 collective-permute-done.17
  60.8 0.0 collective-permute-done.18
  60.8 0.6 %add_add_fusion = f32[1,3072]{1,0:T(1,128)} fusion(f32[1,3072]{1,0:T(1,128)S(1)} %collective-permute-done.18, f32[1,3072]{1,0:T(1,128)S(1)} %collective-permute-done.19, f32[1,3072]{1,0:T(1,128)S(1)} %add.40, f32[1,3072]{1,0:T(1,128)S(1)} %collective-permute-done.17), kind=kLoop, calls=%fused_computation.3 | loop fusion | flops 9216 | bytes 61440 | tf_op jit(solution)/shard_map/add | solution.py:303
  (19 shorter events, 0.1 us)
Async XLA Ops:
  0.6 1.7 %copy-start.6 = (bf16[1,16,3072]{2,1,0:T(8,128)(2,1)S(1)}, bf16[1,16,3072]{2,1,0:T(8,128)(2,1)}, u32[]{:S(2)}) copy-start(bf16[1,16,3072]{2,1,0:T(8,128)(2,1)} %param.14) | copy-start | bytes 294916
  0.6 1.7 %copy-start.7 = (bf16[1,16,3072]{2,1,0:T(8,128)(2,1)S(1)}, bf16[1,16,3072]{2,1,0:T(8,128)(2,1)}, u32[]{:S(2)}) copy-start(bf16[1,16,3072]{2,1,0:T(8,128)(2,1)} %param.13) | copy-start | bytes 294916
  0.7 10.5 %copy-start = (bf16[1,128,3072]{2,1,0:T(8,128)(2,1)S(1)}, bf16[1,128,3072]{2,1,0:T(8,128)(2,1)}, u32[]{:S(2)}) copy-start(bf16[1,128,3072]{2,1,0:T(8,128)(2,1)} %param.10) | copy-start | bytes 2359300
  0.7 10.5 %copy-start.1 = (bf16[1,128,3072]{2,1,0:T(8,128)(2,1)S(1)}, bf16[1,128,3072]{2,1,0:T(8,128)(2,1)}, u32[]{:S(2)}) copy-start(bf16[1,128,3072]{2,1,0:T(8,128)(2,1)} %param.16) | copy-start | bytes 2359300
  0.7 10.5 %copy-start.4 = (s32[128,2]{0,1:T(2,128)S(1)}, s32[128,2]{0,1:T(2,128)}, u32[]{:S(2)}) copy-start(s32[128,2]{0,1:T(2,128)} %param.19) | copy-start | bytes 3076
  2.3 5.3 %collective-permute-start.1 = (bf16[32,3072]{1,0:T(8,128)(2,1)S(1)}, bf16[32,3072]{1,0:T(8,128)(2,1)S(1)}, u32[]{:S(2)}, u32[]{:S(2)}) collective-permute-start(bf16[32,3072]{1,0:T(8,128)(2,1)S(1)} %pad_maximum_fusion.2.a0.a_ref), channel_id=1, source_target_pairs={{0,1},{1,0},{2,3},{3,2},{4,5},{5,4},{6,7},{7,6},{8,9},{9,8},{10,11... | collective-permute-start | bytes 589832 | tf_op jit(solution)/shard_map/ppermute | solution.py:346
  5.7 5.5 %collective-permute-start.2 = (bf16[32,3072]{1,0:T(8,128)(2,1)S(1)}, bf16[32,3072]{1,0:T(8,128)(2,1)}, u32[]{:S(2)}, u32[]{:S(2)}) collective-permute-start(bf16[32,3072]{1,0:T(8,128)(2,1)S(1)} %pad_maximum_fusion.2.a0.a_ref), channel_id=1, source_target_pairs={{0,64},{1,2},{2,1},{3,4},{4,3},{5,6},{6,5},{7,8},{8,7},{9,10},{10,... | collective-permute-start | bytes 589832 | tf_op jit(solution)/shard_map/ppermute | solution.py:354
  5.7 8.7 %collective-permute-start = (bf16[256,3072]{1,0:T(8,128)(2,1)S(1)}, bf16[256,3072]{1,0:T(8,128)(2,1)}, u32[]{:S(2)}, u32[]{:S(2)}) collective-permute-start(bf16[256,3072]{1,0:T(8,128)(2,1)S(1)} %pad_maximum_fusion.kv0.kv_ref), channel_id=1, source_target_pairs={{0,1},{1,0},{2,3},{3,2},{4,5},{5,4},{6,7},{7,6},{8,9},{9,8},{10,11... | collective-permute-start | bytes 4718600 | tf_op jit(solution)/shard_map/ppermute | solution.py:346
  5.9 22.5 %collective-permute-start.4 = (bf16[256,3072]{1,0:T(8,128)(2,1)S(1)}, bf16[256,3072]{1,0:T(8,128)(2,1)}, u32[]{:S(2)}, u32[]{:S(2)}) collective-permute-start(bf16[256,3072]{1,0:T(8,128)(2,1)S(1)} %pad_maximum_fusion.kv0.kv_ref), channel_id=1, source_target_pairs={{0,64},{1,2},{2,1},{3,4},{4,3},{5,6},{6,5},{7,8},{8,7},{9,10},{10,... | collective-permute-start | bytes 4718600 | tf_op jit(solution)/shard_map/ppermute | solution.py:354
  13.0 1.3 %collective-permute-start.3 = (f32[1,3072]{1,0:T(1,128)S(1)}, f32[1,3072]{1,0:T(1,128)S(1)}, u32[]{:S(2)}, u32[]{:S(2)}) collective-permute-start(f32[1,3072]{1,0:T(1,128)S(1)} %gate_terms.1), channel_id=1, source_target_pairs={{0,1},{1,0},{2,3},{3,2},{4,5},{5,4},{6,7},{7,6},{8,9},{9,8},{10,11... | collective-permute-start | bytes 36872 | tf_op jit(solution)/shard_map/ppermute | solution.py:289
  14.3 22.1 %copy-start.2 = (f32[3072]{0:T(1024)S(1)}, f32[3072]{0:T(1024)}, u32[]{:S(2)}) copy-start(f32[3072]{0:T(1024)} %param.15) | copy-start | bytes 36868
  14.3 22.1 %copy-start.3 = (s32[128,4]{0,1:T(4,128)S(1)}, s32[128,4]{0,1:T(4,128)}, u32[]{:S(2)}) copy-start(s32[128,4]{0,1:T(4,128)} %param.17) | copy-start | bytes 6148
  14.3 22.1 %copy-start.5 = (s32[128]{0:T(128)S(1)}, s32[128]{0:T(128)}, u32[]{:S(2)}) copy-start(s32[128]{0:T(128)} %tile_count.3) | copy-start | bytes 1540
  14.4 17.6 %collective-permute-start.5 = (f32[1,3072]{1,0:T(1,128)S(1)}, f32[1,3072]{1,0:T(1,128)S(1)}, u32[]{:S(2)}, u32[]{:S(2)}) collective-permute-start(f32[1,3072]{1,0:T(1,128)S(1)} %add.33), channel_id=1, source_target_pairs={{0,0},{1,9},{2,2},{3,11},{4,4},{5,13},{6,6},{7,15},{8,8},{9,1},{10... | collective-permute-start | bytes 36872 | tf_op jit(solution)/shard_map/ppermute | solution.py:295
  22.1 9.9 %collective-permute-start.6 = (f32[1,3072]{1,0:T(1,128)S(1)}, f32[1,3072]{1,0:T(1,128)S(1)}, u32[]{:S(2)}, u32[]{:S(2)}) collective-permute-start(f32[1,3072]{1,0:T(1,128)S(1)} %add.33), channel_id=1, source_target_pairs={{0,2},{1,11},{2,0},{3,9},{4,6},{5,15},{6,4},{7,13},{8,10},{9,3},{1... | collective-permute-start | bytes 36872 | tf_op jit(solution)/shard_map/ppermute | solution.py:295
  22.2 9.8 %collective-permute-start.7 = (f32[1,3072]{1,0:T(1,128)S(1)}, f32[1,3072]{1,0:T(1,128)S(1)}, u32[]{:S(2)}, u32[]{:S(2)}) collective-permute-start(f32[1,3072]{1,0:T(1,128)S(1)} %add.33), channel_id=1, source_target_pairs={{0,4},{1,13},{2,6},{3,15},{4,0},{5,9},{6,2},{7,11},{8,12},{9,5},{1... | collective-permute-start | bytes 36872 | tf_op jit(solution)/shard_map/ppermute | solution.py:295
  27.4 4.9 %collective-permute-start.8 = (f32[1,3072]{1,0:T(1,128)S(1)}, f32[1,3072]{1,0:T(1,128)S(1)}, u32[]{:S(2)}, u32[]{:S(2)}) collective-permute-start(f32[1,3072]{1,0:T(1,128)S(1)} %add.33), channel_id=1, source_target_pairs={{0,6},{1,15},{2,4},{3,13},{4,2},{5,11},{6,0},{7,9},{8,14},{9,7},{1... | collective-permute-start | bytes 36872 | tf_op jit(solution)/shard_map/ppermute | solution.py:295
  32.3 24.0 %collective-permute-start.9 = (bf16[256,3072]{1,0:T(8,128)(2,1)S(1)}, bf16[256,3072]{1,0:T(8,128)(2,1)S(1)}, u32[]{:S(2)}, u32[]{:S(2)}) collective-permute-start(bf16[256,3072]{1,0:T(8,128)(2,1)S(1)} %pad_maximum_fusion.1), channel_id=1, source_target_pairs={{0,63},{1,2},{2,1},{3,4},{4,3},{5,6},{6,5},{7,8},{8,7},{9,10},{10,... | collective-permute-start | bytes 4718600 | tf_op jit(solution)/shard_map/ppermute | solution.py:354
  32.5 12.2 %collective-permute-start.10 = (f32[1,3072]{1,0:T(1,128)S(1)}, f32[1,3072]{1,0:T(1,128)S(1)}, u32[]{:S(2)}, u32[]{:S(2)}) collective-permute-start(f32[1,3072]{1,0:T(1,128)S(1)} %add_add_fusion.2), channel_id=1, source_target_pairs={{0,64},{64,0},{128,192},{192,128},{1,65},{65,1},{129,193},{193,129... | collective-permute-start | bytes 36872 | tf_op jit(solution)/shard_map/ppermute | solution.py:289
  33.7 10.9 %collective-permute-start.11 = (f32[1,3072]{1,0:T(1,128)S(1)}, f32[1,3072]{1,0:T(1,128)S(1)}, u32[]{:S(2)}, u32[]{:S(2)}) collective-permute-start(f32[1,3072]{1,0:T(1,128)S(1)} %add_add_fusion.2), channel_id=1, source_target_pairs={{0,128},{64,192},{128,0},{192,64},{1,129},{65,193},{129,1},{193,65... | collective-permute-start | bytes 36872 | tf_op jit(solution)/shard_map/ppermute | solution.py:289
  36.2 8.5 %collective-permute-start.12 = (f32[1,3072]{1,0:T(1,128)S(1)}, f32[1,3072]{1,0:T(1,128)S(1)}, u32[]{:S(2)}, u32[]{:S(2)}) collective-permute-start(f32[1,3072]{1,0:T(1,128)S(1)} %add_add_fusion.2), channel_id=1, source_target_pairs={{0,192},{64,128},{128,64},{192,0},{1,193},{65,129},{129,65},{193,1... | collective-permute-start | bytes 36872 | tf_op jit(solution)/shard_map/ppermute | solution.py:289
  44.7 7.7 %collective-permute-start.14 = (bf16[144,3072]{1,0:T(8,128)(2,1)S(1)}, bf16[144,3072]{1,0:T(8,128)(2,1)S(1)}, u32[]{:S(2)}, u32[]{:S(2)}) collective-permute-start(bf16[144,3072]{1,0:T(8,128)(2,1)S(1)} %get-tuple-element.64), channel_id=1, source_target_pairs={{0,1},{1,0},{2,3},{3,2},{4,5},{5,4},{6,7},{7,6},{8,9},{9,8},{10,11... | collective-permute-start | bytes 2654216 | tf_op jit(solution)/shard_map/ppermute | solution.py:346
  47.5 4.8 %collective-permute-start.15 = (bf16[144,3072]{1,0:T(8,128)(2,1)S(1)}, bf16[144,3072]{1,0:T(8,128)(2,1)S(1)}, u32[]{:S(2)}, u32[]{:S(2)}) collective-permute-start(bf16[144,3072]{1,0:T(8,128)(2,1)S(1)} %get-tuple-element.65), channel_id=1, source_target_pairs={{0,1},{1,0},{2,3},{3,2},{4,5},{5,4},{6,7},{7,6},{8,9},{9,8},{10,11... | collective-permute-start | bytes 2654216 | tf_op jit(solution)/shard_map/ppermute | solution.py:346
  47.8 8.5 %collective-permute-start.13 = (f32[96,128]{1,0:T(8,128)S(1)}, f32[96,128]{1,0:T(8,128)S(1)}, u32[]{:S(2)}, u32[]{:S(2)}) collective-permute-start(f32[96,128]{1,0:T(8,128)S(1)} %get-tuple-element.62), channel_id=1, source_target_pairs={{0,63},{1,2},{2,1},{3,4},{4,3},{5,6},{6,5},{7,8},{8,7},{9,10},{10,... | collective-permute-start | bytes 147464 | tf_op jit(solution)/shard_map/ppermute | solution.py:354
  47.9 4.4 %collective-permute-start.16 = (f32[1,3072]{1,0:T(1,128)S(1)}, f32[1,3072]{1,0:T(1,128)S(1)}, u32[]{:S(2)}, u32[]{:S(2)}) collective-permute-start(f32[1,3072]{1,0:T(1,128)S(1)} %add_add_fusion.1), channel_id=1, source_target_pairs={{0,1},{1,0},{2,3},{3,2},{4,5},{5,4},{6,7},{7,6},{8,9},{9,8},{10,11... | collective-permute-start | bytes 36872 | tf_op jit(solution)/shard_map/ppermute | solution.py:289
  52.4 8.4 %collective-permute-start.17 = (f32[1,3072]{1,0:T(1,128)S(1)}, f32[1,3072]{1,0:T(1,128)S(1)}, u32[]{:S(2)}, u32[]{:S(2)}) collective-permute-start(f32[1,3072]{1,0:T(1,128)S(1)} %add.40), channel_id=1, source_target_pairs={{0,16},{1,17},{2,18},{3,19},{4,20},{5,21},{6,22},{7,23},{8,24},{9,... | collective-permute-start | bytes 36872 | tf_op jit(solution)/shard_map/ppermute | solution.py:289
  53.1 7.6 %collective-permute-start.18 = (f32[1,3072]{1,0:T(1,128)S(1)}, f32[1,3072]{1,0:T(1,128)S(1)}, u32[]{:S(2)}, u32[]{:S(2)}) collective-permute-start(f32[1,3072]{1,0:T(1,128)S(1)} %add.40), channel_id=1, source_target_pairs={{0,32},{1,33},{2,34},{3,35},{4,36},{5,37},{6,38},{7,39},{8,40},{9,... | collective-permute-start | bytes 36872 | tf_op jit(solution)/shard_map/ppermute | solution.py:289
  56.1 4.7 %collective-permute-start.19 = (f32[1,3072]{1,0:T(1,128)S(1)}, f32[1,3072]{1,0:T(1,128)S(1)}, u32[]{:S(2)}, u32[]{:S(2)}) collective-permute-start(f32[1,3072]{1,0:T(1,128)S(1)} %add.40), channel_id=1, source_target_pairs={{0,48},{1,49},{2,50},{3,51},{4,52},{5,53},{6,54},{7,55},{8,56},{9,... | collective-permute-start | bytes 36872 | tf_op jit(solution)/shard_map/ppermute | solution.py:289

commit v6 on v5

--- a/solution.py
+++ b/solution.py
@@ -189,9 +189,9 @@
         keys = jnp.concatenate([rows_at(video, 0, own, c), rows_at(audio, 0, block, c)], axis=0)
         both_ds = jnp.concatenate([video_ds, cross_ds], axis=0)
         dq_out[:, c] = (dot_lead(both_ds, keys) * SCALE).astype(jnp.bfloat16)
-        dk = dot(video_ds[: 2 * own], q)
+        from_q = dot(jnp.concatenate([video_ds[: 2 * own], cross_ds[: 2 * block]], axis=0), q)
+        dk, dak = from_q[: 2 * own], from_q[2 * own :]
         dv = dot(video_weights, do)
-        dak = dot(cross_ds[: 2 * block], q)
         dav = dot(cross_weights, gated_by(gate_ref[:, c], do))
         own_out[:own, c] = dk[:own]
         own_out[own : 2 * own, c] = dv[:own]

time: 61.6 us -> 61.4 us (level)
  no operation moved by 1% of the time
where the time goes in v6:
time: 61.4 us; the launch traced here: 61.2 us
  starting transfers between devices  33.3 us (54%)
  Pallas kernels  14.5 us (24%)
  waiting for transfers between devices  10.1 us (16%)
  other arithmetic  2.42 us (4%)
  between operations  0.85 us (1%)
    ppermute x4, starting transfers between devices, flipped_apart(): lax.ppermute(part, 'ctx', [(i, i ^ step + 8 * (i % 2)) for i in range(siz...  13 us
    ppermute x8, starting transfers between devices, flipped(): lax.ppermute(part, axis, [(i, i ^ f) for i in range(size)])  11.8 us
    pallas_call x1, Pallas kernels, per_device(): pl.pallas_call(own_kernel, grid=grid, in_specs=[SMEM] * 4 + [vspec] * 2 +...  8.19 us
    ppermute x4, starting transfers between devices, to_mate(): return lax.ppermute(x, 'ctx', mate_pairs)  6.47 us
    ppermute x4, waiting for transfers between devices, to_far(): return lax.ppermute(x, ('dp', 'ctx'), pairs)  4.58 us
    pallas_call x1, Pallas kernels, per_device(): pl.pallas_call(far_kernel, grid=grid, in_specs=[SMEM] * 4 + [pair, sspec,...  4.46 us
    ppermute x4, waiting for transfers between devices, flipped_apart(): lax.ppermute(part, 'ctx', [(i, i ^ step + 8 * (i % 2)) for i in range(siz...  3.84 us
    ppermute x4, starting transfers between devices, to_far(): return lax.ppermute(x, ('dp', 'ctx'), pairs)  2.05 us
  transfers between devices with their start and end apart: 20, of which 6 were waited for; matrix products, arithmetic and copies ran while one was open for 0% of the time, Pallas kernels for 24%

profile of v6, /device:TPU:1, one launch (start us, length us, event | category | flops | bytes accessed | tf_op | source)
XLA Modules:
  0.0 61.2 jit_solution(4136292077265641874)
XLA Ops:
  0.7 1.6 %pad_maximum_fusion.kv0.kv_ref = bf16[256,3072]{1,0:T(8,128)(2,1)S(1)} fusion(bf16[128,3072]{1,0:T(8,128)(2,1)} %bitcast.29, bf16[128,3072]{1,0:T(8,128)(2,1)} %bitcast.30), kind=kLoop, calls=%fused_computation | loop fusion | flops 3145728 | bytes 3145728 | tf_op jit(solution)/shard_map/concatenate | solution.py:362
  2.3 3.3 %collective-permute-start.1 = (bf16[32,3072]{1,0:T(8,128)(2,1)S(1)}, bf16[32,3072]{1,0:T(8,128)(2,1)S(1)}, u32[]{:S(2)}, u32[]{:S(2)}) collective-permute-start(bf16[32,3072]{1,0:T(8,128)(2,1)S(1)} %pad_maximum_fusion.2.a0.a_ref), channel_id=1, source_target_pairs={{0,1},{1,0},{2,3},{3,2},{4,5},{5,4},{6,7},{7,6},{8,9},{9,8},{10,11... | collective-permute-start | bytes 589832 | tf_op jit(solution)/shard_map/ppermute | solution.py:346
  5.7 0.0 collective-permute-start.2
  5.7 0.2 collective-permute-start
  5.9 1.7 %collective-permute-start.4 = (bf16[256,3072]{1,0:T(8,128)(2,1)S(1)}, bf16[256,3072]{1,0:T(8,128)(2,1)}, u32[]{:S(2)}, u32[]{:S(2)}) collective-permute-start(bf16[256,3072]{1,0:T(8,128)(2,1)S(1)} %pad_maximum_fusion.kv0.kv_ref), channel_id=1, source_target_pairs={{0,64},{1,2},{2,1},{3,4},{4,3},{5,6},{6,5},{7,8},{8,7},{9,10},{10,... | collective-permute-start | bytes 4718600 | tf_op jit(solution)/shard_map/ppermute | solution.py:354
  7.6 0.0 collective-permute-done.1.a1
  7.6 3.6 %collective-permute-done.2.a2 = bf16[32,3072]{1,0:T(8,128)(2,1)} collective-permute-done((bf16[32,3072]{1,0:T(8,128)(2,1)S(1)}, bf16[32,3072]{1,0:T(8,128)(2,1)}, u32[]{:S(2)}, u32[]{:S(2)}) %collective-permute-start.2) | collective-permute-done | bytes 196640 | tf_op jit(solution)/shard_map/ppermute | solution.py:354
  11.2 1.8 %gate_terms.1 = f32[1,3072]{1,0:T(1,128)S(1)} custom-call(s32[1]{0:T(128)} %bitcast.position_ref, s32[2,128]{1,0:T(2,128)S(1)} %bitcast.26, bf16[128,3072]{1,0:T(8,128)(2,1)S(1)} %bitcast.16, bf16[128,3072]{1,0:T(8,128)(2,1)S(1)} %bitcast.19, bf16[32,3072]{1,0:T(8,128)(2,1)S(1)} %pad_maximum_fusion.2.a0.a_ref, ...), custom_call_target="tpu_custom_call" | custom-call | flops 20000000000 | tf_op jit(solution)/shard_map/gate_terms/pallas_call | solution.py:388
  13.0 0.5 collective-permute-start.3
  13.5 0.8 %collective-permute-done.3 = f32[1,3072]{1,0:T(1,128)S(1)} collective-permute-done((f32[1,3072]{1,0:T(1,128)S(1)}, f32[1,3072]{1,0:T(1,128)S(1)}, u32[]{:S(2)}, u32[]{:S(2)}) %collective-permute-start.3) | collective-permute-done | bytes 12320 | tf_op jit(solution)/shard_map/ppermute | solution.py:289
  14.3 0.0 copy-start.2
  14.3 0.0 copy-start.3
  14.3 0.0 copy-start.5
  14.3 0.0 collective-permute-done.kv1
  14.4 7.7 %collective-permute-start.5 = (f32[1,3072]{1,0:T(1,128)S(1)}, f32[1,3072]{1,0:T(1,128)S(1)}, u32[]{:S(2)}, u32[]{:S(2)}) collective-permute-start(f32[1,3072]{1,0:T(1,128)S(1)} %add.33), channel_id=1, source_target_pairs={{0,0},{1,9},{2,2},{3,11},{4,4},{5,13},{6,6},{7,15},{8,8},{9,1},{10... | collective-permute-start | bytes 36872 | tf_op jit(solution)/shard_map/ppermute | solution.py:295
  22.1 0.1 collective-permute-start.6
  22.2 5.2 %collective-permute-start.7 = (f32[1,3072]{1,0:T(1,128)S(1)}, f32[1,3072]{1,0:T(1,128)S(1)}, u32[]{:S(2)}, u32[]{:S(2)}) collective-permute-start(f32[1,3072]{1,0:T(1,128)S(1)} %add.33), channel_id=1, source_target_pairs={{0,4},{1,13},{2,6},{3,15},{4,0},{5,9},{6,2},{7,11},{8,12},{9,5},{1... | collective-permute-start | bytes 36872 | tf_op jit(solution)/shard_map/ppermute | solution.py:295
  27.4 0.0 collective-permute-start.8
  27.4 1.0 %collective-permute-done.4.kv2 = bf16[256,3072]{1,0:T(8,128)(2,1)} collective-permute-done((bf16[256,3072]{1,0:T(8,128)(2,1)S(1)}, bf16[256,3072]{1,0:T(8,128)(2,1)}, u32[]{:S(2)}, u32[]{:S(2)}) %collective-permute-start.4) | collective-permute-done | bytes 1572896 | tf_op jit(solution)/shard_map/ppermute | solution.py:354
  28.4 3.6 %collective-permute-done.5 = f32[1,3072]{1,0:T(1,128)S(1)} collective-permute-done((f32[1,3072]{1,0:T(1,128)S(1)}, f32[1,3072]{1,0:T(1,128)S(1)}, u32[]{:S(2)}, u32[]{:S(2)}) %collective-permute-start.5) | collective-permute-done | bytes 12320 | tf_op jit(solution)/shard_map/ppermute | solution.py:295
  32.0 0.0 collective-permute-done.6
  32.0 0.0 collective-permute-done.7
  32.0 0.2 collective-permute-done.8
  32.2 0.1 pad_maximum_fusion.1
  32.3 0.1 collective-permute-start.9
  32.5 1.3 %collective-permute-start.10 = (f32[1,3072]{1,0:T(1,128)S(1)}, f32[1,3072]{1,0:T(1,128)S(1)}, u32[]{:S(2)}, u32[]{:S(2)}) collective-permute-start(f32[1,3072]{1,0:T(1,128)S(1)} %add_add_fusion.2), channel_id=1, source_target_pairs={{0,64},{64,0},{128,192},{192,128},{1,65},{65,1},{129,193},{193,129... | collective-permute-start | bytes 36872 | tf_op jit(solution)/shard_map/ppermute | solution.py:289
  33.7 2.5 %collective-permute-start.11 = (f32[1,3072]{1,0:T(1,128)S(1)}, f32[1,3072]{1,0:T(1,128)S(1)}, u32[]{:S(2)}, u32[]{:S(2)}) collective-permute-start(f32[1,3072]{1,0:T(1,128)S(1)} %add_add_fusion.2), channel_id=1, source_target_pairs={{0,128},{64,192},{128,0},{192,64},{1,129},{65,193},{129,1},{193,65... | collective-permute-start | bytes 36872 | tf_op jit(solution)/shard_map/ppermute | solution.py:289
  36.2 0.2 collective-permute-start.12
  36.4 8.2 %own_queries.1 = (bf16[128,3072]{1,0:T(8,128)(2,1)}, f32[288,3072]{1,0:T(8,128)S(1)}, bf16[144,3072]{1,0:T(8,128)(2,1)S(1)}, bf16[144,3072]{1,0:T(8,128)(2,1)S(1)}, f32[96,128]{1,0:T(8,128)S(1)}) custom-call(s32[1]{0:T(128)} %bitcast.position_ref, s32[4,128]{1,0:T(4,128)S(1)} %bitcast.24, s32[128]{0:T(128)S(1)} %copy-done.5, s32[2,128]{1,0:T(2,128)S(1)} %bitcast.27, ...), custom_call_target="tpu_custom_call" | custom-call | tf_op jit(solution)/shard_map/own_queries/pallas_call | solution.py:411
  44.6 0.0 collective-permute-done.10
  44.6 0.0 collective-permute-done.11
  44.6 0.0 collective-permute-done.12
  44.6 2.8 %collective-permute-start.14 = (bf16[144,3072]{1,0:T(8,128)(2,1)S(1)}, bf16[144,3072]{1,0:T(8,128)(2,1)S(1)}, u32[]{:S(2)}, u32[]{:S(2)}) collective-permute-start(bf16[144,3072]{1,0:T(8,128)(2,1)S(1)} %get-tuple-element.64), channel_id=1, source_target_pairs={{0,1},{1,0},{2,3},{3,2},{4,5},{5,4},{6,7},{7,6},{8,9},{9,8},{10,11... | collective-permute-start | bytes 2654216 | tf_op jit(solution)/shard_map/ppermute | solution.py:346
  47.5 0.1 collective-permute-start.15
  47.6 0.2 collective-permute-start.13
  47.8 3.4 %collective-permute-start.16 = (f32[1,3072]{1,0:T(1,128)S(1)}, f32[1,3072]{1,0:T(1,128)S(1)}, u32[]{:S(2)}, u32[]{:S(2)}) collective-permute-start(f32[1,3072]{1,0:T(1,128)S(1)} %add_add_fusion.1), channel_id=1, source_target_pairs={{0,1},{1,0},{2,3},{3,2},{4,5},{5,4},{6,7},{7,6},{8,9},{9,8},{10,11... | collective-permute-start | bytes 36872 | tf_op jit(solution)/shard_map/ppermute | solution.py:289
  51.3 0.8 %collective-permute-done.16 = f32[1,3072]{1,0:T(1,128)S(1)} collective-permute-done((f32[1,3072]{1,0:T(1,128)S(1)}, f32[1,3072]{1,0:T(1,128)S(1)}, u32[]{:S(2)}, u32[]{:S(2)}) %collective-permute-start.16) | collective-permute-done | bytes 12320 | tf_op jit(solution)/shard_map/ppermute | solution.py:289
  52.1 0.0 collective-permute-done.14.mate_k_in
  52.1 0.0 collective-permute-done.15.mate_v_in
  52.1 1.0 %collective-permute-start.17 = (f32[1,3072]{1,0:T(1,128)S(1)}, f32[1,3072]{1,0:T(1,128)S(1)}, u32[]{:S(2)}, u32[]{:S(2)}) collective-permute-start(f32[1,3072]{1,0:T(1,128)S(1)} %add.40), channel_id=1, source_target_pairs={{0,16},{1,17},{2,18},{3,19},{4,20},{5,21},{6,22},{7,23},{8,24},{9,... | collective-permute-start | bytes 36872 | tf_op jit(solution)/shard_map/ppermute | solution.py:289
  53.1 2.9 %collective-permute-start.18 = (f32[1,3072]{1,0:T(1,128)S(1)}, f32[1,3072]{1,0:T(1,128)S(1)}, u32[]{:S(2)}, u32[]{:S(2)}) collective-permute-start(f32[1,3072]{1,0:T(1,128)S(1)} %add.40), channel_id=1, source_target_pairs={{0,32},{1,33},{2,34},{3,35},{4,36},{5,37},{6,38},{7,39},{8,40},{9,... | collective-permute-start | bytes 36872 | tf_op jit(solution)/shard_map/ppermute | solution.py:289
  56.0 0.1 collective-permute-start.19
  56.1 0.0 collective-permute-done.13.stat_ref
  56.1 0.0 collective-permute-done.9.qo_ref
  56.1 4.5 %far_queries.1 = (bf16[128,3072]{1,0:T(8,128)(2,1)}, bf16[128,3072]{1,0:T(8,128)(2,1)}, bf16[16,3072]{1,0:T(8,128)(2,1)}, bf16[16,3072]{1,0:T(8,128)(2,1)}) custom-call(s32[1]{0:T(128)} %bitcast.position_ref, s32[4,128]{1,0:T(4,128)S(1)} %bitcast.25, s32[128]{0:T(128)S(1)} %copy-done.5, s32[2,128]{1,0:T(2,128)S(1)} %bitcast.28, ...), custom_call_target="tpu_custom_call" | custom-call | flops 5000000000 | tf_op jit(solution)/shard_map/far_queries/pallas_call | solution.py:436
  60.5 0.0 collective-permute-done.17
  60.6 0.0 collective-permute-done.19
  60.6 0.6 %add_add_fusion = f32[1,3072]{1,0:T(1,128)} fusion(f32[1,3072]{1,0:T(1,128)S(1)} %collective-permute-done.18, f32[1,3072]{1,0:T(1,128)S(1)} %collective-permute-done.19, f32[1,3072]{1,0:T(1,128)S(1)} %add.40, f32[1,3072]{1,0:T(1,128)S(1)} %collective-permute-done.17), kind=kLoop, calls=%fused_computation.3 | loop fusion | flops 9216 | bytes 61440 | tf_op jit(solution)/shard_map/add | solution.py:303
  (19 shorter events, 0.1 us)
Async XLA Ops:
  0.6 1.7 %copy-start.6 = (bf16[1,16,3072]{2,1,0:T(8,128)(2,1)S(1)}, bf16[1,16,3072]{2,1,0:T(8,128)(2,1)}, u32[]{:S(2)}) copy-start(bf16[1,16,3072]{2,1,0:T(8,128)(2,1)} %param.14) | copy-start | bytes 294916
  0.6 1.7 %copy-start.7 = (bf16[1,16,3072]{2,1,0:T(8,128)(2,1)S(1)}, bf16[1,16,3072]{2,1,0:T(8,128)(2,1)}, u32[]{:S(2)}) copy-start(bf16[1,16,3072]{2,1,0:T(8,128)(2,1)} %param.13) | copy-start | bytes 294916
  0.7 10.5 %copy-start = (bf16[1,128,3072]{2,1,0:T(8,128)(2,1)S(1)}, bf16[1,128,3072]{2,1,0:T(8,128)(2,1)}, u32[]{:S(2)}) copy-start(bf16[1,128,3072]{2,1,0:T(8,128)(2,1)} %param.10) | copy-start | bytes 2359300
  0.7 10.5 %copy-start.1 = (bf16[1,128,3072]{2,1,0:T(8,128)(2,1)S(1)}, bf16[1,128,3072]{2,1,0:T(8,128)(2,1)}, u32[]{:S(2)}) copy-start(bf16[1,128,3072]{2,1,0:T(8,128)(2,1)} %param.16) | copy-start | bytes 2359300
  0.7 10.5 %copy-start.4 = (s32[128,2]{0,1:T(2,128)S(1)}, s32[128,2]{0,1:T(2,128)}, u32[]{:S(2)}) copy-start(s32[128,2]{0,1:T(2,128)} %param.19) | copy-start | bytes 3076
  2.3 5.3 %collective-permute-start.1 = (bf16[32,3072]{1,0:T(8,128)(2,1)S(1)}, bf16[32,3072]{1,0:T(8,128)(2,1)S(1)}, u32[]{:S(2)}, u32[]{:S(2)}) collective-permute-start(bf16[32,3072]{1,0:T(8,128)(2,1)S(1)} %pad_maximum_fusion.2.a0.a_ref), channel_id=1, source_target_pairs={{0,1},{1,0},{2,3},{3,2},{4,5},{5,4},{6,7},{7,6},{8,9},{9,8},{10,11... | collective-permute-start | bytes 589832 | tf_op jit(solution)/shard_map/ppermute | solution.py:346
  5.7 5.5 %collective-permute-start.2 = (bf16[32,3072]{1,0:T(8,128)(2,1)S(1)}, bf16[32,3072]{1,0:T(8,128)(2,1)}, u32[]{:S(2)}, u32[]{:S(2)}) collective-permute-start(bf16[32,3072]{1,0:T(8,128)(2,1)S(1)} %pad_maximum_fusion.2.a0.a_ref), channel_id=1, source_target_pairs={{0,64},{1,2},{2,1},{3,4},{4,3},{5,6},{6,5},{7,8},{8,7},{9,10},{10,... | collective-permute-start | bytes 589832 | tf_op jit(solution)/shard_map/ppermute | solution.py:354
  5.7 8.7 %collective-permute-start = (bf16[256,3072]{1,0:T(8,128)(2,1)S(1)}, bf16[256,3072]{1,0:T(8,128)(2,1)}, u32[]{:S(2)}, u32[]{:S(2)}) collective-permute-start(bf16[256,3072]{1,0:T(8,128)(2,1)S(1)} %pad_maximum_fusion.kv0.kv_ref), channel_id=1, source_target_pairs={{0,1},{1,0},{2,3},{3,2},{4,5},{5,4},{6,7},{7,6},{8,9},{9,8},{10,11... | collective-permute-start | bytes 4718600 | tf_op jit(solution)/shard_map/ppermute | solution.py:346
  5.9 22.5 %collective-permute-start.4 = (bf16[256,3072]{1,0:T(8,128)(2,1)S(1)}, bf16[256,3072]{1,0:T(8,128)(2,1)}, u32[]{:S(2)}, u32[]{:S(2)}) collective-permute-start(bf16[256,3072]{1,0:T(8,128)(2,1)S(1)} %pad_maximum_fusion.kv0.kv_ref), channel_id=1, source_target_pairs={{0,64},{1,2},{2,1},{3,4},{4,3},{5,6},{6,5},{7,8},{8,7},{9,10},{10,... | collective-permute-start | bytes 4718600 | tf_op jit(solution)/shard_map/ppermute | solution.py:354
  13.0 1.3 %collective-permute-start.3 = (f32[1,3072]{1,0:T(1,128)S(1)}, f32[1,3072]{1,0:T(1,128)S(1)}, u32[]{:S(2)}, u32[]{:S(2)}) collective-permute-start(f32[1,3072]{1,0:T(1,128)S(1)} %gate_terms.1), channel_id=1, source_target_pairs={{0,1},{1,0},{2,3},{3,2},{4,5},{5,4},{6,7},{7,6},{8,9},{9,8},{10,11... | collective-permute-start | bytes 36872 | tf_op jit(solution)/shard_map/ppermute | solution.py:289
  14.3 22.1 %copy-start.2 = (f32[3072]{0:T(1024)S(1)}, f32[3072]{0:T(1024)}, u32[]{:S(2)}) copy-start(f32[3072]{0:T(1024)} %param.15) | copy-start | bytes 36868
  14.3 22.1 %copy-start.3 = (s32[128,4]{0,1:T(4,128)S(1)}, s32[128,4]{0,1:T(4,128)}, u32[]{:S(2)}) copy-start(s32[128,4]{0,1:T(4,128)} %param.17) | copy-start | bytes 6148
  14.3 22.1 %copy-start.5 = (s32[128]{0:T(128)S(1)}, s32[128]{0:T(128)}, u32[]{:S(2)}) copy-start(s32[128]{0:T(128)} %tile_count.3) | copy-start | bytes 1540
  14.4 17.6 %collective-permute-start.5 = (f32[1,3072]{1,0:T(1,128)S(1)}, f32[1,3072]{1,0:T(1,128)S(1)}, u32[]{:S(2)}, u32[]{:S(2)}) collective-permute-start(f32[1,3072]{1,0:T(1,128)S(1)} %add.33), channel_id=1, source_target_pairs={{0,0},{1,9},{2,2},{3,11},{4,4},{5,13},{6,6},{7,15},{8,8},{9,1},{10... | collective-permute-start | bytes 36872 | tf_op jit(solution)/shard_map/ppermute | solution.py:295
  22.1 9.9 %collective-permute-start.6 = (f32[1,3072]{1,0:T(1,128)S(1)}, f32[1,3072]{1,0:T(1,128)S(1)}, u32[]{:S(2)}, u32[]{:S(2)}) collective-permute-start(f32[1,3072]{1,0:T(1,128)S(1)} %add.33), channel_id=1, source_target_pairs={{0,2},{1,11},{2,0},{3,9},{4,6},{5,15},{6,4},{7,13},{8,10},{9,3},{1... | collective-permute-start | bytes 36872 | tf_op jit(solution)/shard_map/ppermute | solution.py:295
  22.2 9.8 %collective-permute-start.7 = (f32[1,3072]{1,0:T(1,128)S(1)}, f32[1,3072]{1,0:T(1,128)S(1)}, u32[]{:S(2)}, u32[]{:S(2)}) collective-permute-start(f32[1,3072]{1,0:T(1,128)S(1)} %add.33), channel_id=1, source_target_pairs={{0,4},{1,13},{2,6},{3,15},{4,0},{5,9},{6,2},{7,11},{8,12},{9,5},{1... | collective-permute-start | bytes 36872 | tf_op jit(solution)/shard_map/ppermute | solution.py:295
  27.4 4.9 %collective-permute-start.8 = (f32[1,3072]{1,0:T(1,128)S(1)}, f32[1,3072]{1,0:T(1,128)S(1)}, u32[]{:S(2)}, u32[]{:S(2)}) collective-permute-start(f32[1,3072]{1,0:T(1,128)S(1)} %add.33), channel_id=1, source_target_pairs={{0,6},{1,15},{2,4},{3,13},{4,2},{5,11},{6,0},{7,9},{8,14},{9,7},{1... | collective-permute-start | bytes 36872 | tf_op jit(solution)/shard_map/ppermute | solution.py:295
  32.3 23.8 %collective-permute-start.9 = (bf16[256,3072]{1,0:T(8,128)(2,1)S(1)}, bf16[256,3072]{1,0:T(8,128)(2,1)S(1)}, u32[]{:S(2)}, u32[]{:S(2)}) collective-permute-start(bf16[256,3072]{1,0:T(8,128)(2,1)S(1)} %pad_maximum_fusion.1), channel_id=1, source_target_pairs={{0,63},{1,2},{2,1},{3,4},{4,3},{5,6},{6,5},{7,8},{8,7},{9,10},{10,... | collective-permute-start | bytes 4718600 | tf_op jit(solution)/shard_map/ppermute | solution.py:354
  32.5 12.2 %collective-permute-start.10 = (f32[1,3072]{1,0:T(1,128)S(1)}, f32[1,3072]{1,0:T(1,128)S(1)}, u32[]{:S(2)}, u32[]{:S(2)}) collective-permute-start(f32[1,3072]{1,0:T(1,128)S(1)} %add_add_fusion.2), channel_id=1, source_target_pairs={{0,64},{64,0},{128,192},{192,128},{1,65},{65,1},{129,193},{193,129... | collective-permute-start | bytes 36872 | tf_op jit(solution)/shard_map/ppermute | solution.py:289
  33.7 10.9 %collective-permute-start.11 = (f32[1,3072]{1,0:T(1,128)S(1)}, f32[1,3072]{1,0:T(1,128)S(1)}, u32[]{:S(2)}, u32[]{:S(2)}) collective-permute-start(f32[1,3072]{1,0:T(1,128)S(1)} %add_add_fusion.2), channel_id=1, source_target_pairs={{0,128},{64,192},{128,0},{192,64},{1,129},{65,193},{129,1},{193,65... | collective-permute-start | bytes 36872 | tf_op jit(solution)/shard_map/ppermute | solution.py:289
  36.2 8.4 %collective-permute-start.12 = (f32[1,3072]{1,0:T(1,128)S(1)}, f32[1,3072]{1,0:T(1,128)S(1)}, u32[]{:S(2)}, u32[]{:S(2)}) collective-permute-start(f32[1,3072]{1,0:T(1,128)S(1)} %add_add_fusion.2), channel_id=1, source_target_pairs={{0,192},{64,128},{128,64},{192,0},{1,193},{65,129},{129,65},{193,1... | collective-permute-start | bytes 36872 | tf_op jit(solution)/shard_map/ppermute | solution.py:289
  44.6 7.5 %collective-permute-start.14 = (bf16[144,3072]{1,0:T(8,128)(2,1)S(1)}, bf16[144,3072]{1,0:T(8,128)(2,1)S(1)}, u32[]{:S(2)}, u32[]{:S(2)}) collective-permute-start(bf16[144,3072]{1,0:T(8,128)(2,1)S(1)} %get-tuple-element.64), channel_id=1, source_target_pairs={{0,1},{1,0},{2,3},{3,2},{4,5},{5,4},{6,7},{7,6},{8,9},{9,8},{10,11... | collective-permute-start | bytes 2654216 | tf_op jit(solution)/shard_map/ppermute | solution.py:346
  47.5 4.7 %collective-permute-start.15 = (bf16[144,3072]{1,0:T(8,128)(2,1)S(1)}, bf16[144,3072]{1,0:T(8,128)(2,1)S(1)}, u32[]{:S(2)}, u32[]{:S(2)}) collective-permute-start(bf16[144,3072]{1,0:T(8,128)(2,1)S(1)} %get-tuple-element.65), channel_id=1, source_target_pairs={{0,1},{1,0},{2,3},{3,2},{4,5},{5,4},{6,7},{7,6},{8,9},{9,8},{10,11... | collective-permute-start | bytes 2654216 | tf_op jit(solution)/shard_map/ppermute | solution.py:346
  47.6 8.5 %collective-permute-start.13 = (f32[96,128]{1,0:T(8,128)S(1)}, f32[96,128]{1,0:T(8,128)S(1)}, u32[]{:S(2)}, u32[]{:S(2)}) collective-permute-start(f32[96,128]{1,0:T(8,128)S(1)} %get-tuple-element.62), channel_id=1, source_target_pairs={{0,63},{1,2},{2,1},{3,4},{4,3},{5,6},{6,5},{7,8},{8,7},{9,10},{10,... | collective-permute-start | bytes 147464 | tf_op jit(solution)/shard_map/ppermute | solution.py:354
  47.8 4.3 %collective-permute-start.16 = (f32[1,3072]{1,0:T(1,128)S(1)}, f32[1,3072]{1,0:T(1,128)S(1)}, u32[]{:S(2)}, u32[]{:S(2)}) collective-permute-start(f32[1,3072]{1,0:T(1,128)S(1)} %add_add_fusion.1), channel_id=1, source_target_pairs={{0,1},{1,0},{2,3},{3,2},{4,5},{5,4},{6,7},{7,6},{8,9},{9,8},{10,11... | collective-permute-start | bytes 36872 | tf_op jit(solution)/shard_map/ppermute | solution.py:289
  52.1 8.4 %collective-permute-start.17 = (f32[1,3072]{1,0:T(1,128)S(1)}, f32[1,3072]{1,0:T(1,128)S(1)}, u32[]{:S(2)}, u32[]{:S(2)}) collective-permute-start(f32[1,3072]{1,0:T(1,128)S(1)} %add.40), channel_id=1, source_target_pairs={{0,16},{1,17},{2,18},{3,19},{4,20},{5,21},{6,22},{7,23},{8,24},{9,... | collective-permute-start | bytes 36872 | tf_op jit(solution)/shard_map/ppermute | solution.py:289
  53.1 7.4 %collective-permute-start.18 = (f32[1,3072]{1,0:T(1,128)S(1)}, f32[1,3072]{1,0:T(1,128)S(1)}, u32[]{:S(2)}, u32[]{:S(2)}) collective-permute-start(f32[1,3072]{1,0:T(1,128)S(1)} %add.40), channel_id=1, source_target_pairs={{0,32},{1,33},{2,34},{3,35},{4,36},{5,37},{6,38},{7,39},{8,40},{9,... | collective-permute-start | bytes 36872 | tf_op jit(solution)/shard_map/ppermute | solution.py:289
  56.0 4.6 %collective-permute-start.19 = (f32[1,3072]{1,0:T(1,128)S(1)}, f32[1,3072]{1,0:T(1,128)S(1)}, u32[]{:S(2)}, u32[]{:S(2)}) collective-permute-start(f32[1,3072]{1,0:T(1,128)S(1)} %add.40), channel_id=1, source_target_pairs={{0,48},{1,49},{2,50},{3,51},{4,52},{5,53},{6,54},{7,55},{8,56},{9,... | collective-permute-start | bytes 36872 | tf_op jit(solution)/shard_map/ppermute | solution.py:289
